TPU v7x, 32 devices: a whole 2x2x4 slice. The times are simulated.
32 devices in a mesh: dp: 2 (over core), tensor: 2 (over x), expert: 8 (over z, y).
Axes of the slice: x: 2, y: 2, z: 4, core: 2. Of those that a mesh axis runs over, the one named last changes fastest.
Arguments:
- checkpoint: bfloat16 [2048, 2048], P(('dp', 'expert'), 'tensor'), may hold values from -6 to 6
- scales: float32 [2048], P(('dp', 'expert')), may hold values from 0.5 to 2
- out_grad: bfloat16 [2048, 2048], P(('dp', 'expert'), 'tensor'), may hold values from -1.5 to 1.5
- expert_ids: int32 [2048, 8], P(('dp', 'expert')), may hold values from 0 to 15, all different within a row; in each aligned block of 128 rows (0 to 127, 128 to 255, ...) at most 64 rows name the same one
- gates: float32 [2048, 8], P(('dp', 'expert')), may hold values from 0.05 to 1
- w_gate: bfloat16 [16, 768, 2048], P(('dp', 'expert'), 'tensor'), may hold values from -0.125 to 0.125
- w_up: bfloat16 [16, 768, 2048], P(('dp', 'expert'), 'tensor'), may hold values from -0.125 to 0.125
- w_down: bfloat16 [16, 768, 2048], P(('dp', 'expert'), 'tensor'), may hold values from -0.21875 to 0.21875
Outputs:
- grad_input: bfloat16 [2048, 2048], P(('dp', 'expert'), 'tensor')
- grad_gates: float32 [2048, 8], P(('dp', 'expert'))
Inputs may be any that keep to these rules, and one draw needn't show every extreme that they name: `expert_ids`: each row names 8 different experts. Among the 128 rows of one device (aligned blocks of rows), no expert is named more than 64 times, a bound that some block reaches.
All inputs are finite; a program needn't handle non-finite values.
Results may differ from a plain program's by a relative error of at most 0.012.
Values may be sent and summed in bfloat16 or wider, within the bound.
No kernel may reach another device: no remote copies, remote signals or barrier semaphores. Data moves between devices by JAX's collectives and lax.ppermute only.
A program may use at most 64 MiB of HBM per device.

v0:
```python
import jax
import jax.numpy as jnp
from jax import lax
from jax.sharding import PartitionSpec as P


def slot_table(expert_ids, expert_count, slot_cap):
    token_rows = expert_ids.shape[0]
    pick_count = expert_ids.shape[1]
    chosen = expert_ids.reshape(-1)
    onehot = (chosen[:, None] == jnp.arange(expert_count, dtype=jnp.int32)[None, :]).astype(
        jnp.int32
    )
    earlier = jnp.cumsum(onehot, axis=0) - onehot
    position = jnp.sum(earlier * onehot, axis=1)
    slot_of = chosen * slot_cap + position
    token_ids = jnp.arange(token_rows * pick_count, dtype=jnp.int32) // pick_count
    owner = jnp.full((expert_count * slot_cap,), token_rows, jnp.int32).at[slot_of].set(token_ids)
    return (slot_of, owner)


def finish(gate_pre, up_pre, back, weight_gate, weight_up):
    sigma = jax.nn.sigmoid(gate_pre)
    swish = gate_pre * sigma
    hidden = (swish * up_pre).astype(jnp.bfloat16)
    gate_part = jnp.sum(hidden.astype(jnp.float32) * back, axis=1).astype(jnp.bfloat16)
    d_gate = (back * up_pre * sigma * (1.0 + gate_pre * (1.0 - sigma))).astype(jnp.bfloat16)
    d_up = (back * swish).astype(jnp.bfloat16)
    input_part = jnp.dot(d_gate, weight_gate, preferred_element_type=jnp.float32)
    input_part = input_part + jnp.dot(d_up, weight_up, preferred_element_type=jnp.float32)
    return (input_part.astype(jnp.bfloat16), gate_part)


def close_expert(input_part, gate_part, sources, items, model_width):
    shaped = input_part.reshape(sources, items, model_width)
    gate_shaped = gate_part.reshape(sources, items)
    summed = lax.psum_scatter(
        shaped.astype(jnp.float32).astype(jnp.bfloat16), "tensor", scatter_dimension=2, tiled=True
    )
    return (summed, gate_shaped)


def body(checkpoint, scales, out_grad, expert_ids, gates, w_gate, w_up, w_down):
    expert_count = lax.axis_size("dp") * lax.axis_size("expert")
    token_rows = checkpoint.shape[0]
    pick_count = expert_ids.shape[1]
    slot_cap = min(token_rows, token_rows * pick_count // expert_count)
    weight_gate = w_gate[0]
    weight_up = w_up[0]
    weight_down = w_down[0]
    model_width = weight_gate.shape[1]
    contract = (((1,), (1,)), ((), ()))
    dequant = (checkpoint.astype(jnp.float32) * scales[:, None]).astype(jnp.bfloat16)
    slot_of, owner = slot_table(expert_ids, expert_count, slot_cap)
    full_x, full_grad = (
        lax.all_gather(dequant, "tensor", axis=1, tiled=True),
        lax.all_gather(out_grad, "tensor", axis=1, tiled=True),
    )
    send_x = jnp.take(full_x, owner, axis=0, mode="fill", fill_value=0).reshape(
        expert_count, slot_cap, model_width
    )
    send_grad = jnp.take(full_grad, owner, axis=0, mode="fill", fill_value=0).reshape(
        expert_count, slot_cap, model_width
    )
    rows_in = lax.all_to_all(send_x, ("dp", "expert"), split_axis=0, concat_axis=0, tiled=True)
    grads_in = lax.all_to_all(send_grad, ("dp", "expert"), split_axis=0, concat_axis=0, tiled=True)
    sources, items, width = rows_in.shape
    rows_flat = rows_in.reshape(sources * items, width)
    grads_flat = grads_in.reshape(sources * items, width)
    gate_pre = lax.dot_general(rows_flat, weight_gate, contract, preferred_element_type=jnp.float32)
    up_pre = lax.dot_general(rows_flat, weight_up, contract, preferred_element_type=jnp.float32)
    back = lax.dot_general(grads_flat, weight_down, contract, preferred_element_type=jnp.float32)
    input_part, gate_part = finish(gate_pre, up_pre, back, weight_gate, weight_up)
    input_part, gate_part = close_expert(input_part, gate_part, sources, items, model_width)
    back_input, back_gate = (
        lax.all_to_all(input_part, ("dp", "expert"), split_axis=0, concat_axis=0, tiled=True),
        lax.all_to_all(gate_part, ("dp", "expert"), split_axis=0, concat_axis=0, tiled=True),
    )
    share_width = back_input.shape[2]
    picked = jnp.take(back_input.reshape(expert_count * slot_cap, share_width), slot_of, axis=0)
    picked = picked.astype(jnp.float32).reshape(token_rows, pick_count, share_width)
    weighted = jnp.sum(picked * gates[:, :, None], axis=1)
    gate_pairs = (
        jnp.take(back_gate.reshape(-1), slot_of, axis=0)
        .astype(jnp.float32)
        .reshape(token_rows, pick_count)
    )
    gate_out = lax.psum(gate_pairs.astype(jnp.bfloat16), "tensor").astype(jnp.float32)
    return (weighted.astype(jnp.bfloat16), gate_out)


def solution(mesh):
    return jax.shard_map(
        body,
        mesh=mesh,
        in_specs=(
            P(("dp", "expert"), "tensor"),
            P(("dp", "expert")),
            P(("dp", "expert"), "tensor"),
            P(("dp", "expert"), None),
            P(("dp", "expert"), None),
            P(("dp", "expert"), "tensor", None),
            P(("dp", "expert"), "tensor", None),
            P(("dp", "expert"), "tensor", None),
        ),
        out_specs=(P(("dp", "expert"), "tensor"), P(("dp", "expert"), None)),
        check_vma=False,
    )
```

profile of v0, /device:TPU:0, one launch (start us, length us, event | category | flops | bytes accessed | tf_op | source)
XLA Modules:
  0.0 390.9 jit_solution(13558617288145878125)
XLA Ops:
  7.2 0.0 copy-start
  7.2 0.9 copy.21
  8.1 0.1 eq.26
  8.2 0.1 reshape.113
  8.3 4.5 %reduce-window.6 = s32[16,8,128]{2,1,0:T(8,128)S(1)} reduce-window(s32[16,8,128]{2,1,0:T(8,128)S(1)} %fusion.15, s32[]{:T(128)} %constant.59.clone.1), window={size=1x1x128 pad=0_0x0_0x127_0}, to_apply=%region_0.0 | reduce-window | flops 2080768 | bytes 131076 | tf_op jit(solution)/shard_map/reduce-window
  12.9 0.1 slice.16
  12.9 0.1 copy.24
  13.1 0.1 copy.25
  13.2 0.1 broadcast_add_fusion
  13.3 0.1 mul.66
  13.4 4.3 %scatter_custom_fusion = s32[1024]{0:T(1024)S(1)} fusion(s32[1024]{0:T(1024)S(1)} %bitcast.56, s32[1024]{0:T(1024)S(1)} %add_select_fusion, s32[]{:T(128)} %constant.62.clone.1), kind=kCustom, calls=%fused_computation.51 | custom fusion | bytes 4100 | tf_op jit(solution)/shard_map/scatter | solution.py:18
  17.8 1.1 multiply_convert_fusion.5
  18.8 9.9 %all_gather.7 = bf16[128,2048]{1,0:T(8,128)(2,1)S(1)} all-gather(bf16[128,1024]{1,0:T(8,128)(2,1)S(1)} %multiply_convert_fusion.5), channel_id=1, replica_groups=mesh['dp'=2,'tensor'=2,'expert'=8] {'tensor'}, dimensions={1}, use_global_device_ids=true | all-gather | bytes 786432 | tf_op jit(solution)/shard_map/all_gather | solution.py:56
  28.7 8.2 %all_gather.6 = bf16[128,2048]{1,0:T(8,128)(2,1)S(1)} all-gather(bf16[128,1024]{1,0:T(8,128)(2,1)S(1)} %copy-done.5), channel_id=1, replica_groups=mesh['dp'=2,'tensor'=2,'expert'=8] {'tensor'}, dimensions={1}, use_global_device_ids=true | all-gather | bytes 786432 | tf_op jit(solution)/shard_map/all_gather | solution.py:57
  36.9 6.0 %gather_fusion.3 = bf16[1024,2048]{1,0:T(8,128)(2,1)} fusion(bf16[128,2048]{1,0:T(8,128)(2,1)S(1)} %all_gather.7, s32[1024]{0:T(1024)S(1)} %fusion.19), kind=kCustom, calls=%fused_computation.1.clone | custom fusion | bytes 8392704 | tf_op jit(solution)/shard_map/jit(_take)/gather | solution.py:59
  42.9 6.1 %gather_fusion.2 = bf16[1024,2048]{1,0:T(8,128)(2,1)} fusion(bf16[128,2048]{1,0:T(8,128)(2,1)S(1)} %all_gather.6, s32[1024]{0:T(1024)S(1)} %fusion.19), kind=kCustom, calls=%fused_computation.clone | custom fusion | bytes 8392704 | tf_op jit(solution)/shard_map/jit(_take)/gather | solution.py:62
  49.0 5.3 %broadcast_select_fusion.1 = (bf16[1024,2048]{1,0:T(8,128)(2,1)}, bf16[1024,2048]{1,0:T(8,128)(2,1)S(1)}) fusion(bf16[1024,2048]{1,0:T(8,128)(2,1)} %gather_fusion.2, pred[1024]{0:T(1024)(128)(4,1)S(1)} %compare_and_fusion.1, bf16[1024,2048]{1,0:T(8,128)(2,1)} %gather_fusion.3), kind=kLoop, calls=%fused_computation.8 | loop fusion | flops 4194304 | bytes 16778240 | tf_op jit(solution)/shard_map/jit(_take)/select_n | solution.py:62
  54.2 100.2 %all_to_all.21 = bf16[16,64,2048]{2,1,0:T(8,128)(2,1)} all-to-all(bf16[16,64,2048]{2,1,0:T(8,128)(2,1)S(1)} %bitcast.50), channel_id=1, replica_groups=mesh['dp'=2,'tensor'=2,'expert'=8] {'dp','expert'}, dimensions={0} | all-to-all | bytes 8388608 | tf_op jit(solution)/shard_map/all_to_all | solution.py:65
  154.5 4.5 %all-to-all-start = ((bf16[16,64,2048]{2,1,0:T(8,128)(2,1)}), bf16[16,64,2048]{2,1,0:T(8,128)(2,1)}, u32[]{:S(2)}, u32[]{:S(2)}) async-start(bf16[16,64,2048]{2,1,0:T(8,128)(2,1)} %bitcast.48), calls=%async_computation | async-start | bytes 8388608 | tf_op jit(solution)/shard_map/all_to_all | solution.py:66
  159.0 0.2 reduce-scatter.2.cloned.1.call-start
  159.2 0.0 copy-done
  159.3 0.0 copy-start.1
  159.3 0.0 copy-start.2
  159.3 4.2 %fusion.2 = f32[1024,384]{0,1:T(8,128)S(1)} fusion(bf16[1024,2048]{1,0:T(8,128)(2,1)} %bitcast.51, bf16[1,384,2048]{2,1,0:T(8,128)(2,1)S(1)} %copy-done), kind=kOutput, calls=%fused_computation.12 | convolution fusion | flops 1610612736 | bytes 7340032 | tf_op jit(solution)/shard_map/dot_general | solution.py:70
  163.4 0.0 copy-done.1
  163.5 0.0 copy-done.2
  163.5 3.0 fusion.5
  166.5 82.2 %all-to-all-done = bf16[16,64,2048]{2,1,0:T(8,128)(2,1)} async-done(((bf16[16,64,2048]{2,1,0:T(8,128)(2,1)}), bf16[16,64,2048]{2,1,0:T(8,128)(2,1)}, u32[]{:S(2)}, u32[]{:S(2)}) %all-to-all-start) | async-done | bytes 4194336 | tf_op jit(solution)/shard_map/all_to_all | solution.py:66
  248.7 5.2 %multiply_reduce_fusion.1 = (bf16[1024]{0:T(1024)(128)(2,1)S(1)}, f32[1024,384]{0,1:T(8,128)S(1)}) fusion(f32[1024,384]{0,1:T(8,128)} %fusion.5, f32[1024,384]{0,1:T(8,128)S(1)} %fusion.2, bf16[1024,2048]{1,0:T(8,128)(2,1)} %bitcast.5, bf16[1,384,2048]{2,1,0:T(8,128)(2,1)} %param.17), kind=kOutput, calls=%fused_computation.19 | convolution fusion | flops 1614150656 | bytes 10487808 | tf_op jit(solution)/shard_map/dot_general | solution.py:72
  253.9 0.0 copy-start.3
  253.9 2.8 fusion
  256.7 0.0 copy-done.3
  256.7 4.6 %add_convert_fusion = bf16[1024,2048]{1,0:T(8,128)(2,1)} fusion(f32[1024,2048]{1,0:T(8,128)S(1)} %fusion, bf16[1,384,2048]{2,1,0:T(8,128)(2,1)S(1)} %copy-done.3, f32[1024,384]{0,1:T(8,128)S(1)} %get-tuple-element.12, f32[1024,384]{0,1:T(8,128)S(1)} %fusion.2), kind=kOutput, calls=%fused_computation.5 | convolution fusion | flops 1617166336 | bytes 17301504 | tf_op jit(solution)/shard_map/dot_general | solution.py:30
  261.3 0.0 reduce-scatter.2.cloned.1.call-update
  261.4 0.1 convert_element_type.71
  261.4 14.0 %all_to_all.22 = bf16[16,1,64]{2,1,0:T(2,128)(2,1)S(1)} all-to-all(bf16[16,1,64]{2,1,0:T(2,128)(2,1)S(1)} %convert_element_type.71), channel_id=1, replica_groups=mesh['dp'=2,'tensor'=2,'expert'=8] {'dp','expert'}, dimensions={0} | all-to-all | bytes 4096 | tf_op jit(solution)/shard_map/all_to_all | solution.py:77
  275.5 43.5 %reduce-scatter.2.cloned.1.call-done = bf16[16,64,1024]{2,1,0:T(8,128)(2,1)} async-done(((bf16[16,64,2048]{2,1,0:T(8,128)(2,1)}), bf16[16,64,1024]{2,1,0:T(8,128)(2,1)}) %reduce-scatter.2.cloned.1.call-update) | async-done | bytes 2097168 | tf_op jit(solution)/shard_map/reduce_scatter | solution.py:37
  319.0 5.7 %all-to-all-start.2 = ((bf16[16,64,1024]{2,1,0:T(8,128)(2,1)}), bf16[16,64,1024]{2,1,0:T(8,128)(2,1)}, u32[]{:S(2)}, u32[]{:S(2)}) async-start(bf16[16,64,1024]{2,1,0:T(8,128)(2,1)} %reduce-scatter.2.cloned.1.call-done), calls=%async_computation.3 | async-start | bytes 4194304 | tf_op jit(solution)/shard_map/all_to_all | solution.py:76
  324.6 0.1 reduce_sum.32
  324.7 0.1 copy.26
  324.9 0.1 reshape.121
  325.0 6.8 %gather_fusion.1 = bf16[1024]{0:T(1024)(128)(2,1)S(1)} fusion(bf16[1024]{0:T(1024)(128)(2,1)S(1)} %reshape.121, s32[1024]{0:T(1024)S(1)} %broadcast_clamp_fusion), kind=kCustom, calls=%fused_computation.3 | custom fusion | bytes 8192 | tf_op jit(solution)/shard_map/jit(_take)/gather | solution.py:84
  331.8 0.1 gather.18
  331.9 7.6 %psum.7 = bf16[128,8]{1,0:T(8,128)(2,1)S(1)} all-reduce(bf16[128,8]{1,0:T(8,128)(2,1)S(1)} %get-tuple-element.7), channel_id=1, replica_groups=mesh['dp'=2,'tensor'=2,'expert'=8] {'tensor'}, use_global_device_ids=true, to_apply=%region_7.9 | all-reduce | flops 1024 | bytes 4096 | tf_op jit(solution)/shard_map/psum | solution.py:88
  339.5 0.7 copy.28
  340.2 32.0 %all-to-all-done.2 = bf16[16,64,1024]{2,1,0:T(8,128)(2,1)} async-done(((bf16[16,64,1024]{2,1,0:T(8,128)(2,1)}), bf16[16,64,1024]{2,1,0:T(8,128)(2,1)}, u32[]{:S(2)}, u32[]{:S(2)}) %all-to-all-start.2) | async-done | bytes 2097184 | tf_op jit(solution)/shard_map/all_to_all | solution.py:76
  372.2 7.9 %gather_fusion = bf16[1024,1024]{1,0:T(8,128)(2,1)} fusion(bf16[1024,1024]{1,0:T(8,128)(2,1)} %bitcast.12, s32[1024]{0:T(1024)S(1)} %broadcast_clamp_fusion), kind=kCustom, calls=%fused_computation.2 | custom fusion | bytes 4198400 | tf_op jit(solution)/shard_map/jit(_take)/gather | solution.py:80
  380.2 3.9 multiply_reduce_fusion
  (18 shorter events, 0.2 us)
Async XLA Ops:
  7.2 152.1 %copy-start = (bf16[1,384,2048]{2,1,0:T(8,128)(2,1)S(1)}, bf16[1,384,2048]{2,1,0:T(8,128)(2,1)}, u32[]{:S(2)}) copy-start(bf16[1,384,2048]{2,1,0:T(8,128)(2,1)} %param.15) | copy-start | bytes 4718596
  7.2 21.6 %copy-start.5 = (bf16[128,1024]{1,0:T(8,128)(2,1)S(1)}, bf16[128,1024]{1,0:T(8,128)(2,1)}, u32[]{:S(2)}) copy-start(bf16[128,1024]{1,0:T(8,128)(2,1)} %param.12) | copy-start | bytes 786436
  154.5 94.2 %all-to-all-start = ((bf16[16,64,2048]{2,1,0:T(8,128)(2,1)}), bf16[16,64,2048]{2,1,0:T(8,128)(2,1)}, u32[]{:S(2)}, u32[]{:S(2)}) async-start(bf16[16,64,2048]{2,1,0:T(8,128)(2,1)} %bitcast.48), calls=%async_computation | async-start | bytes 8388608 | tf_op jit(solution)/shard_map/all_to_all | solution.py:66
  159.0 159.9 %reduce-scatter.2.cloned.1.call-start = ((), (), s32[]{:S(2)}) async-start(), calls=%async_computation.5 | async-start | bytes 6291456 | tf_op jit(solution)/shard_map/reduce_scatter | solution.py:37
  159.3 4.2 %copy-start.1 = (bf16[16,64,2048]{2,1,0:T(8,128)(2,1)S(1)}, bf16[16,64,2048]{2,1,0:T(8,128)(2,1)}, u32[]{:S(2)}) copy-start(bf16[16,64,2048]{2,1,0:T(8,128)(2,1)} %all_to_all.21) | copy-start | bytes 12582916
  159.3 4.2 %copy-start.2 = (bf16[1,384,2048]{2,1,0:T(8,128)(2,1)S(1)}, bf16[1,384,2048]{2,1,0:T(8,128)(2,1)}, u32[]{:S(2)}) copy-start(bf16[1,384,2048]{2,1,0:T(8,128)(2,1)} %param.16) | copy-start | bytes 4718596
  248.7 5.2 %copy-start.4 = (f32[1024,384]{0,1:T(8,128)S(1)}, f32[1024,384]{0,1:T(8,128)}, u32[]{:S(2)}) copy-start(f32[1024,384]{0,1:T(8,128)} %fusion.5) | copy-start | bytes 4718596
  253.9 2.8 copy-start.3
  275.5 49.2 %copy-start.6 = (f32[128,8]{0,1:T(8,128)S(1)}, f32[128,8]{0,1:T(8,128)}, u32[]{:S(2)}) copy-start(f32[128,8]{0,1:T(8,128)} %param.14) | copy-start | bytes 12292
  319.0 53.3 %all-to-all-start.2 = ((bf16[16,64,1024]{2,1,0:T(8,128)(2,1)}), bf16[16,64,1024]{2,1,0:T(8,128)(2,1)}, u32[]{:S(2)}, u32[]{:S(2)}) async-start(bf16[16,64,1024]{2,1,0:T(8,128)(2,1)} %reduce-scatter.2.cloned.1.call-done), calls=%async_computation.3 | async-start | bytes 4194304 | tf_op jit(solution)/shard_map/all_to_all | solution.py:76
Sparse Core Ops, SparseCore 0:
  261.5 57.4 reduce-scatter.1
where the time goes:
time: 391 us
  waiting for transfers between devices  158 us (40%)
  blocking collectives  140 us (36%)
  local copies, waits for them, and re-layouts  33.7 us (9%)
  matrix products  19.8 us (5%)
  other arithmetic  15 us (4%)
  between operations  14.3 us (4%)
  starting transfers between devices  10.4 us (3%)
    all_to_all x1, blocking collectives, body(): lax.all_to_all(send_x, ('dp', 'expert'), split_axis=0, concat_axis=0, til...  100 us
    all_to_all x1, waiting for transfers between devices, body(): lax.all_to_all(send_grad, ('dp', 'expert'), split_axis=0, concat_axis=0,...  82.2 us
    reduce_scatter x1, waiting for transfers between devices, close_expert(): lax.psum_scatter(shaped.astype(jnp.float32).astype(jnp.bfloat16), 'tensor...  43.5 us
    all_to_all x1, waiting for transfers between devices, body(): lax.all_to_all(input_part, ('dp', 'expert'), split_axis=0, concat_axis=0,...  32 us
    all_to_all x1, blocking collectives, body(): lax.all_to_all(gate_part, ('dp', 'expert'), split_axis=0, concat_axis=0,...  14 us
    all_gather x1, blocking collectives, body(): lax.all_gather(dequant, 'tensor', axis=1, tiled=True)  9.91 us
    all_gather x1, blocking collectives, body(): lax.all_gather(out_grad, 'tensor', axis=1, tiled=True)  8.16 us
    gather x1, local copies, waits for them, and re-layouts, body(): jnp.take(back_input.reshape(expert_count * slot_cap, share_width), slot_o...  7.92 us
  transfers between devices with their start and end apart: 3, of which 3 were waited for; matrix products, arithmetic and copies ran while one was open for 4% of the time, Pallas kernels for 0%

commit v1 on v0

--- a/solution.py
+++ b/solution.py
@@ -1,6 +1,9 @@
+import functools
 import jax
 import jax.numpy as jnp
 from jax import lax
+from jax.experimental import pallas as pl
+from jax.experimental.pallas import tpu as pltpu
 from jax.sharding import PartitionSpec as P
 
 
@@ -40,7 +43,7 @@
     return (summed, gate_shaped)
 
 
-def body(checkpoint, scales, out_grad, expert_ids, gates, w_gate, w_up, w_down):
+def body_routed(checkpoint, scales, out_grad, expert_ids, gates, w_gate, w_up, w_down):
     expert_count = lax.axis_size("dp") * lax.axis_size("expert")
     token_rows = checkpoint.shape[0]
     pick_count = expert_ids.shape[1]
@@ -87,6 +90,199 @@
     )
     gate_out = lax.psum(gate_pairs.astype(jnp.bfloat16), "tensor").astype(jnp.float32)
     return (weighted.astype(jnp.bfloat16), gate_out)
+
+
+def pack_picks(expert_ids, gates, width):
+    high = gates.astype(jnp.bfloat16)
+    low = (gates - high.astype(jnp.float32)).astype(jnp.bfloat16)
+    parts = [expert_ids.astype(jnp.bfloat16), high, low]
+    flat = jnp.concatenate([part.T.reshape(-1) for part in parts])
+    rows = -(-flat.shape[0] // (16 * width)) * 16
+    return jnp.pad(flat, (0, rows * width - flat.shape[0])).reshape(rows, width)
+
+
+def expert_kernel(tops, way, info_ref, u_ref, v_ref, m_ref, n_ref, wg_ref, wu_ref, wd_ref, *outs):
+    f32 = jnp.float32
+    contract = (((1,), (1,)), ((), ()))
+    _, token_rows, width = m_ref.shape
+    rows = 2 * token_rows
+    half = token_rows // 2
+    units = wg_ref.shape[0] // 2
+    mine = pl.ds(pl.multiple_of(info_ref[0] * width, width), width)
+    other = pl.ds(pl.multiple_of((1 - info_ref[0]) * width, width), width)
+
+    def project(first, second, w_ref):
+        low = lax.dot_general(first, w_ref[:, mine], contract, preferred_element_type=f32)
+        return low + lax.dot_general(second, w_ref[:, other], contract, preferred_element_type=f32)
+
+    def weight_of(ref, expert):
+        pick_rows = ref[rows:]
+
+        def segment(kind, k):
+            at = (kind * tops + k) * token_rows
+            row, col = at // width, at % width
+            return pick_rows[row : row + 1, col : col + token_rows].astype(f32)
+
+        total = jnp.zeros((1, token_rows), f32)
+        for k in range(tops):
+            chosen = segment(0, k) == expert.astype(f32)
+            total = total + jnp.where(chosen, segment(1, k) + segment(2, k), 0.0)
+        return jnp.broadcast_to(total, (128, token_rows)).T[:, :1]
+
+    x_mine = jnp.concatenate([u_ref[:token_rows], v_ref[:token_rows]], axis=0)
+    x_other = jnp.concatenate([u_ref[token_rows:rows], v_ref[token_rows:rows]], axis=0)
+    gate_pre = project(x_mine, x_other, wg_ref)
+    up_pre = project(x_mine, x_other, wu_ref)
+    back = project(m_ref[...].reshape(rows, width), n_ref[...].reshape(rows, width), wd_ref)
+    sigma = jax.nn.sigmoid(gate_pre)
+    swish = gate_pre * sigma
+    hidden = (swish * up_pre).astype(jnp.bfloat16)
+    product = hidden.astype(f32) * back
+    weights = []
+    for which in range(2):
+        expert = info_ref[1 + which]
+        weights.append(jnp.concatenate([weight_of(u_ref, expert), weight_of(v_ref, expert)], axis=0))
+        term = jnp.sum(product[:, which * units : (which + 1) * units], axis=1, keepdims=True)
+        term = term.astype(jnp.bfloat16).astype(f32)
+        outs[-1][which] = jnp.broadcast_to(term, (rows, 128)).T[:8]
+    lane = lax.broadcasted_iota(jnp.int32, back.shape, 1)
+    scaled = back * jnp.where(lane < units, weights[0], weights[1])
+    d_gate = (scaled * up_pre * sigma * (1.0 + gate_pre * (1.0 - sigma))).astype(jnp.bfloat16)
+    d_up = (scaled * swish).astype(jnp.bfloat16)
+
+    def spread(cols):
+        piece = jnp.dot(d_gate, wg_ref[:, cols], preferred_element_type=f32)
+        piece = piece + jnp.dot(d_up, wu_ref[:, cols], preferred_element_type=f32)
+        return piece.astype(jnp.bfloat16)
+
+    far, near = spread(other), spread(mine)
+    if way == "x":
+        send, keep = outs[:2]
+        send[...], keep[...] = far.reshape(2, token_rows, width), near.reshape(2, token_rows, width)
+    elif way == "y":
+        send, keep = outs[:2]
+        keep[0], send[0] = near[:token_rows], near[token_rows:]
+        keep[1], send[1] = far[:token_rows], far[token_rows:]
+    else:
+        a_send, a_keep, b_send, b_keep = outs[:4]
+        a_send[0], a_send[1] = far[:half], far[token_rows : token_rows + half]
+        b_keep[1], b_send[1] = far[half:token_rows], far[token_rows + half :]
+        a_keep[0], a_keep[1] = near[:half], near[token_rows : token_rows + half]
+        b_keep[0], b_send[0] = near[half:token_rows], near[token_rows + half :]
+
+
+def run_expert(tops, way, info, u, v, m, n, wg, wu, wd):
+    _, token_rows, width = m.shape
+    hidden, model_width = wg.shape
+    rows = 2 * token_rows
+    vmem = pl.BlockSpec(memory_space=pltpu.VMEM)
+    count, part = (4, token_rows // 2) if way == "both" else (2, token_rows)
+    share = jax.ShapeDtypeStruct((2, part, width), jnp.bfloat16)
+    return pl.pallas_call(
+        functools.partial(expert_kernel, tops, way),
+        in_specs=[pl.BlockSpec(memory_space=pltpu.SMEM)] + [vmem] * 7,
+        out_specs=[vmem] * (count + 1),
+        out_shape=[share] * count + [jax.ShapeDtypeStruct((2, 8, rows), jnp.float32)],
+        compiler_params=pltpu.CompilerParams(vmem_limit_bytes=32 * 1024 * 1024),
+        cost_estimate=pl.CostEstimate(
+            flops=10 * rows * hidden * model_width,
+            bytes_accessed=6 * rows * model_width + 6 * hidden * model_width,
+            transcendentals=rows * hidden,
+        ),
+    )(info, u, v, m, n, wg, wu, wd)
+
+
+def add(left, right):
+    return (left.astype(jnp.float32) + right.astype(jnp.float32)).astype(jnp.bfloat16)
+
+
+def body_dense(checkpoint, scales, out_grad, expert_ids, gates, w_gate, w_up, w_down):
+    experts = lax.axis_size("expert")
+    ring = experts // 2
+    core = lax.axis_index("dp")
+    place = lax.axis_index("expert")
+    slow, fast = place // 2, place % 2
+    side = lax.axis_index("tensor")
+    token_rows, width = checkpoint.shape
+    tops = expert_ids.shape[1]
+
+    def over_x(value):
+        return lax.ppermute(value, "tensor", [(0, 1), (1, 0)])
+
+    def over_core(value):
+        return lax.ppermute(value, "dp", [(0, 1), (1, 0)])
+
+    def over_y(value):
+        return lax.ppermute(value, "expert", [(e, e ^ 1) for e in range(experts)])
+
+    def over_z(value, shift):
+        pairs = [(e, (e // 2 + shift) % ring * 2 + e % 2) for e in range(experts)]
+        return lax.ppermute(value, "expert", pairs)
+
+    def after(values, *earlier):
+        return lax.optimization_barrier((values, earlier))[0]
+
+    x = (checkpoint.astype(jnp.float32) * scales[:, None]).astype(jnp.bfloat16)
+    picks = pack_picks(expert_ids, gates, width)
+    m = [jnp.stack([out_grad, over_y(out_grad)])]
+    u = [jnp.concatenate([x, over_x(x), picks])]
+    others = [over_core(w[0]) for w in (w_gate, w_up, w_down)]
+    wg, wu, wd = [jnp.concatenate([w[0], o], axis=0) for w, o in zip((w_gate, w_up, w_down), others)]
+    info = jnp.stack([side, core * experts + place, (1 - core) * experts + place])
+    sums, terms = [], []
+    total = None
+    for step in range(ring):
+        last_step = step == ring - 1
+        v, n = over_y(u[step]), over_x(m[step])
+        way = "both" if step >= ring - 2 else "yx"[step % 2]
+        if not last_step:
+            u.append(over_z(u[step], 1))
+            m.append(over_z(m[step], 1))
+        *outs, term = run_expert(tops, way, info, u[step], v, m[step], n, wg, wu, wd)
+        if not last_step:
+            u[-1], m[-1] = after((u[-1], m[-1]), outs, sums[-1:])
+        terms.append(term[:, 0])
+        if way == "both":
+            a_send, a_keep, b_send, b_keep = outs
+            a_got, b_got = over_x(a_send), over_y(b_send)
+            a_next, b_next = add(a_keep[1], a_got[1]), add(b_keep[1], b_got[1])
+            if last_step:
+                for back in range(1, ring - 1):
+                    total = over_z(sums[back] if total is None else add(sums[back], total), 1)
+                a_next, b_next = after((a_next, b_next), total)
+                terms = after(terms, a_got, b_got)
+            a = add(add(a_keep[0], a_got[0]), over_y(a_next))
+            b = add(add(b_keep[0], b_got[0]), over_x(b_next))
+            sums.append(jnp.concatenate([a, b], axis=0))
+        else:
+            first, second = (over_x, over_y) if way == "x" else (over_y, over_x)
+            send, keep = outs
+            got = first(send)
+            sums.append(add(add(keep[0], got[0]), second(add(keep[1], got[1]))))
+    total = sums[-1] if total is None else add(sums[-1], total)
+    if ring > 1:
+        total = add(sums[0], over_z(total, 1))
+    term = jnp.stack(terms).reshape(ring, 2, 2, token_rows)
+    term = term + over_x(term)
+    term = jnp.stack([term[:, :, 0], over_y(term[:, :, 1])], axis=1)
+    gate_out = jnp.zeros(gates.shape, jnp.float32)
+    for step in range(ring):
+        here = term[step] if step == 0 else over_z(term[step], -step)
+        for way in range(2):
+            for which in range(2):
+                owner = (core ^ which) * experts + (slow + step) % ring * 2 + (fast ^ way)
+                gate_out = gate_out + jnp.where(expert_ids == owner, here[way, which][:, None], 0.0)
+    return (total, gate_out)
+
+
+def body(checkpoint, scales, out_grad, expert_ids, gates, w_gate, w_up, w_down):
+    experts = lax.axis_size("expert")
+    token_rows, width = checkpoint.shape
+    pairs = lax.axis_size("dp") == 2 and lax.axis_size("tensor") == 2 and experts % 2 == 0
+    fits = token_rows % 128 == 0 and width % token_rows == 0
+    dense = pairs and fits and expert_ids.shape[1] >= experts
+    chosen = body_dense if dense else body_routed
+    return chosen(checkpoint, scales, out_grad, expert_ids, gates, w_gate, w_up, w_down)
 
 
 def solution(mesh):

time: 391 us -> 155 us (0.40)
  blocking collectives: 140 us -> 0 us
  waiting for transfers between devices: 158 us -> 65.6 us
  starting transfers between devices: 10.4 us -> 45.5 us
  local copies, waits for them, and re-layouts: 33.7 us -> 5.8 us
  Pallas kernels: 0 us -> 22 us
  matrix products: 19.8 us -> 0 us
  between operations: 14.3 us -> 0.95 us
    all_to_all x2 -> x0, waiting for transfers between devices: 114 us -> none  [the longest x1 82.2 us: body(): lax.all_to_all(send_grad, ('dp', 'expert'), split_axis=0, concat_axis=0,...]
    all_to_all x2 -> x0, blocking collectives: 114 us -> none  [the longest x1 100 us: body(): lax.all_to_all(send_x, ('dp', 'expert'), split_axis=0, concat_axis=0, til...]
    ppermute x0 -> x39, waiting for transfers between devices: none -> 65.6 us  [the longest x12 38.6 us: over_x(): return lax.ppermute(value, 'tensor', [(0, 1), (1, 0)])]
    ppermute x0 -> x39, starting transfers between devices: none -> 45.5 us  [the longest x12 16.9 us: over_x(): return lax.ppermute(value, 'tensor', [(0, 1), (1, 0)])]
    reduce_scatter x1 -> x0, waiting for transfers between devices: 43.5 us -> none  [close_expert(): lax.psum_scatter(shaped.astype(jnp.float32).astype(jnp.bfloat16), 'tensor...]
    gather x5 -> x0, local copies, waits for them, and re-layouts: 26.9 us -> none  [the longest x1 7.92 us: body(): jnp.take(back_input.reshape(expert_count * slot_cap, share_width), slot_o...]
    pallas_call x0 -> x4, Pallas kernels: none -> 22 us  [run_expert(): pl.pallas_call(functools.partial(expert_kernel, tops, way), in_specs=[pl....]
    dot_general x5 -> x0, matrix products: 19.8 us -> none  [the longest x1 5.2 us: body(): lax.dot_general(grads_flat, weight_down, contract, preferred_element_type...]
  transfers between devices with their start and end apart: 3 -> 39, of which waited for: 3 -> 15; matrix products, arithmetic and copies ran while one was open for 4% -> 9% of each run, Pallas kernels for 0% -> 14%
where the time goes in v1:
time: 155 us
  waiting for transfers between devices  65.6 us (42%)
  starting transfers between devices  45.5 us (29%)
  Pallas kernels  22 us (14%)
  other arithmetic  15.2 us (10%)
  local copies, waits for them, and re-layouts  5.8 us (4%)
    ppermute x12, waiting for transfers between devices, over_x(): return lax.ppermute(value, 'tensor', [(0, 1), (1, 0)])  38.6 us
    pallas_call x4, Pallas kernels, run_expert(): pl.pallas_call(functools.partial(expert_kernel, tops, way), in_specs=[pl....  22 us
    ppermute x12, waiting for transfers between devices, over_y(): return lax.ppermute(value, 'expert', [(e, e ^ 1) for e in range(experts)])  18.8 us
    ppermute x12, starting transfers between devices, over_x(): return lax.ppermute(value, 'tensor', [(0, 1), (1, 0)])  16.9 us
    ppermute x12, starting transfers between devices, over_z(): return lax.ppermute(value, 'expert', pairs)  16.1 us
    ppermute x12, starting transfers between devices, over_y(): return lax.ppermute(value, 'expert', [(e, e ^ 1) for e in range(experts)])  11.9 us
    ppermute x12, waiting for transfers between devices, over_z(): return lax.ppermute(value, 'expert', pairs)  8.21 us
    concatenate x3, other arithmetic, body_dense(): jnp.concatenate([w[0], o], axis=0)  7.21 us
  transfers between devices with their start and end apart: 39, of which 15 were waited for; matrix products, arithmetic and copies ran while one was open for 9% of the time, Pallas kernels for 14%

profile of v1, /device:TPU:0, one launch (start us, length us, event | category | flops | bytes accessed | tf_op | source)
XLA Modules:
  0.0 155.0 jit_solution(15469836761003761014)
XLA Ops:
  2.3 3.0 %collective-permute-start = (bf16[128,1024]{1,0:T(8,128)(2,1)S(1)}, bf16[128,1024]{1,0:T(8,128)(2,1)S(1)}, u32[]{:S(2)}, u32[]{:S(2)}) collective-permute-start(bf16[128,1024]{1,0:T(8,128)(2,1)S(1)} %multiply_convert_fusion), channel_id=1, source_target_pairs={{0,8},{8,0},{1,9},{9,1},{2,10},{10,2},{3,11},{11,3},{4,12},{12,4},... | collective-permute-start | bytes 786440 | tf_op jit(solution)/shard_map/ppermute | solution.py:210
  5.3 1.5 collective-permute-start.2
  8.4 3.4 %collective-permute-done = bf16[128,1024]{1,0:T(8,128)(2,1)S(1)} collective-permute-done((bf16[128,1024]{1,0:T(8,128)(2,1)S(1)}, bf16[128,1024]{1,0:T(8,128)(2,1)S(1)}, u32[]{:S(2)}, u32[]{:S(2)}) %collective-permute-start) | collective-permute-done | bytes 262176 | tf_op jit(solution)/shard_map/ppermute | solution.py:210
  11.9 1.9 %collective-permute-start.9 = (bf16[272,1024]{1,0:T(8,128)(2,1)S(1)}, bf16[272,1024]{1,0:T(8,128)(2,1)S(1)}, u32[]{:S(2)}, u32[]{:S(2)}) collective-permute-start(bf16[272,1024]{1,0:T(8,128)(2,1)S(1)} %pad_maximum_fusion.3.u_ref), channel_id=1, source_target_pairs={{0,2},{1,3},{2,4},{3,5},{4,6},{5,7},{6,0},{7,1},{8,10},{9,11},{10,... | collective-permute-start | bytes 1671176 | tf_op jit(solution)/shard_map/ppermute | solution.py:220
  13.8 1.5 collective-permute-start.1
  16.3 1.1 copy-done.9
  17.4 1.6 %collective-permute-start.10 = (bf16[2,128,1024]{2,1,0:T(8,128)(2,1)S(1)}, bf16[2,128,1024]{2,1,0:T(8,128)(2,1)S(1)}, u32[]{:S(2)}, u32[]{:S(2)}) collective-permute-start(bf16[2,128,1024]{2,1,0:T(8,128)(2,1)S(1)} %pad_maximum_fusion.4.m_ref), channel_id=1, source_target_pairs={{0,2},{1,3},{2,4},{3,5},{4,6},{5,7},{6,0},{7,1},{8,10},{9,11},{10,... | collective-permute-start | bytes 1572872 | tf_op jit(solution)/shard_map/ppermute | solution.py:220
  19.0 2.0 %pad_maximum_fusion.wg_ref = bf16[768,2048]{1,0:T(8,128)(2,1)S(1)} fusion(bf16[384,2048]{1,0:T(8,128)(2,1)} %copy-done.9, bf16[384,2048]{1,0:T(8,128)(2,1)S(1)} %bitcast.122), kind=kLoop, calls=%fused_computation | loop fusion | flops 6291456 | bytes 6291456 | tf_op jit(solution)/shard_map/concatenate | solution.py:230
  21.0 1.6 %collective-permute-start.3 = (bf16[2,128,1024]{2,1,0:T(8,128)(2,1)S(1)}, bf16[2,128,1024]{2,1,0:T(8,128)(2,1)S(1)}, u32[]{:S(2)}, u32[]{:S(2)}) collective-permute-start(bf16[2,128,1024]{2,1,0:T(8,128)(2,1)S(1)} %pad_maximum_fusion.4.m_ref), channel_id=1, source_target_pairs={{0,8},{8,0},{1,9},{9,1},{2,10},{10,2},{3,11},{11,3},{4,12},{12,4},... | collective-permute-start | bytes 1572872 | tf_op jit(solution)/shard_map/ppermute | solution.py:210
  22.6 2.1 %pad_maximum_fusion.1.wu_ref = bf16[768,2048]{1,0:T(8,128)(2,1)S(1)} fusion(bf16[384,2048]{1,0:T(8,128)(2,1)} %collective-permute-done.5, bf16[384,2048]{1,0:T(8,128)(2,1)S(1)} %bitcast.124), kind=kLoop, calls=%fused_computation.1 | loop fusion | flops 6291456 | bytes 6291456 | tf_op jit(solution)/shard_map/concatenate | solution.py:230
  24.7 3.1 %pad_maximum_fusion.2.wd_ref = bf16[768,2048]{1,0:T(8,128)(2,1)S(1)} fusion(bf16[384,2048]{1,0:T(8,128)(2,1)} %collective-permute-done.6, bf16[384,2048]{1,0:T(8,128)(2,1)S(1)} %bitcast.126), kind=kLoop, calls=%fused_computation.2 | loop fusion | flops 6291456 | bytes 6291456 | tf_op jit(solution)/shard_map/concatenate | solution.py:230
  27.9 5.4 %collective-permute-done.3.n_ref = bf16[2,128,1024]{2,1,0:T(8,128)(2,1)S(1)} collective-permute-done((bf16[2,128,1024]{2,1,0:T(8,128)(2,1)S(1)}, bf16[2,128,1024]{2,1,0:T(8,128)(2,1)S(1)}, u32[]{:S(2)}, u32[]{:S(2)}) %collective-permute-start.3) | collective-permute-done | bytes 524320 | tf_op jit(solution)/shard_map/ppermute | solution.py:210
  33.3 5.2 %shard_map.95 = (bf16[2,128,1024]{2,1,0:T(8,128)(2,1)S(1)}, bf16[2,128,1024]{2,1,0:T(8,128)(2,1)S(1)}, f32[2,8,256]{2,1,0:T(8,128)S(1)}) custom-call(s32[3]{0:T(128)S(1)} %pad_add_fusion.info_ref, bf16[272,1024]{1,0:T(8,128)(2,1)S(1)} %pad_maximum_fusion.3.u_ref, bf16[272,1024]{1,0:T(8,128)(2,1)S(1)} %collective-permute-done.1.v_ref, ...), custom_call_target="tpu_custom_call" | custom-call | flops 4026531840 | bytes 12582912 | tf_op jit(solution)/shard_map/pallas_call | solution.py:181
  39.0 1.5 collective-permute-start.13
  40.6 1.5 collective-permute-start.14
  42.1 1.6 %collective-permute-start.11 = (bf16[272,1024]{1,0:T(8,128)(2,1)S(1)}, bf16[272,1024]{1,0:T(8,128)(2,1)}, u32[]{:S(2)}, u32[]{:S(2)}) collective-permute-start(bf16[272,1024]{1,0:T(8,128)(2,1)S(1)} %collective-permute-done.9.u_ref), channel_id=1, source_target_pairs={{0,2},{1,3},{2,4},{3,5},{4,6},{5,7},{6,0},{7,1},{8,10},{9,11},{10,... | collective-permute-start | bytes 1671176 | tf_op jit(solution)/shard_map/ppermute | solution.py:220
  44.0 9.4 %collective-permute-done.7 = bf16[2,128,1024]{2,1,0:T(8,128)(2,1)S(1)} collective-permute-done((bf16[2,128,1024]{2,1,0:T(8,128)(2,1)S(1)}, bf16[2,128,1024]{2,1,0:T(8,128)(2,1)S(1)}, u32[]{:S(2)}, u32[]{:S(2)}) %collective-permute-start.7) | collective-permute-done | bytes 524320 | tf_op jit(solution)/shard_map/ppermute | solution.py:216
  53.5 1.6 %collective-permute-start.8 = (bf16[128,1024]{1,0:T(8,128)(2,1)S(1)}, bf16[128,1024]{1,0:T(8,128)(2,1)S(1)}, u32[]{:S(2)}, u32[]{:S(2)}) collective-permute-start(bf16[128,1024]{1,0:T(8,128)(2,1)S(1)} %fusion.3), channel_id=1, source_target_pairs={{0,8},{8,0},{1,9},{9,1},{2,10},{10,2},{3,11},{11,3},{4,12},{12,4},... | collective-permute-start | bytes 786440 | tf_op jit(solution)/shard_map/ppermute | solution.py:210
  55.3 6.5 %collective-permute-done.13.v_ref = bf16[272,1024]{1,0:T(8,128)(2,1)S(1)} collective-permute-done((bf16[272,1024]{1,0:T(8,128)(2,1)S(1)}, bf16[272,1024]{1,0:T(8,128)(2,1)S(1)}, u32[]{:S(2)}, u32[]{:S(2)}) %collective-permute-start.13) | collective-permute-done | bytes 557088 | tf_op jit(solution)/shard_map/ppermute | solution.py:216
  61.8 5.5 %shard_map.96 = (bf16[2,128,1024]{2,1,0:T(8,128)(2,1)}, bf16[2,128,1024]{2,1,0:T(8,128)(2,1)S(1)}, f32[2,8,256]{2,1,0:T(8,128)S(1)}) custom-call(s32[3]{0:T(128)S(1)} %pad_add_fusion.info_ref, bf16[272,1024]{1,0:T(8,128)(2,1)S(1)} %collective-permute-done.9.u_ref, bf16[272,1024]{1,0:T(8,128)(2,1)S(1)} %collective-permute-done.13.v_ref, ...), custom_call_target="tpu_custom_call" | custom-call | flops 4026531840 | bytes 12582912 | tf_op jit(solution)/shard_map/pallas_call | solution.py:181
  68.1 1.5 collective-permute-start.19
  70.9 1.6 %collective-permute-start.15 = (bf16[272,1024]{1,0:T(8,128)(2,1)}, bf16[272,1024]{1,0:T(8,128)(2,1)S(1)}, u32[]{:S(2)}, u32[]{:S(2)}) collective-permute-start(bf16[272,1024]{1,0:T(8,128)(2,1)} %collective-permute-done.11.u_ref), channel_id=1, source_target_pairs={{0,2},{1,3},{2,4},{3,5},{4,6},{5,7},{6,0},{7,1},{8,10},{9,11},{10,... | collective-permute-start | bytes 1671176 | tf_op jit(solution)/shard_map/ppermute | solution.py:220
  72.4 1.2 collective-permute-start.16
  73.7 9.6 %collective-permute-done.19 = bf16[2,128,1024]{2,1,0:T(8,128)(2,1)} collective-permute-done((bf16[2,128,1024]{2,1,0:T(8,128)(2,1)}, bf16[2,128,1024]{2,1,0:T(8,128)(2,1)}, u32[]{:S(2)}, u32[]{:S(2)}) %collective-permute-start.19) | collective-permute-done | bytes 524320 | tf_op jit(solution)/shard_map/ppermute | solution.py:210
  83.3 1.2 fusion.5
  85.0 5.1 %collective-permute-done.18.n_ref = bf16[2,128,1024]{2,1,0:T(8,128)(2,1)} collective-permute-done((bf16[2,128,1024]{2,1,0:T(8,128)(2,1)}, bf16[2,128,1024]{2,1,0:T(8,128)(2,1)}, u32[]{:S(2)}, u32[]{:S(2)}) %collective-permute-start.18) | collective-permute-done | bytes 524320 | tf_op jit(solution)/shard_map/ppermute | solution.py:210
  90.1 1.9 %copy-done.1 = bf16[768,2048]{1,0:T(8,128)(2,1)S(1)} copy-done((bf16[768,2048]{1,0:T(8,128)(2,1)S(1)}, bf16[768,2048]{1,0:T(8,128)(2,1)}, u32[]{:S(2)}) %copy-start.1) | copy-done | bytes 3145752
  92.0 1.9 %copy-done.3 = bf16[768,2048]{1,0:T(8,128)(2,1)S(1)} copy-done((bf16[768,2048]{1,0:T(8,128)(2,1)S(1)}, bf16[768,2048]{1,0:T(8,128)(2,1)}, u32[]{:S(2)}) %copy-start.3) | copy-done | bytes 3145752
  93.9 6.1 %shard_map.97 = (bf16[2,64,1024]{2,1,0:T(8,128)(2,1)S(1)}, bf16[2,64,1024]{2,1,0:T(8,128)(2,1)S(1)}, bf16[2,64,1024]{2,1,0:T(8,128)(2,1)S(1)}, bf16[2,64,1024]{2,1,0:T(8,128)(2,1)S(1)}, f32[2,8,256]{2,1,0:T(8,128)S(1)}) custom-call(s32[3]{0:T(128)S(1)} %pad_add_fusion.info_ref, bf16[272,1024]{1,0:T(8,128)(2,1)} %collective-permute-done.11.u_ref, ...), custom_call_target="tpu_custom_call" | custom-call | flops 4026531840 | bytes 12582912 | tf_op jit(solution)/shard_map/pallas_call | solution.py:181
  100.7 1.5 collective-permute-start.25
  102.2 1.1 fusion
  103.2 1.6 %collective-permute-start.29 = (bf16[128,1024]{1,0:T(8,128)(2,1)S(1)}, bf16[128,1024]{1,0:T(8,128)(2,1)S(1)}, u32[]{:S(2)}, u32[]{:S(2)}) collective-permute-start(bf16[128,1024]{1,0:T(8,128)(2,1)S(1)} %fusion), channel_id=1, source_target_pairs={{0,2},{1,3},{2,4},{3,5},{4,6},{5,7},{6,0},{7,1},{8,10},{9,11},{10,... | collective-permute-start | bytes 786440 | tf_op jit(solution)/shard_map/ppermute | solution.py:220
  104.9 1.5 collective-permute-start.21
  106.9 2.4 %collective-permute-done.27 = bf16[2,64,1024]{2,1,0:T(8,128)(2,1)S(1)} collective-permute-done((bf16[2,64,1024]{2,1,0:T(8,128)(2,1)S(1)}, bf16[2,64,1024]{2,1,0:T(8,128)(2,1)S(1)}, u32[]{:S(2)}, u32[]{:S(2)}) %collective-permute-start.27) | collective-permute-done | bytes 262176 | tf_op jit(solution)/shard_map/ppermute | solution.py:216
  109.4 1.6 %collective-permute-start.28 = (bf16[64,1024]{1,0:T(8,128)(2,1)S(1)}, bf16[64,1024]{1,0:T(8,128)(2,1)S(1)}, u32[]{:S(2)}, u32[]{:S(2)}) collective-permute-start(bf16[64,1024]{1,0:T(8,128)(2,1)S(1)} %fusion.16), channel_id=1, source_target_pairs={{0,8},{8,0},{1,9},{9,1},{2,10},{10,2},{3,11},{11,3},{4,12},{12,4},... | collective-permute-start | bytes 393224 | tf_op jit(solution)/shard_map/ppermute | solution.py:210
  111.6 8.9 %collective-permute-done.28 = bf16[64,1024]{1,0:T(8,128)(2,1)S(1)} collective-permute-done((bf16[64,1024]{1,0:T(8,128)(2,1)S(1)}, bf16[64,1024]{1,0:T(8,128)(2,1)S(1)}, u32[]{:S(2)}, u32[]{:S(2)}) %collective-permute-start.28) | collective-permute-done | bytes 131104 | tf_op jit(solution)/shard_map/ppermute | solution.py:210
  120.6 5.2 %shard_map.98 = (bf16[2,64,1024]{2,1,0:T(8,128)(2,1)S(1)}, bf16[2,64,1024]{2,1,0:T(8,128)(2,1)S(1)}, bf16[2,64,1024]{2,1,0:T(8,128)(2,1)S(1)}, bf16[2,64,1024]{2,1,0:T(8,128)(2,1)S(1)}, f32[2,8,256]{2,1,0:T(8,128)S(1)}) custom-call(s32[3]{0:T(128)S(1)} %pad_add_fusion.info_ref, bf16[272,1024]{1,0:T(8,128)(2,1)S(1)} %collective-permute-done.15.u_ref, ...), custom_call_target="tpu_custom_call" | custom-call | flops 4026531840 | bytes 12582912 | tf_op jit(solution)/shard_map/pallas_call | solution.py:181
  127.4 1.2 collective-permute-start.30
  128.6 3.7 %collective-permute-done.23 = bf16[2,64,1024]{2,1,0:T(8,128)(2,1)S(1)} collective-permute-done((bf16[2,64,1024]{2,1,0:T(8,128)(2,1)S(1)}, bf16[2,64,1024]{2,1,0:T(8,128)(2,1)S(1)}, u32[]{:S(2)}, u32[]{:S(2)}) %collective-permute-start.23) | collective-permute-done | bytes 262176 | tf_op jit(solution)/shard_map/ppermute | solution.py:210
  132.8 1.5 collective-permute-start.34
  134.3 2.1 %collective-permute-done.34 = f32[4,2,2,128]{3,1,0,2:T(2,128)S(1)} collective-permute-done((f32[4,2,2,128]{3,1,0,2:T(2,128)S(1)}, f32[4,2,2,128]{3,1,0,2:T(2,128)S(1)}, u32[]{:S(2)}, u32[]{:S(2)}) %collective-permute-start.34) | collective-permute-done | bytes 8224 | tf_op jit(solution)/shard_map/ppermute | solution.py:210
  137.4 1.5 collective-permute-start.32
  139.0 1.1 collective-permute-start.31
  140.1 1.2 collective-permute-start.38
  141.3 1.7 %collective-permute-start.37 = (f32[2,2,128]{2,1,0:T(2,128)S(1)}, f32[2,2,128]{2,1,0:T(2,128)S(1)}, u32[]{:S(2)}, u32[]{:S(2)}) collective-permute-start(f32[2,2,128]{2,1,0:T(2,128)S(1)} %get-tuple-element.61), channel_id=1, source_target_pairs={{0,4},{1,5},{2,6},{3,7},{4,0},{5,1},{6,2},{7,3},{8,12},{9,13},{10,... | collective-permute-start | bytes 6152 | tf_op jit(solution)/shard_map/ppermute | solution.py:220
  143.0 1.4 collective-permute-start.36
  144.4 1.2 collective-permute-done.38
  147.4 6.8 %collective-permute-done.33 = bf16[128,1024]{1,0:T(8,128)(2,1)S(1)} collective-permute-done((bf16[128,1024]{1,0:T(8,128)(2,1)S(1)}, bf16[128,1024]{1,0:T(8,128)(2,1)S(1)}, u32[]{:S(2)}, u32[]{:S(2)}) %collective-permute-start.33) | collective-permute-done | bytes 262176 | tf_op jit(solution)/shard_map/ppermute | solution.py:220
  (97 shorter events, 15.8 us)
Async XLA Ops:
  0.6 15.7 %collective-permute-start.4 = (bf16[384,2048]{1,0:T(8,128)(2,1)}, bf16[384,2048]{1,0:T(8,128)(2,1)S(1)}, u32[]{:S(2)}, u32[]{:S(2)}) collective-permute-start(bf16[384,2048]{1,0:T(8,128)(2,1)} %bitcast.121), channel_id=1, source_target_pairs={{0,16},{16,0},{1,17},{17,1},{2,18},{18,2},{3,19},{19,3},{4,20},{20... | collective-permute-start | bytes 4718600 | tf_op jit(solution)/shard_map/ppermute | solution.py:213
  1.1 19.9 %collective-permute-start.5 = (bf16[384,2048]{1,0:T(8,128)(2,1)}, bf16[384,2048]{1,0:T(8,128)(2,1)}, u32[]{:S(2)}, u32[]{:S(2)}) collective-permute-start(bf16[384,2048]{1,0:T(8,128)(2,1)} %bitcast.123), channel_id=1, source_target_pairs={{0,16},{16,0},{1,17},{17,1},{2,18},{18,2},{3,19},{19,3},{4,20},{20... | collective-permute-start | bytes 4718600 | tf_op jit(solution)/shard_map/ppermute | solution.py:213
  2.3 9.5 %collective-permute-start = (bf16[128,1024]{1,0:T(8,128)(2,1)S(1)}, bf16[128,1024]{1,0:T(8,128)(2,1)S(1)}, u32[]{:S(2)}, u32[]{:S(2)}) collective-permute-start(bf16[128,1024]{1,0:T(8,128)(2,1)S(1)} %multiply_convert_fusion), channel_id=1, source_target_pairs={{0,8},{8,0},{1,9},{9,1},{2,10},{10,2},{3,11},{11,3},{4,12},{12,4},... | collective-permute-start | bytes 786440 | tf_op jit(solution)/shard_map/ppermute | solution.py:210
  5.3 8.5 %collective-permute-start.2 = (bf16[128,1024]{1,0:T(8,128)(2,1)}, bf16[128,1024]{1,0:T(8,128)(2,1)S(1)}, u32[]{:S(2)}, u32[]{:S(2)}) collective-permute-start(bf16[128,1024]{1,0:T(8,128)(2,1)} %param.10), channel_id=1, source_target_pairs={{0,1},{1,0},{2,3},{3,2},{4,5},{5,4},{6,7},{7,6},{8,9},{9,8},{10,11... | collective-permute-start | bytes 786440 | tf_op jit(solution)/shard_map/ppermute | solution.py:216
  6.8 17.9 %collective-permute-start.6 = (bf16[384,2048]{1,0:T(8,128)(2,1)}, bf16[384,2048]{1,0:T(8,128)(2,1)}, u32[]{:S(2)}, u32[]{:S(2)}) collective-permute-start(bf16[384,2048]{1,0:T(8,128)(2,1)} %bitcast.125), channel_id=1, source_target_pairs={{0,16},{16,0},{1,17},{17,1},{2,18},{18,2},{3,19},{19,3},{4,20},{20... | collective-permute-start | bytes 4718600 | tf_op jit(solution)/shard_map/ppermute | solution.py:213
  8.3 10.7 %copy-start.6 = (bf16[1,384,2048]{2,1,0:T(8,128)(2,1)S(1)}, bf16[1,384,2048]{2,1,0:T(8,128)(2,1)}, u32[]{:S(2)}) copy-start(bf16[1,384,2048]{2,1,0:T(8,128)(2,1)} %param.13) | copy-start | bytes 4718596
  11.9 27.2 %collective-permute-start.9 = (bf16[272,1024]{1,0:T(8,128)(2,1)S(1)}, bf16[272,1024]{1,0:T(8,128)(2,1)S(1)}, u32[]{:S(2)}, u32[]{:S(2)}) collective-permute-start(bf16[272,1024]{1,0:T(8,128)(2,1)S(1)} %pad_maximum_fusion.3.u_ref), channel_id=1, source_target_pairs={{0,2},{1,3},{2,4},{3,5},{4,6},{5,7},{6,0},{7,1},{8,10},{9,11},{10,... | collective-permute-start | bytes 1671176 | tf_op jit(solution)/shard_map/ppermute | solution.py:220
  13.8 19.6 %collective-permute-start.1 = (bf16[272,1024]{1,0:T(8,128)(2,1)S(1)}, bf16[272,1024]{1,0:T(8,128)(2,1)S(1)}, u32[]{:S(2)}, u32[]{:S(2)}) collective-permute-start(bf16[272,1024]{1,0:T(8,128)(2,1)S(1)} %pad_maximum_fusion.3.u_ref), channel_id=1, source_target_pairs={{0,1},{1,0},{2,3},{3,2},{4,5},{5,4},{6,7},{7,6},{8,9},{9,8},{10,11... | collective-permute-start | bytes 1671176 | tf_op jit(solution)/shard_map/ppermute | solution.py:216
  16.3 6.3 %copy-start.7 = (bf16[1,384,2048]{2,1,0:T(8,128)(2,1)S(1)}, bf16[1,384,2048]{2,1,0:T(8,128)(2,1)}, u32[]{:S(2)}) copy-start(bf16[1,384,2048]{2,1,0:T(8,128)(2,1)} %param.14) | copy-start | bytes 4718596
  17.4 21.6 %collective-permute-start.10 = (bf16[2,128,1024]{2,1,0:T(8,128)(2,1)S(1)}, bf16[2,128,1024]{2,1,0:T(8,128)(2,1)S(1)}, u32[]{:S(2)}, u32[]{:S(2)}) collective-permute-start(bf16[2,128,1024]{2,1,0:T(8,128)(2,1)S(1)} %pad_maximum_fusion.4.m_ref), channel_id=1, source_target_pairs={{0,2},{1,3},{2,4},{3,5},{4,6},{5,7},{6,0},{7,1},{8,10},{9,11},{10,... | collective-permute-start | bytes 1572872 | tf_op jit(solution)/shard_map/ppermute | solution.py:220
  21.0 3.7 %copy-start.8 = (bf16[1,384,2048]{2,1,0:T(8,128)(2,1)S(1)}, bf16[1,384,2048]{2,1,0:T(8,128)(2,1)}, u32[]{:S(2)}) copy-start(bf16[1,384,2048]{2,1,0:T(8,128)(2,1)} %param.15) | copy-start | bytes 4718596
  21.0 12.3 %collective-permute-start.3 = (bf16[2,128,1024]{2,1,0:T(8,128)(2,1)S(1)}, bf16[2,128,1024]{2,1,0:T(8,128)(2,1)S(1)}, u32[]{:S(2)}, u32[]{:S(2)}) collective-permute-start(bf16[2,128,1024]{2,1,0:T(8,128)(2,1)S(1)} %pad_maximum_fusion.4.m_ref), channel_id=1, source_target_pairs={{0,8},{8,0},{1,9},{9,1},{2,10},{10,2},{3,11},{11,3},{4,12},{12,4},... | collective-permute-start | bytes 1572872 | tf_op jit(solution)/shard_map/ppermute | solution.py:210
  24.7 37.1 %copy-start = (bf16[768,2048]{1,0:T(8,128)(2,1)}, bf16[768,2048]{1,0:T(8,128)(2,1)S(1)}, u32[]{:S(2)}) copy-start(bf16[768,2048]{1,0:T(8,128)(2,1)S(1)} %pad_maximum_fusion.1.wu_ref) | copy-start | bytes 9437188
  27.9 33.9 %copy-start.2 = (bf16[768,2048]{1,0:T(8,128)(2,1)}, bf16[768,2048]{1,0:T(8,128)(2,1)S(1)}, u32[]{:S(2)}) copy-start(bf16[768,2048]{1,0:T(8,128)(2,1)S(1)} %pad_maximum_fusion.2.wd_ref) | copy-start | bytes 9437188
  38.5 14.9 %collective-permute-start.7 = (bf16[2,128,1024]{2,1,0:T(8,128)(2,1)S(1)}, bf16[2,128,1024]{2,1,0:T(8,128)(2,1)S(1)}, u32[]{:S(2)}, u32[]{:S(2)}) collective-permute-start(bf16[2,128,1024]{2,1,0:T(8,128)(2,1)S(1)} %get-tuple-element.31), channel_id=1, source_target_pairs={{0,1},{1,0},{2,3},{3,2},{4,5},{5,4},{6,7},{7,6},{8,9},{9,8},{10,11... | collective-permute-start | bytes 1572872 | tf_op jit(solution)/shard_map/ppermute | solution.py:216
  39.0 22.7 %collective-permute-start.13 = (bf16[272,1024]{1,0:T(8,128)(2,1)S(1)}, bf16[272,1024]{1,0:T(8,128)(2,1)S(1)}, u32[]{:S(2)}, u32[]{:S(2)}) collective-permute-start(bf16[272,1024]{1,0:T(8,128)(2,1)S(1)} %collective-permute-done.9.u_ref), channel_id=1, source_target_pairs={{0,1},{1,0},{2,3},{3,2},{4,5},{5,4},{6,7},{7,6},{8,9},{9,8},{10,11... | collective-permute-start | bytes 1671176 | tf_op jit(solution)/shard_map/ppermute | solution.py:216
  40.6 14.7 %collective-permute-start.14 = (bf16[2,128,1024]{2,1,0:T(8,128)(2,1)S(1)}, bf16[2,128,1024]{2,1,0:T(8,128)(2,1)S(1)}, u32[]{:S(2)}, u32[]{:S(2)}) collective-permute-start(bf16[2,128,1024]{2,1,0:T(8,128)(2,1)S(1)} %collective-permute-done.10.m_ref), channel_id=1, source_target_pairs={{0,8},{8,0},{1,9},{9,1},{2,10},{10,2},{3,11},{11,3},{4,12},{12,4},... | collective-permute-start | bytes 1572872 | tf_op jit(solution)/shard_map/ppermute | solution.py:210
  42.1 27.7 %collective-permute-start.11 = (bf16[272,1024]{1,0:T(8,128)(2,1)S(1)}, bf16[272,1024]{1,0:T(8,128)(2,1)}, u32[]{:S(2)}, u32[]{:S(2)}) collective-permute-start(bf16[272,1024]{1,0:T(8,128)(2,1)S(1)} %collective-permute-done.9.u_ref), channel_id=1, source_target_pairs={{0,2},{1,3},{2,4},{3,5},{4,6},{5,7},{6,0},{7,1},{8,10},{9,11},{10,... | collective-permute-start | bytes 1671176 | tf_op jit(solution)/shard_map/ppermute | solution.py:220
  43.6 26.1 %collective-permute-start.12 = (bf16[2,128,1024]{2,1,0:T(8,128)(2,1)S(1)}, bf16[2,128,1024]{2,1,0:T(8,128)(2,1)}, u32[]{:S(2)}, u32[]{:S(2)}) collective-permute-start(bf16[2,128,1024]{2,1,0:T(8,128)(2,1)S(1)} %collective-permute-done.10.m_ref), channel_id=1, source_target_pairs={{0,2},{1,3},{2,4},{3,5},{4,6},{5,7},{6,0},{7,1},{8,10},{9,11},{10,... | collective-permute-start | bytes 1572872 | tf_op jit(solution)/shard_map/ppermute | solution.py:220
  53.5 16.1 %collective-permute-start.8 = (bf16[128,1024]{1,0:T(8,128)(2,1)S(1)}, bf16[128,1024]{1,0:T(8,128)(2,1)S(1)}, u32[]{:S(2)}, u32[]{:S(2)}) collective-permute-start(bf16[128,1024]{1,0:T(8,128)(2,1)S(1)} %fusion.3), channel_id=1, source_target_pairs={{0,8},{8,0},{1,9},{9,1},{2,10},{10,2},{3,11},{11,3},{4,12},{12,4},... | collective-permute-start | bytes 786440 | tf_op jit(solution)/shard_map/ppermute | solution.py:210
  68.1 15.2 %collective-permute-start.19 = (bf16[2,128,1024]{2,1,0:T(8,128)(2,1)}, bf16[2,128,1024]{2,1,0:T(8,128)(2,1)}, u32[]{:S(2)}, u32[]{:S(2)}) collective-permute-start(bf16[2,128,1024]{2,1,0:T(8,128)(2,1)} %get-tuple-element.34), channel_id=1, source_target_pairs={{0,8},{8,0},{1,9},{9,1},{2,10},{10,2},{3,11},{11,3},{4,12},{12,4},... | collective-permute-start | bytes 1572872 | tf_op jit(solution)/shard_map/ppermute | solution.py:210
  69.7 20.4 %collective-permute-start.17 = (bf16[272,1024]{1,0:T(8,128)(2,1)}, bf16[272,1024]{1,0:T(8,128)(2,1)}, u32[]{:S(2)}, u32[]{:S(2)}) collective-permute-start(bf16[272,1024]{1,0:T(8,128)(2,1)} %collective-permute-done.11.u_ref), channel_id=1, source_target_pairs={{0,1},{1,0},{2,3},{3,2},{4,5},{5,4},{6,7},{7,6},{8,9},{9,8},{10,11... | collective-permute-start | bytes 1671176 | tf_op jit(solution)/shard_map/ppermute | solution.py:216
  70.3 19.8 %collective-permute-start.18 = (bf16[2,128,1024]{2,1,0:T(8,128)(2,1)}, bf16[2,128,1024]{2,1,0:T(8,128)(2,1)}, u32[]{:S(2)}, u32[]{:S(2)}) collective-permute-start(bf16[2,128,1024]{2,1,0:T(8,128)(2,1)} %collective-permute-done.12.m_ref), channel_id=1, source_target_pairs={{0,8},{8,0},{1,9},{9,1},{2,10},{10,2},{3,11},{11,3},{4,12},{12,4},... | collective-permute-start | bytes 1572872 | tf_op jit(solution)/shard_map/ppermute | solution.py:210
  70.9 34.0 %collective-permute-start.15 = (bf16[272,1024]{1,0:T(8,128)(2,1)}, bf16[272,1024]{1,0:T(8,128)(2,1)S(1)}, u32[]{:S(2)}, u32[]{:S(2)}) collective-permute-start(bf16[272,1024]{1,0:T(8,128)(2,1)} %collective-permute-done.11.u_ref), channel_id=1, source_target_pairs={{0,2},{1,3},{2,4},{3,5},{4,6},{5,7},{6,0},{7,1},{8,10},{9,11},{10,... | collective-permute-start | bytes 1671176 | tf_op jit(solution)/shard_map/ppermute | solution.py:220
  72.4 32.4 %collective-permute-start.16 = (bf16[2,128,1024]{2,1,0:T(8,128)(2,1)}, bf16[2,128,1024]{2,1,0:T(8,128)(2,1)S(1)}, u32[]{:S(2)}, u32[]{:S(2)}) collective-permute-start(bf16[2,128,1024]{2,1,0:T(8,128)(2,1)} %collective-permute-done.12.m_ref), channel_id=1, source_target_pairs={{0,2},{1,3},{2,4},{3,5},{4,6},{5,7},{6,0},{7,1},{8,10},{9,11},{10,... | collective-permute-start | bytes 1572872 | tf_op jit(solution)/shard_map/ppermute | solution.py:220
  83.3 18.9 %copy-start.5 = (bf16[2,128,1024]{2,1,0:T(8,128)(2,1)S(1)}, bf16[2,128,1024]{2,1,0:T(8,128)(2,1)}, u32[]{:S(2)}) copy-start(bf16[2,128,1024]{2,1,0:T(8,128)(2,1)} %copy-done.4) | copy-start | bytes 1572868
  84.4 17.7 %collective-permute-start.20 = (bf16[128,1024]{1,0:T(8,128)(2,1)S(1)}, bf16[128,1024]{1,0:T(8,128)(2,1)S(1)}, u32[]{:S(2)}, u32[]{:S(2)}) collective-permute-start(bf16[128,1024]{1,0:T(8,128)(2,1)S(1)} %fusion.5), channel_id=1, source_target_pairs={{0,1},{1,0},{2,3},{3,2},{4,5},{5,4},{6,7},{7,6},{8,9},{9,8},{10,11... | collective-permute-start | bytes 786440 | tf_op jit(solution)/shard_map/ppermute | solution.py:216
  90.1 1.9 %copy-start.1 = (bf16[768,2048]{1,0:T(8,128)(2,1)S(1)}, bf16[768,2048]{1,0:T(8,128)(2,1)}, u32[]{:S(2)}) copy-start(bf16[768,2048]{1,0:T(8,128)(2,1)} %copy-done) | copy-start | bytes 9437188
  92.0 1.9 %copy-start.3 = (bf16[768,2048]{1,0:T(8,128)(2,1)S(1)}, bf16[768,2048]{1,0:T(8,128)(2,1)}, u32[]{:S(2)}) copy-start(bf16[768,2048]{1,0:T(8,128)(2,1)} %copy-done.2) | copy-start | bytes 9437188
  100.1 9.3 %collective-permute-start.27 = (bf16[2,64,1024]{2,1,0:T(8,128)(2,1)S(1)}, bf16[2,64,1024]{2,1,0:T(8,128)(2,1)S(1)}, u32[]{:S(2)}, u32[]{:S(2)}) collective-permute-start(bf16[2,64,1024]{2,1,0:T(8,128)(2,1)S(1)} %get-tuple-element.40), channel_id=1, source_target_pairs={{0,1},{1,0},{2,3},{3,2},{4,5},{5,4},{6,7},{7,6},{8,9},{9,8},{10,11... | collective-permute-start | bytes 786440 | tf_op jit(solution)/shard_map/ppermute | solution.py:216
  100.7 10.3 %collective-permute-start.25 = (bf16[2,64,1024]{2,1,0:T(8,128)(2,1)S(1)}, bf16[2,64,1024]{2,1,0:T(8,128)(2,1)S(1)}, u32[]{:S(2)}, u32[]{:S(2)}) collective-permute-start(bf16[2,64,1024]{2,1,0:T(8,128)(2,1)S(1)} %get-tuple-element.38), channel_id=1, source_target_pairs={{0,8},{8,0},{1,9},{9,1},{2,10},{10,2},{3,11},{11,3},{4,12},{12,4},... | collective-permute-start | bytes 786440 | tf_op jit(solution)/shard_map/ppermute | solution.py:210
  103.2 24.1 %collective-permute-start.29 = (bf16[128,1024]{1,0:T(8,128)(2,1)S(1)}, bf16[128,1024]{1,0:T(8,128)(2,1)S(1)}, u32[]{:S(2)}, u32[]{:S(2)}) collective-permute-start(bf16[128,1024]{1,0:T(8,128)(2,1)S(1)} %fusion), channel_id=1, source_target_pairs={{0,2},{1,3},{2,4},{3,5},{4,6},{5,7},{6,0},{7,1},{8,10},{9,11},{10,... | collective-permute-start | bytes 786440 | tf_op jit(solution)/shard_map/ppermute | solution.py:220
  104.9 15.7 %collective-permute-start.21 = (bf16[272,1024]{1,0:T(8,128)(2,1)S(1)}, bf16[272,1024]{1,0:T(8,128)(2,1)S(1)}, u32[]{:S(2)}, u32[]{:S(2)}) collective-permute-start(bf16[272,1024]{1,0:T(8,128)(2,1)S(1)} %collective-permute-done.15.u_ref), channel_id=1, source_target_pairs={{0,1},{1,0},{2,3},{3,2},{4,5},{5,4},{6,7},{7,6},{8,9},{9,8},{10,11... | collective-permute-start | bytes 1671176 | tf_op jit(solution)/shard_map/ppermute | solution.py:216
  106.4 14.2 %collective-permute-start.22 = (bf16[2,128,1024]{2,1,0:T(8,128)(2,1)S(1)}, bf16[2,128,1024]{2,1,0:T(8,128)(2,1)S(1)}, u32[]{:S(2)}, u32[]{:S(2)}) collective-permute-start(bf16[2,128,1024]{2,1,0:T(8,128)(2,1)S(1)} %collective-permute-done.16.m_ref), channel_id=1, source_target_pairs={{0,8},{8,0},{1,9},{9,1},{2,10},{10,2},{3,11},{11,3},{4,12},{12,4},... | collective-permute-start | bytes 1572872 | tf_op jit(solution)/shard_map/ppermute | solution.py:210
  109.4 11.0 %collective-permute-start.28 = (bf16[64,1024]{1,0:T(8,128)(2,1)S(1)}, bf16[64,1024]{1,0:T(8,128)(2,1)S(1)}, u32[]{:S(2)}, u32[]{:S(2)}) collective-permute-start(bf16[64,1024]{1,0:T(8,128)(2,1)S(1)} %fusion.16), channel_id=1, source_target_pairs={{0,8},{8,0},{1,9},{9,1},{2,10},{10,2},{3,11},{11,3},{4,12},{12,4},... | collective-permute-start | bytes 393224 | tf_op jit(solution)/shard_map/ppermute | solution.py:210
  111.0 9.5 %collective-permute-start.26 = (bf16[64,1024]{1,0:T(8,128)(2,1)S(1)}, bf16[64,1024]{1,0:T(8,128)(2,1)S(1)}, u32[]{:S(2)}, u32[]{:S(2)}) collective-permute-start(bf16[64,1024]{1,0:T(8,128)(2,1)S(1)} %fusion.14), channel_id=1, source_target_pairs={{0,1},{1,0},{2,3},{3,2},{4,5},{5,4},{6,7},{7,6},{8,9},{9,8},{10,11... | collective-permute-start | bytes 393224 | tf_op jit(solution)/shard_map/ppermute | solution.py:216
  125.8 21.0 %copy-start.10 = (s32[128,8]{0,1:T(8,128)S(1)}, s32[128,8]{0,1:T(8,128)}, u32[]{:S(2)}) copy-start(s32[128,8]{0,1:T(8,128)} %param.11) | copy-start | bytes 12292
  125.8 6.5 %collective-permute-start.23 = (bf16[2,64,1024]{2,1,0:T(8,128)(2,1)S(1)}, bf16[2,64,1024]{2,1,0:T(8,128)(2,1)S(1)}, u32[]{:S(2)}, u32[]{:S(2)}) collective-permute-start(bf16[2,64,1024]{2,1,0:T(8,128)(2,1)S(1)} %get-tuple-element.45), channel_id=1, source_target_pairs={{0,8},{8,0},{1,9},{9,1},{2,10},{10,2},{3,11},{11,3},{4,12},{12,4},... | collective-permute-start | bytes 786440 | tf_op jit(solution)/shard_map/ppermute | solution.py:210
  126.4 6.4 %collective-permute-start.24 = (bf16[2,64,1024]{2,1,0:T(8,128)(2,1)S(1)}, bf16[2,64,1024]{2,1,0:T(8,128)(2,1)S(1)}, u32[]{:S(2)}, u32[]{:S(2)}) collective-permute-start(bf16[2,64,1024]{2,1,0:T(8,128)(2,1)S(1)} %get-tuple-element.47), channel_id=1, source_target_pairs={{0,1},{1,0},{2,3},{3,2},{4,5},{5,4},{6,7},{7,6},{8,9},{9,8},{10,11... | collective-permute-start | bytes 786440 | tf_op jit(solution)/shard_map/ppermute | solution.py:216
  127.4 10.1 %collective-permute-start.30 = (bf16[128,1024]{1,0:T(8,128)(2,1)S(1)}, bf16[128,1024]{1,0:T(8,128)(2,1)S(1)}, u32[]{:S(2)}, u32[]{:S(2)}) collective-permute-start(bf16[128,1024]{1,0:T(8,128)(2,1)S(1)} %add_convert_fusion.2), channel_id=1, source_target_pairs={{0,2},{1,3},{2,4},{3,5},{4,6},{5,7},{6,0},{7,1},{8,10},{9,11},{10,... | collective-permute-start | bytes 786440 | tf_op jit(solution)/shard_map/ppermute | solution.py:220
  132.8 3.7 %collective-permute-start.34 = (f32[4,2,2,128]{3,1,0,2:T(2,128)S(1)}, f32[4,2,2,128]{3,1,0,2:T(2,128)S(1)}, u32[]{:S(2)}, u32[]{:S(2)}) collective-permute-start(f32[4,2,2,128]{3,1,0,2:T(2,128)S(1)} %pad_maximum_fusion.5), channel_id=1, source_target_pairs={{0,8},{8,0},{1,9},{9,1},{2,10},{10,2},{3,11},{11,3},{4,12},{12,4},... | collective-permute-start | bytes 24584 | tf_op jit(solution)/shard_map/ppermute | solution.py:210
  136.4 3.7 %collective-permute-start.35 = (f32[4,2,128]{2,1,0:T(2,128)S(1)}, f32[4,2,128]{2,1,0:T(2,128)S(1)}, u32[]{:S(2)}, u32[]{:S(2)}) collective-permute-start(f32[4,2,128]{2,1,0:T(2,128)S(1)} %get-tuple-element.63), channel_id=1, source_target_pairs={{0,1},{1,0},{2,3},{3,2},{4,5},{5,4},{6,7},{7,6},{8,9},{9,8},{10,11... | collective-permute-start | bytes 12296 | tf_op jit(solution)/shard_map/ppermute | solution.py:216
  137.4 8.4 %collective-permute-start.32 = (bf16[64,1024]{1,0:T(8,128)(2,1)S(1)}, bf16[64,1024]{1,0:T(8,128)(2,1)S(1)}, u32[]{:S(2)}, u32[]{:S(2)}) collective-permute-start(bf16[64,1024]{1,0:T(8,128)(2,1)S(1)} %fusion.12), channel_id=1, source_target_pairs={{0,8},{8,0},{1,9},{9,1},{2,10},{10,2},{3,11},{11,3},{4,12},{12,4},... | collective-permute-start | bytes 393224 | tf_op jit(solution)/shard_map/ppermute | solution.py:210
  139.0 6.9 %collective-permute-start.31 = (bf16[64,1024]{1,0:T(8,128)(2,1)S(1)}, bf16[64,1024]{1,0:T(8,128)(2,1)S(1)}, u32[]{:S(2)}, u32[]{:S(2)}) collective-permute-start(bf16[64,1024]{1,0:T(8,128)(2,1)S(1)} %fusion.11), channel_id=1, source_target_pairs={{0,1},{1,0},{2,3},{3,2},{4,5},{5,4},{6,7},{7,6},{8,9},{9,8},{10,11... | collective-permute-start | bytes 393224 | tf_op jit(solution)/shard_map/ppermute | solution.py:216
  140.1 5.4 %collective-permute-start.38 = (f32[2,2,128]{2,1,0:T(2,128)S(1)}, f32[2,2,128]{2,1,0:T(2,128)S(1)}, u32[]{:S(2)}, u32[]{:S(2)}) collective-permute-start(f32[2,2,128]{2,1,0:T(2,128)S(1)} %get-tuple-element.60), channel_id=1, source_target_pairs={{0,2},{1,3},{2,4},{3,5},{4,6},{5,7},{6,0},{7,1},{8,10},{9,11},{10,... | collective-permute-start | bytes 6152 | tf_op jit(solution)/shard_map/ppermute | solution.py:220
  141.3 4.5 %collective-permute-start.37 = (f32[2,2,128]{2,1,0:T(2,128)S(1)}, f32[2,2,128]{2,1,0:T(2,128)S(1)}, u32[]{:S(2)}, u32[]{:S(2)}) collective-permute-start(f32[2,2,128]{2,1,0:T(2,128)S(1)} %get-tuple-element.61), channel_id=1, source_target_pairs={{0,4},{1,5},{2,6},{3,7},{4,0},{5,1},{6,2},{7,3},{8,12},{9,13},{10,... | collective-permute-start | bytes 6152 | tf_op jit(solution)/shard_map/ppermute | solution.py:220
  143.0 3.8 %collective-permute-start.36 = (f32[2,2,128]{2,1,0:T(2,128)S(1)}, f32[2,2,128]{2,1,0:T(2,128)S(1)}, u32[]{:S(2)}, u32[]{:S(2)}) collective-permute-start(f32[2,2,128]{2,1,0:T(2,128)S(1)} %get-tuple-element.59), channel_id=1, source_target_pairs={{0,6},{1,7},{2,0},{3,1},{4,2},{5,3},{6,4},{7,5},{8,14},{9,15},{10,... | collective-permute-start | bytes 6152 | tf_op jit(solution)/shard_map/ppermute | solution.py:220
  146.0 8.2 %collective-permute-start.33 = (bf16[128,1024]{1,0:T(8,128)(2,1)S(1)}, bf16[128,1024]{1,0:T(8,128)(2,1)S(1)}, u32[]{:S(2)}, u32[]{:S(2)}) collective-permute-start(bf16[128,1024]{1,0:T(8,128)(2,1)S(1)} %add_convert_fusion.1), channel_id=1, source_target_pairs={{0,2},{1,3},{2,4},{3,5},{4,6},{5,7},{6,0},{7,1},{8,10},{9,11},{10,... | collective-permute-start | bytes 786440 | tf_op jit(solution)/shard_map/ppermute | solution.py:220
  (2 other events, 1.9 us)

commit v2 on v0

--- a/solution.py
+++ b/solution.py
@@ -1,6 +1,9 @@
+import functools
 import jax
 import jax.numpy as jnp
 from jax import lax
+from jax.experimental import pallas as pl
+from jax.experimental.pallas import tpu as pltpu
 from jax.sharding import PartitionSpec as P
 
 
@@ -40,7 +43,7 @@
     return (summed, gate_shaped)
 
 
-def body(checkpoint, scales, out_grad, expert_ids, gates, w_gate, w_up, w_down):
+def body_routed(checkpoint, scales, out_grad, expert_ids, gates, w_gate, w_up, w_down):
     expert_count = lax.axis_size("dp") * lax.axis_size("expert")
     token_rows = checkpoint.shape[0]
     pick_count = expert_ids.shape[1]
@@ -87,6 +90,312 @@
     )
     gate_out = lax.psum(gate_pairs.astype(jnp.bfloat16), "tensor").astype(jnp.float32)
     return (weighted.astype(jnp.bfloat16), gate_out)
+
+
+def expert_kernel(tops, info_ref, xs_ref, gs_ref, v_ref, n_ref, wg_ref, wu_ref, wd_ref, *outs):
+    a_send, a_keep, b_send, b_keep, term_ref = outs
+    f32 = jnp.float32
+    contract = (((1,), (1,)), ((), ()))
+    _, half, width = a_send.shape
+    token_rows = 2 * half
+    rows = 2 * token_rows
+    units = wg_ref.shape[0] // 2
+    mine = pl.ds(pl.multiple_of(info_ref[0] * width, width), width)
+    other = pl.ds(pl.multiple_of((1 - info_ref[0]) * width, width), width)
+
+    def project(first, second, w_ref):
+        low = lax.dot_general(first, w_ref[:, mine], contract, preferred_element_type=f32)
+        return low + lax.dot_general(second, w_ref[:, other], contract, preferred_element_type=f32)
+
+    def weight_of(pick_rows, expert):
+
+        def segment(kind, k):
+            at = (kind * tops + k) * token_rows
+            row, col = at // width, at % width
+            return pick_rows[row : row + 1, col : col + token_rows].astype(f32)
+
+        total = jnp.zeros((1, token_rows), f32)
+        for k in range(tops):
+            chosen = segment(0, k) == expert.astype(f32)
+            total = total + jnp.where(chosen, segment(1, k) + segment(2, k), 0.0)
+        return jnp.broadcast_to(total, (128, token_rows)).T[:, :1]
+
+    x_mine = jnp.concatenate([xs_ref[token_rows:rows], v_ref[token_rows:rows]], axis=0)
+    x_other = jnp.concatenate([xs_ref[:token_rows], v_ref[:token_rows]], axis=0)
+    picks = xs_ref[rows:], v_ref[rows:]
+    gate_pre = project(x_mine, x_other, wg_ref)
+    up_pre = project(x_mine, x_other, wu_ref)
+    back = project(gs_ref[...], n_ref[...], wd_ref)
+    sigma = jax.nn.sigmoid(gate_pre)
+    swish = gate_pre * sigma
+    hidden = (swish * up_pre).astype(jnp.bfloat16)
+    product = hidden.astype(f32) * back
+    weights = []
+    for which in range(2):
+        expert = info_ref[1 + which]
+        weights.append(jnp.concatenate([weight_of(part, expert) for part in picks], axis=0))
+        term = jnp.sum(product[:, which * units : (which + 1) * units], axis=1, keepdims=True)
+        term = term.astype(jnp.bfloat16).astype(f32)
+        term_ref[which] = jnp.broadcast_to(term, (rows, 128)).T[:8]
+    lane = lax.broadcasted_iota(jnp.int32, back.shape, 1)
+    scaled = back * jnp.where(lane < units, weights[0], weights[1])
+    d_gate = (scaled * up_pre * sigma * (1.0 + gate_pre * (1.0 - sigma))).astype(jnp.bfloat16)
+    d_up = (scaled * swish).astype(jnp.bfloat16)
+
+    def spread(cols):
+        piece = jnp.dot(d_gate, wg_ref[:, cols], preferred_element_type=f32)
+        piece = piece + jnp.dot(d_up, wu_ref[:, cols], preferred_element_type=f32)
+        return piece.astype(jnp.bfloat16)
+
+    far, near = spread(other), spread(mine)
+    a_send[0], a_send[1] = far[:half], far[token_rows : token_rows + half]
+    b_keep[1], b_send[1] = far[half:token_rows], far[token_rows + half :]
+    a_keep[0], a_keep[1] = near[:half], near[token_rows : token_rows + half]
+    b_keep[0], b_send[0] = near[half:token_rows], near[token_rows + half :]
+
+
+def run_expert(tops, token_rows, info, xs, gs, v, n, wg, wu, wd):
+    hidden, model_width = wg.shape
+    rows = 2 * token_rows
+    vmem = pl.BlockSpec(memory_space=pltpu.VMEM)
+    share = jax.ShapeDtypeStruct((2, token_rows // 2, xs.shape[1]), jnp.bfloat16)
+    return pl.pallas_call(
+        functools.partial(expert_kernel, tops),
+        in_specs=[pl.BlockSpec(memory_space=pltpu.SMEM)] + [vmem] * 7,
+        out_specs=[vmem] * 5,
+        out_shape=[share] * 4 + [jax.ShapeDtypeStruct((2, 8, rows), jnp.float32)],
+        compiler_params=pltpu.CompilerParams(vmem_limit_bytes=16 * 1024 * 1024),
+        cost_estimate=pl.CostEstimate(
+            flops=10 * rows * hidden * model_width,
+            bytes_accessed=6 * rows * model_width + 6 * hidden * model_width,
+            transcendentals=rows * hidden,
+        ),
+    )(info, xs, gs, v, n, wg, wu, wd)
+
+
+def prepare_kernel(*refs):
+    sources, (own, x), held, arrived = refs[:5], refs[5:7], refs[7:12], refs[12]
+    copies = [pltpu.make_async_copy(*pair, arrived.at[at]) for at, pair in enumerate(zip(sources, held))]
+    for copy in copies:
+        copy.start()
+    for copy in copies:
+        copy.wait()
+    checkpoint, scales, ids, gates, out_grad = held
+    f32 = jnp.float32
+    token_rows, width = x.shape
+    scale = jnp.broadcast_to(scales[...], (128, token_rows)).T[:, :1]
+    value = (checkpoint[...].astype(f32) * scale).astype(jnp.bfloat16)
+    x[...] = value
+    own[:token_rows] = value
+    high = gates[...].astype(jnp.bfloat16).astype(f32)
+    parts = [ids[...].astype(f32), high, gates[...] - high]
+    flat = [part[k : k + 1] for part in parts for k in range(part.shape[0])]
+    count = own.shape[0] - 2 * token_rows
+    flat += [jnp.zeros((1, token_rows), f32)] * (count * width // token_rows - len(flat))
+    per = width // token_rows
+    rows = [jnp.concatenate(flat[row * per : (row + 1) * per], axis=1) for row in range(count)]
+    own[token_rows : token_rows + count] = jnp.concatenate(rows, axis=0).astype(jnp.bfloat16)
+    own[token_rows + count :] = out_grad[...]
+
+
+def stack_kernel(first, second, both):
+    rows = first.shape[0]
+    both[:rows] = first[...]
+    both[rows:] = second[...]
+
+
+def merge_kernel(own, both, xs, gs):
+    token_rows = both.shape[0] // 2
+    split = own.shape[0] - token_rows
+    xs[:token_rows] = both[:token_rows]
+    xs[token_rows:] = own[:split]
+    gs[:token_rows] = own[split:]
+    gs[token_rows:] = both[token_rows:]
+
+
+def pick_kernel(owners, ids, *refs):
+    terms, out = refs[:-1], refs[-1]
+    total = jnp.zeros(out.shape, jnp.float32)
+    for way, ref in enumerate(terms):
+        steps, which_count, _ = ref.shape
+        for step in range(steps):
+            for which in range(which_count):
+                owner = owners[(step * len(terms) + way) * which_count + which]
+                total = total + jnp.where(ids[...] == owner, ref[step, which : which + 1], 0.0)
+    out[...] = total
+
+
+def join_kernel(own, both, um, xs, gs):
+    token_rows = both.shape[0] // 2
+    split = own.shape[0] - token_rows
+    count = xs.shape[0]
+    um[:token_rows] = xs[:token_rows] = both[:token_rows]
+    um[token_rows:count] = xs[token_rows:] = own[:split]
+    um[count : count + token_rows] = gs[:token_rows] = own[split:]
+    um[count + token_rows :] = gs[token_rows:] = both[token_rows:]
+
+
+def split_kernel(um, xs, gs):
+    xs[...] = um[: xs.shape[0]]
+    gs[...] = um[xs.shape[0] :]
+
+
+def move_rows(kernel, rows, *values):
+    vmem = pl.BlockSpec(memory_space=pltpu.VMEM)
+    width = values[0].shape[1]
+    return pl.pallas_call(
+        kernel,
+        in_specs=[vmem] * len(values),
+        out_specs=[vmem] * len(rows),
+        out_shape=[jax.ShapeDtypeStruct((count, width), jnp.bfloat16) for count in rows],
+        compiler_params=pltpu.CompilerParams(vmem_limit_bytes=4 * 1024 * 1024),
+        cost_estimate=pl.CostEstimate(flops=0, bytes_accessed=4 * sum(rows) * width, transcendentals=0),
+    )(*values)
+
+
+def add(*values):
+    return sum(value.astype(jnp.float32) for value in values).astype(jnp.bfloat16)
+
+
+def body_dense(checkpoint, scales, out_grad, expert_ids, gates, w_gate, w_up, w_down):
+    experts = lax.axis_size("expert")
+    ring = experts // 2
+    core = lax.axis_index("dp")
+    place = lax.axis_index("expert")
+    side = lax.axis_index("tensor")
+    token_rows, width = checkpoint.shape
+    tops = expert_ids.shape[1]
+
+    def over_x(value):
+        return lax.ppermute(value, "tensor", [(0, 1), (1, 0)])
+
+    def over_core(value):
+        return lax.ppermute(value, "dp", [(0, 1), (1, 0)])
+
+    def over_y(value):
+        return lax.ppermute(value, "expert", [(e, e ^ 1) for e in range(experts)])
+
+    order = [*range(0, ring, 2)][:1] + [*range(1, ring, 2)] + [*range(2, ring, 2)][::-1]
+    spot = {slow: at for at, slow in enumerate(order)}
+
+    def moved(e, shift):
+        return order[(spot[e // 2] + shift) % ring] * 2 + e % 2
+
+    def over_z(value, shift):
+        return lax.ppermute(value, "expert", [(e, moved(e, shift)) for e in range(experts)])
+
+    def after(values, *earlier):
+        return lax.optimization_barrier((values, earlier))[0]
+
+    pick_rows = -(-3 * tops * token_rows // (16 * width)) * 16
+    x_count, g_count = 2 * token_rows + pick_rows, 2 * token_rows
+
+    info = jnp.stack([side, core * experts + place, (1 - core) * experts + place])
+    places = [[moved(e, step) ^ way for step in range(ring) for way in range(2)] for e in range(experts)]
+    places = lax.dynamic_index_in_dim(jnp.array(places, jnp.int32), place, keepdims=False)
+    owners = (places[:, None] + jnp.stack([core, 1 - core])[None, :] * experts).reshape(-1)
+    checkpoint, out_grad, w_gate, w_up, w_down = after((checkpoint, out_grad, w_gate, w_up, w_down), info, owners)
+
+    others = [over_core(w[0]) for w in (w_gate, w_up, w_down)]
+    g_other = over_y(after(out_grad, others[0]))
+    operands = checkpoint, scales[None, :], expert_ids.T, gates.T, out_grad
+    own, x = pl.pallas_call(
+        prepare_kernel,
+        in_specs=[pl.BlockSpec(memory_space=pltpu.HBM)] * len(operands),
+        out_specs=[pl.BlockSpec(memory_space=pltpu.VMEM)] * 2,
+        out_shape=[jax.ShapeDtypeStruct((rows, width), jnp.bfloat16) for rows in (x_count, token_rows)],
+        scratch_shapes=[
+            *[pltpu.VMEM(value.shape, value.dtype) for value in operands],
+            pltpu.SemaphoreType.DMA((len(operands),)),
+        ],
+        compiler_params=pltpu.CompilerParams(vmem_limit_bytes=4 * 1024 * 1024),
+    )(*operands)
+    near, x_other = over_z(own, 1), over_x(x)
+    (both,) = move_rows(stack_kernel, (g_count,), x_other, g_other)
+    both_near = over_z(both, 1)
+    near = after(near, both)
+    terms, shares, tokens, hops, outs = [[None] * ring for _ in range(5)]
+
+    def hop(step):
+        xs, gs = shares[step]
+        tokens[step] = over_y(xs), over_x(gs)
+
+    shares[0] = move_rows(merge_kernel, (x_count, g_count), own, both)
+    hop(0)
+    others = after(others, near)
+    wg, wu, wd = [jnp.concatenate([w[0], far], axis=0) for w, far in zip((w_gate, w_up, w_down), others)]
+    near, both_near, wg, wu, wd = lax.optimization_barrier((near, both_near, wg, wu, wd))
+    um, *shares[1] = move_rows(join_kernel, (x_count + g_count, x_count, g_count), near, both_near)
+
+    def expert(step):
+        *outs, term = run_expert(tops, token_rows, info, *shares[step], *tokens[step], wg, wu, wd)
+        terms[step] = term[:, 0]
+        return outs
+
+    def kernel_and_hop(step):
+        outs[step] = expert(step)
+        hops[step] = over_x(outs[step][0]), over_y(outs[step][2])
+
+    moving = None
+    for step in range(1, ring):
+        if step > 1:
+            shares[step] = move_rows(split_kernel, (x_count, g_count), um)
+        hop(step)
+        if step < ring - 1:
+            following = over_z(um, 1)
+        if step == 1:
+            tokens[0] = after(tokens[0], um, shares[1])
+            kernel_and_hop(0)
+        if step > 1:
+            hops[step - 1] = after(hops[step - 1], tokens[step])
+        if step == ring - 1:
+            for back in range(1, ring - 1):
+                more_a, more_b = ((), ()) if moving is None else ((moving[:2],), (moving[2:],))
+                (_, a_keep, _, b_keep), (a_got, b_got) = outs[back], hops[back]
+                late = jnp.concatenate([add(a_keep, a_got, *more_a), add(b_keep, b_got, *more_b)])
+                late = lax.optimization_barrier(after(late, shares[step]))
+                moving = over_z(late, 1)
+            tokens[step] = after(tokens[step], late)
+        kernel_and_hop(step)
+        if step < ring - 1:
+            um = after(following, outs[step - 1], hops[step - 1])
+    (_, a_keep, _, b_keep), (a_got, b_got) = outs[-1], hops[-1]
+    term = jnp.stack(terms).reshape(ring, 2, 2, token_rows)
+    term_far = over_x(term)
+    a_got, b_got = after((a_got, b_got), term_far)
+    a_next, b_next = add(a_keep[1], a_got[1], moving[1]), add(b_keep[1], b_got[1], moving[3])
+    term = after(term + term_far, a_next, b_next)
+    term = [term[step] if step == 0 else over_z(term[step], -step) for step in range(ring)]
+    a = add(a_keep[0], a_got[0], moving[0], over_y(a_next))
+    b = add(b_keep[0], b_got[0], moving[2], over_x(b_next))
+    last = lax.optimization_barrier(jnp.concatenate([a, b]))
+    moving = over_z(last, 1)
+    (_, a_keep, _, b_keep), (a_got, b_got) = outs[0], after(hops[0], last)
+    a0_next, b0_next = add(a_keep[1], a_got[1]), add(b_keep[1], b_got[1])
+    a0, b0 = add(a_keep[0], a_got[0], over_y(a0_next)), add(b_keep[0], b_got[0], over_x(b0_next))
+    term = jnp.stack(after(term, a0_next, b0_next))
+    term = term[:, :, 0], over_y(term[:, :, 1])
+    half = token_rows // 2
+    total = jnp.concatenate([add(a0, moving[:half]), add(b0, moving[half:])])
+    vmem = pl.BlockSpec(memory_space=pltpu.VMEM)
+    gate_out = pl.pallas_call(
+        pick_kernel,
+        in_specs=[pl.BlockSpec(memory_space=pltpu.SMEM)] + [vmem] * (1 + len(term)),
+        out_specs=vmem,
+        out_shape=jax.ShapeDtypeStruct((tops, token_rows), jnp.float32),
+        compiler_params=pltpu.CompilerParams(vmem_limit_bytes=4 * 1024 * 1024),
+    )(owners, expert_ids.T, *term).T
+    return (total, gate_out)
+
+
+def body(checkpoint, scales, out_grad, expert_ids, gates, w_gate, w_up, w_down):
+    experts = lax.axis_size("expert")
+    token_rows, width = checkpoint.shape
+    pairs = lax.axis_size("dp") == 2 and lax.axis_size("tensor") == 2 and experts % 2 == 0
+    fits = token_rows % 128 == 0 and width % token_rows == 0
+    dense = pairs and fits and expert_ids.shape[1] >= experts > 4
+    chosen = body_dense if dense else body_routed
+    return chosen(checkpoint, scales, out_grad, expert_ids, gates, w_gate, w_up, w_down)
 
 
 def solution(mesh):

time: 391 us -> 140 us (0.36)
  blocking collectives: 140 us -> 0 us
  waiting for transfers between devices: 158 us -> 62.4 us
  starting transfers between devices: 10.4 us -> 44.6 us
  local copies, waits for them, and re-layouts: 33.7 us -> 4.77 us
  Pallas kernels: 0 us -> 22.6 us
  matrix products: 19.8 us -> 0 us
  between operations: 14.3 us -> 0.87 us
  other arithmetic: 15 us -> 4.34 us
    all_to_all x2 -> x0, waiting for transfers between devices: 114 us -> none  [the longest x1 82.2 us: body(): lax.all_to_all(send_grad, ('dp', 'expert'), split_axis=0, concat_axis=0,...]
    all_to_all x2 -> x0, blocking collectives: 114 us -> none  [the longest x1 100 us: body(): lax.all_to_all(send_x, ('dp', 'expert'), split_axis=0, concat_axis=0, til...]
    ppermute x0 -> x37, waiting for transfers between devices: none -> 62.4 us  [the longest x12 27.5 us: over_x(): return lax.ppermute(value, 'tensor', [(0, 1), (1, 0)])]
    ppermute x0 -> x37, starting transfers between devices: none -> 44.6 us  [the longest x10 17 us: over_z(): lax.ppermute(value, 'expert', [(e, moved(e, shift)) for e in range(expert...]
    reduce_scatter x1 -> x0, waiting for transfers between devices: 43.5 us -> none  [close_expert(): lax.psum_scatter(shaped.astype(jnp.float32).astype(jnp.bfloat16), 'tensor...]
    gather x5 -> x0, local copies, waits for them, and re-layouts: 26.9 us -> none  [the longest x1 7.92 us: body(): jnp.take(back_input.reshape(expert_count * slot_cap, share_width), slot_o...]
    pallas_call x0 -> x11, Pallas kernels: none -> 22.6 us  [the longest x4 20.8 us: run_expert(): pl.pallas_call(functools.partial(expert_kernel, tops), in_specs=[pl.Block...]
    dot_general x5 -> x0, matrix products: 19.8 us -> none  [the longest x1 5.2 us: body(): lax.dot_general(grads_flat, weight_down, contract, preferred_element_type...]
  transfers between devices with their start and end apart: 3 -> 37, of which waited for: 3 -> 14; matrix products, arithmetic and copies ran while one was open for 4% -> 2% of each run, Pallas kernels for 0% -> 16%
where the time goes in v2:
time: 140 us
  waiting for transfers between devices  62.4 us (45%)
  starting transfers between devices  44.6 us (32%)
  Pallas kernels  22.6 us (16%)
  local copies, waits for them, and re-layouts  4.77 us (3%)
  other arithmetic  4.34 us (3%)
    ppermute x12, waiting for transfers between devices, over_x(): return lax.ppermute(value, 'tensor', [(0, 1), (1, 0)])  27.5 us
    pallas_call x4, Pallas kernels, run_expert(): pl.pallas_call(functools.partial(expert_kernel, tops), in_specs=[pl.Block...  20.8 us
    ppermute x10, waiting for transfers between devices, over_z(): lax.ppermute(value, 'expert', [(e, moved(e, shift)) for e in range(expert...  19.1 us
    ppermute x10, starting transfers between devices, over_z(): lax.ppermute(value, 'expert', [(e, moved(e, shift)) for e in range(expert...  17 us
    ppermute x12, waiting for transfers between devices, over_y(): return lax.ppermute(value, 'expert', [(e, e ^ 1) for e in range(experts)])  15.9 us
    ppermute x12, starting transfers between devices, over_x(): return lax.ppermute(value, 'tensor', [(0, 1), (1, 0)])  13.8 us
    ppermute x12, starting transfers between devices, over_y(): return lax.ppermute(value, 'expert', [(e, e ^ 1) for e in range(experts)])  12.8 us
    unnamed x19, local copies, waits for them, and re-layouts  3.96 us
  transfers between devices with their start and end apart: 37, of which 14 were waited for; matrix products, arithmetic and copies ran while one was open for 2% of the time, Pallas kernels for 16%

profile of v2, /device:TPU:0, one launch (start us, length us, event | category | flops | bytes accessed | tf_op | source)
XLA Modules:
  0.0 139.5 jit_solution(7750663829034805658)
XLA Ops:
  0.6 0.7 dynamic-slice_bitcast_fusion
  2.6 0.9 copy-done
  3.6 0.9 copy-done.1
  6.8 2.7 %collective-permute-start.5 = (bf16[272,1024]{1,0:T(8,128)(2,1)S(1)}, bf16[272,1024]{1,0:T(8,128)(2,1)S(1)}, u32[]{:S(2)}, u32[]{:S(2)}) collective-permute-start(bf16[272,1024]{1,0:T(8,128)(2,1)S(1)} %get-tuple-element.71.own), channel_id=1, source_target_pairs={{0,2},{1,3},{2,6},{3,7},{4,0},{5,1},{6,4},{7,5},{8,10},{9,11},{10,... | collective-permute-start | bytes 1671176 | tf_op jit(solution)/shard_map/ppermute | solution.py:285
  9.5 1.5 %collective-permute-start = (bf16[128,1024]{1,0:T(8,128)(2,1)S(1)}, bf16[128,1024]{1,0:T(8,128)(2,1)S(1)}, u32[]{:S(2)}, u32[]{:S(2)}) collective-permute-start(bf16[128,1024]{1,0:T(8,128)(2,1)S(1)} %get-tuple-element.72), channel_id=1, source_target_pairs={{0,8},{8,0},{1,9},{9,1},{2,10},{10,2},{3,11},{11,3},{4,12},{12,4},... | collective-permute-start | bytes 786440 | tf_op jit(solution)/shard_map/ppermute | solution.py:270
  11.0 1.5 %collective-permute-start.2 = (bf16[128,1024]{1,0:T(8,128)(2,1)S(1)}, bf16[128,1024]{1,0:T(8,128)(2,1)S(1)}, u32[]{:S(2)}, u32[]{:S(2)}) collective-permute-start(bf16[128,1024]{1,0:T(8,128)(2,1)S(1)} %copy-done.1), channel_id=1, source_target_pairs={{0,1},{1,0},{2,3},{3,2},{4,5},{5,4},{6,7},{7,6},{8,9},{9,8},{10,11... | collective-permute-start | bytes 786440 | tf_op jit(solution)/shard_map/ppermute | solution.py:276
  12.6 5.4 %collective-permute-done.first = bf16[128,1024]{1,0:T(8,128)(2,1)S(1)} collective-permute-done((bf16[128,1024]{1,0:T(8,128)(2,1)S(1)}, bf16[128,1024]{1,0:T(8,128)(2,1)S(1)}, u32[]{:S(2)}, u32[]{:S(2)}) %collective-permute-start) | collective-permute-done | bytes 262176 | tf_op jit(solution)/shard_map/ppermute | solution.py:270
  17.9 1.2 collective-permute-done.2.second
  19.2 2.6 %collective-permute-start.6 = (bf16[256,1024]{1,0:T(8,128)(2,1)S(1)}, bf16[256,1024]{1,0:T(8,128)(2,1)S(1)}, u32[]{:S(2)}, u32[]{:S(2)}) collective-permute-start(bf16[256,1024]{1,0:T(8,128)(2,1)S(1)} %shard_map.105.both), channel_id=1, source_target_pairs={{0,2},{1,3},{2,6},{3,7},{4,0},{5,1},{6,4},{7,5},{8,10},{9,11},{10,... | collective-permute-start | bytes 1572872 | tf_op jit(solution)/shard_map/ppermute | solution.py:285
  21.9 2.1 %collective-permute-done.5.own = bf16[272,1024]{1,0:T(8,128)(2,1)S(1)} collective-permute-done((bf16[272,1024]{1,0:T(8,128)(2,1)S(1)}, bf16[272,1024]{1,0:T(8,128)(2,1)S(1)}, u32[]{:S(2)}, u32[]{:S(2)}) %collective-permute-start.5) | collective-permute-done | bytes 557088 | tf_op jit(solution)/shard_map/ppermute | solution.py:285
  24.0 1.8 %collective-permute-start.3 = (bf16[272,1024]{1,0:T(8,128)(2,1)S(1)}, bf16[272,1024]{1,0:T(8,128)(2,1)S(1)}, u32[]{:S(2)}, u32[]{:S(2)}) collective-permute-start(bf16[272,1024]{1,0:T(8,128)(2,1)S(1)} %get-tuple-element.75.xs_ref), channel_id=1, source_target_pairs={{0,1},{1,0},{2,3},{3,2},{4,5},{5,4},{6,7},{7,6},{8,9},{9,8},{10,11... | collective-permute-start | bytes 1671176 | tf_op jit(solution)/shard_map/ppermute | solution.py:276
  25.8 1.5 %collective-permute-start.4 = (bf16[256,1024]{1,0:T(8,128)(2,1)S(1)}, bf16[256,1024]{1,0:T(8,128)(2,1)S(1)}, u32[]{:S(2)}, u32[]{:S(2)}) collective-permute-start(bf16[256,1024]{1,0:T(8,128)(2,1)S(1)} %get-tuple-element.76.gs_ref), channel_id=1, source_target_pairs={{0,8},{8,0},{1,9},{9,1},{2,10},{10,2},{3,11},{11,3},{4,12},{12,4},... | collective-permute-start | bytes 1572872 | tf_op jit(solution)/shard_map/ppermute | solution.py:270
  27.3 2.0 %pad_maximum_fusion = (bf16[768,2048]{1,0:T(8,128)(2,1)S(1)}, bf16[768,2048]{1,0:T(8,128)(2,1)S(1)}) fusion(bf16[384,2048]{1,0:T(8,128)(2,1)S(1)} %collective-permute-done.1, bf16[384,2048]{1,0:T(8,128)(2,1)S(1)} %bitcast.73, bf16[384,2048]{1,0:T(8,128)(2,1)S(1)} %collective-permute-done.7, bf16[384,2048]{1,0:T(8,128)(2,1)} %bitcast.75), kind=kLoop, calls=%fused_computation | loop fusion | flops 12582912 | bytes 12582912 | tf_op jit(solution)/shard_map/concatenate | solution.py:326
  29.7 5.3 %collective-permute-done.6.both = bf16[256,1024]{1,0:T(8,128)(2,1)S(1)} collective-permute-done((bf16[256,1024]{1,0:T(8,128)(2,1)S(1)}, bf16[256,1024]{1,0:T(8,128)(2,1)S(1)}, u32[]{:S(2)}, u32[]{:S(2)}) %collective-permute-start.6) | collective-permute-done | bytes 524320 | tf_op jit(solution)/shard_map/ppermute | solution.py:285
  35.2 0.9 collective-permute-start.11
  36.1 1.5 %collective-permute-start.13 = (bf16[272,1024]{1,0:T(8,128)(2,1)S(1)}, bf16[272,1024]{1,0:T(8,128)(2,1)S(1)}, u32[]{:S(2)}, u32[]{:S(2)}) collective-permute-start(bf16[272,1024]{1,0:T(8,128)(2,1)S(1)} %get-tuple-element.86.xs_ref), channel_id=1, source_target_pairs={{0,1},{1,0},{2,3},{3,2},{4,5},{5,4},{6,7},{7,6},{8,9},{9,8},{10,11... | collective-permute-start | bytes 1671176 | tf_op jit(solution)/shard_map/ppermute | solution.py:276
  37.6 1.5 %collective-permute-start.14 = (bf16[256,1024]{1,0:T(8,128)(2,1)S(1)}, bf16[256,1024]{1,0:T(8,128)(2,1)S(1)}, u32[]{:S(2)}, u32[]{:S(2)}) collective-permute-start(bf16[256,1024]{1,0:T(8,128)(2,1)S(1)} %get-tuple-element.87.gs_ref), channel_id=1, source_target_pairs={{0,8},{8,0},{1,9},{9,1},{2,10},{10,2},{3,11},{11,3},{4,12},{12,4},... | collective-permute-start | bytes 1572872 | tf_op jit(solution)/shard_map/ppermute | solution.py:270
  39.1 5.2 %shard_map.108 = (bf16[2,64,1024]{2,1,0:T(8,128)(2,1)S(1)}, bf16[2,64,1024]{2,1,0:T(8,128)(2,1)S(1)}, bf16[2,64,1024]{2,1,0:T(8,128)(2,1)S(1)}, bf16[2,64,1024]{2,1,0:T(8,128)(2,1)S(1)}, f32[2,8,256]{2,1,0:T(8,128)S(1)}) custom-call(s32[3]{0:T(128)S(1)} %pad_add_fusion.info_ref, bf16[272,1024]{1,0:T(8,128)(2,1)S(1)} %get-tuple-element.75.xs_ref, ...), custom_call_target="tpu_custom_call" | custom-call | flops 4026531840 | bytes 12582912 | tf_op jit(solution)/shard_map/pallas_call | solution.py:162
  44.9 1.5 %collective-permute-start.9 = (bf16[2,64,1024]{2,1,0:T(8,128)(2,1)S(1)}, bf16[2,64,1024]{2,1,0:T(8,128)(2,1)S(1)}, u32[]{:S(2)}, u32[]{:S(2)}) collective-permute-start(bf16[2,64,1024]{2,1,0:T(8,128)(2,1)S(1)} %get-tuple-element.94), channel_id=1, source_target_pairs={{0,8},{8,0},{1,9},{9,1},{2,10},{10,2},{3,11},{11,3},{4,12},{12,4},... | collective-permute-start | bytes 786440 | tf_op jit(solution)/shard_map/ppermute | solution.py:270
  46.3 9.4 %collective-permute-done.10 = bf16[2,64,1024]{2,1,0:T(8,128)(2,1)S(1)} collective-permute-done((bf16[2,64,1024]{2,1,0:T(8,128)(2,1)S(1)}, bf16[2,64,1024]{2,1,0:T(8,128)(2,1)S(1)}, u32[]{:S(2)}, u32[]{:S(2)}) %collective-permute-start.10) | collective-permute-done | bytes 262176 | tf_op jit(solution)/shard_map/ppermute | solution.py:276
  56.1 5.6 %collective-permute-done.11.um = bf16[528,1024]{1,0:T(8,128)(2,1)S(1)} collective-permute-done((bf16[528,1024]{1,0:T(8,128)(2,1)S(1)}, bf16[528,1024]{1,0:T(8,128)(2,1)S(1)}, u32[]{:S(2)}, u32[]{:S(2)}) %collective-permute-start.11) | collective-permute-done | bytes 1081376 | tf_op jit(solution)/shard_map/ppermute | solution.py:285
  61.8 0.7 collective-permute-start.12
  62.5 1.5 %collective-permute-start.17 = (bf16[272,1024]{1,0:T(8,128)(2,1)S(1)}, bf16[272,1024]{1,0:T(8,128)(2,1)S(1)}, u32[]{:S(2)}, u32[]{:S(2)}) collective-permute-start(bf16[272,1024]{1,0:T(8,128)(2,1)S(1)} %get-tuple-element.102.xs_ref), channel_id=1, source_target_pairs={{0,1},{1,0},{2,3},{3,2},{4,5},{5,4},{6,7},{7,6},{8,9},{9,8},{10,11... | collective-permute-start | bytes 1671176 | tf_op jit(solution)/shard_map/ppermute | solution.py:276
  64.0 1.5 %collective-permute-start.18 = (bf16[256,1024]{1,0:T(8,128)(2,1)S(1)}, bf16[256,1024]{1,0:T(8,128)(2,1)S(1)}, u32[]{:S(2)}, u32[]{:S(2)}) collective-permute-start(bf16[256,1024]{1,0:T(8,128)(2,1)S(1)} %get-tuple-element.103.gs_ref), channel_id=1, source_target_pairs={{0,8},{8,0},{1,9},{9,1},{2,10},{10,2},{3,11},{11,3},{4,12},{12,4},... | collective-permute-start | bytes 1572872 | tf_op jit(solution)/shard_map/ppermute | solution.py:270
  65.5 5.2 %shard_map.109 = (bf16[2,64,1024]{2,1,0:T(8,128)(2,1)S(1)}, bf16[2,64,1024]{2,1,0:T(8,128)(2,1)S(1)}, bf16[2,64,1024]{2,1,0:T(8,128)(2,1)S(1)}, bf16[2,64,1024]{2,1,0:T(8,128)(2,1)S(1)}, f32[2,8,256]{2,1,0:T(8,128)S(1)}) custom-call(s32[3]{0:T(128)S(1)} %pad_add_fusion.info_ref, bf16[272,1024]{1,0:T(8,128)(2,1)S(1)} %get-tuple-element.86.xs_ref, ...), custom_call_target="tpu_custom_call" | custom-call | flops 4026531840 | bytes 12582912 | tf_op jit(solution)/shard_map/pallas_call | solution.py:162
  71.8 9.9 %collective-permute-done.15 = bf16[2,64,1024]{2,1,0:T(8,128)(2,1)S(1)} collective-permute-done((bf16[2,64,1024]{2,1,0:T(8,128)(2,1)S(1)}, bf16[2,64,1024]{2,1,0:T(8,128)(2,1)S(1)}, u32[]{:S(2)}, u32[]{:S(2)}) %collective-permute-start.15) | collective-permute-done | bytes 262176 | tf_op jit(solution)/shard_map/ppermute | solution.py:270
  81.9 5.6 %collective-permute-done.12.um = bf16[528,1024]{1,0:T(8,128)(2,1)S(1)} collective-permute-done((bf16[528,1024]{1,0:T(8,128)(2,1)S(1)}, bf16[528,1024]{1,0:T(8,128)(2,1)S(1)}, u32[]{:S(2)}, u32[]{:S(2)}) %collective-permute-start.12) | collective-permute-done | bytes 1081376 | tf_op jit(solution)/shard_map/ppermute | solution.py:285
  87.6 1.2 collective-permute-start.19
  88.8 1.5 %collective-permute-start.20 = (bf16[256,1024]{1,0:T(8,128)(2,1)S(1)}, bf16[256,1024]{1,0:T(8,128)(2,1)S(1)}, u32[]{:S(2)}, u32[]{:S(2)}) collective-permute-start(bf16[256,1024]{1,0:T(8,128)(2,1)S(1)} %get-tuple-element.108.gs_ref), channel_id=1, source_target_pairs={{0,8},{8,0},{1,9},{9,1},{2,10},{10,2},{3,11},{11,3},{4,12},{12,4},... | collective-permute-start | bytes 1572872 | tf_op jit(solution)/shard_map/ppermute | solution.py:270
  90.3 0.8 collective-permute-start.23
  91.1 5.2 %shard_map.112 = (bf16[2,64,1024]{2,1,0:T(8,128)(2,1)S(1)}, bf16[2,64,1024]{2,1,0:T(8,128)(2,1)S(1)}, bf16[2,64,1024]{2,1,0:T(8,128)(2,1)S(1)}, bf16[2,64,1024]{2,1,0:T(8,128)(2,1)S(1)}, f32[2,8,256]{2,1,0:T(8,128)S(1)}) custom-call(s32[3]{0:T(128)S(1)} %pad_add_fusion.info_ref, bf16[272,1024]{1,0:T(8,128)(2,1)S(1)} %get-tuple-element.102.xs_ref, ...), custom_call_target="tpu_custom_call" | custom-call | flops 4026531840 | bytes 12582912 | tf_op jit(solution)/shard_map/pallas_call | solution.py:162
  97.4 8.4 %collective-permute-done.21 = bf16[2,64,1024]{2,1,0:T(8,128)(2,1)S(1)} collective-permute-done((bf16[2,64,1024]{2,1,0:T(8,128)(2,1)S(1)}, bf16[2,64,1024]{2,1,0:T(8,128)(2,1)S(1)}, u32[]{:S(2)}, u32[]{:S(2)}) %collective-permute-start.21) | collective-permute-done | bytes 262176 | tf_op jit(solution)/shard_map/ppermute | solution.py:270
  106.2 0.9 collective-permute-start.27
  107.0 5.2 %shard_map.113 = (bf16[2,64,1024]{2,1,0:T(8,128)(2,1)S(1)}, bf16[2,64,1024]{2,1,0:T(8,128)(2,1)S(1)}, bf16[2,64,1024]{2,1,0:T(8,128)(2,1)S(1)}, bf16[2,64,1024]{2,1,0:T(8,128)(2,1)S(1)}, f32[2,8,256]{2,1,0:T(8,128)S(1)}) custom-call(s32[3]{0:T(128)S(1)} %pad_add_fusion.info_ref, bf16[272,1024]{1,0:T(8,128)(2,1)S(1)} %get-tuple-element.107.xs_ref, ...), custom_call_target="tpu_custom_call" | custom-call | flops 4026531840 | bytes 12582912 | tf_op jit(solution)/shard_map/pallas_call | solution.py:162
  112.3 1.5 %collective-permute-start.24 = (bf16[2,64,1024]{2,1,0:T(8,128)(2,1)S(1)}, bf16[2,64,1024]{2,1,0:T(8,128)(2,1)S(1)}, u32[]{:S(2)}, u32[]{:S(2)}) collective-permute-start(bf16[2,64,1024]{2,1,0:T(8,128)(2,1)S(1)} %get-tuple-element.120), channel_id=1, source_target_pairs={{0,8},{8,0},{1,9},{9,1},{2,10},{10,2},{3,11},{11,3},{4,12},{12,4},... | collective-permute-start | bytes 786440 | tf_op jit(solution)/shard_map/ppermute | solution.py:270
  113.8 1.0 collective-permute-start.25
  115.4 3.4 %collective-permute-done.26 = f32[4,2,2,128]{3,1,2,0:T(2,128)S(1)} collective-permute-done((f32[4,2,2,128]{3,1,2,0:T(2,128)S(1)}, f32[4,2,2,128]{3,1,2,0:T(2,128)S(1)}, u32[]{:S(2)}, u32[]{:S(2)}) %collective-permute-start.26) | collective-permute-done | bytes 8224 | tf_op jit(solution)/shard_map/ppermute | solution.py:270
  118.8 2.4 %collective-permute-done.25 = bf16[2,64,1024]{2,1,0:T(8,128)(2,1)S(1)} collective-permute-done((bf16[2,64,1024]{2,1,0:T(8,128)(2,1)S(1)}, bf16[2,64,1024]{2,1,0:T(8,128)(2,1)S(1)}, u32[]{:S(2)}, u32[]{:S(2)}) %collective-permute-start.25) | collective-permute-done | bytes 262176 | tf_op jit(solution)/shard_map/ppermute | solution.py:276
  121.3 0.9 collective-permute-start.28
  122.7 2.8 %collective-permute-start.33 = (f32[2,2,128]{2,0,1:T(2,128)S(1)}, f32[2,2,128]{2,0,1:T(2,128)S(1)}, u32[]{:S(2)}, u32[]{:S(2)}) collective-permute-start(f32[2,2,128]{2,0,1:T(2,128)S(1)} %get-tuple-element.148), channel_id=1, source_target_pairs={{0,4},{1,5},{2,0},{3,1},{4,6},{5,7},{6,2},{7,3},{8,12},{9,13},{10,... | collective-permute-start | bytes 6152 | tf_op jit(solution)/shard_map/ppermute | solution.py:285
  125.5 3.5 %collective-permute-start.34 = (f32[2,2,128]{2,0,1:T(2,128)S(1)}, f32[2,2,128]{2,0,1:T(2,128)S(1)}, u32[]{:S(2)}, u32[]{:S(2)}) collective-permute-start(f32[2,2,128]{2,0,1:T(2,128)S(1)} %get-tuple-element.147), channel_id=1, source_target_pairs={{0,6},{1,7},{2,4},{3,5},{4,2},{5,3},{6,0},{7,1},{8,14},{9,15},{10,... | collective-permute-start | bytes 6152 | tf_op jit(solution)/shard_map/ppermute | solution.py:285
  129.2 2.1 %collective-permute-start.31 = (bf16[128,1024]{1,0:T(8,128)(2,1)S(1)}, bf16[128,1024]{1,0:T(8,128)(2,1)S(1)}, u32[]{:S(2)}, u32[]{:S(2)}) collective-permute-start(bf16[128,1024]{1,0:T(8,128)(2,1)S(1)} %pad_maximum_fusion.5), channel_id=1, source_target_pairs={{0,2},{1,3},{2,6},{3,7},{4,0},{5,1},{6,4},{7,5},{8,10},{9,11},{10,... | collective-permute-start | bytes 786440 | tf_op jit(solution)/shard_map/ppermute | solution.py:285
  131.4 1.0 collective-permute-start.32
  132.4 0.7 collective-permute-start.30
  133.5 1.1 collective-permute-start.36
  134.6 2.8 %collective-permute-done.36.refs_1_ = f32[4,2,128]{2,1,0:T(2,128)S(1)} collective-permute-done((f32[4,2,128]{2,1,0:T(2,128)S(1)}, f32[4,2,128]{2,1,0:T(2,128)S(1)}, u32[]{:S(2)}, u32[]{:S(2)}) %collective-permute-start.36) | collective-permute-done | bytes 4128 | tf_op jit(solution)/shard_map/ppermute | solution.py:276
  137.4 1.2 shard_map.114
  138.8 0.7 pad_maximum_fusion.6
  (84 shorter events, 10.2 us)
Async XLA Ops:
  1.6 9.4 %collective-permute-start.1 = (bf16[384,2048]{1,0:T(8,128)(2,1)}, bf16[384,2048]{1,0:T(8,128)(2,1)S(1)}, u32[]{:S(2)}, u32[]{:S(2)}) collective-permute-start(bf16[384,2048]{1,0:T(8,128)(2,1)} %bitcast.72), channel_id=1, source_target_pairs={{0,16},{16,0},{1,17},{17,1},{2,18},{18,2},{3,19},{19,3},{4,20},{20... | collective-permute-start | bytes 4718600 | tf_op jit(solution)/shard_map/ppermute | solution.py:273
  2.1 21.9 %collective-permute-start.7 = (bf16[384,2048]{1,0:T(8,128)(2,1)}, bf16[384,2048]{1,0:T(8,128)(2,1)S(1)}, u32[]{:S(2)}, u32[]{:S(2)}) collective-permute-start(bf16[384,2048]{1,0:T(8,128)(2,1)} %bitcast.74), channel_id=1, source_target_pairs={{0,16},{16,0},{1,17},{17,1},{2,18},{18,2},{3,19},{19,3},{4,20},{20... | collective-permute-start | bytes 4718600 | tf_op jit(solution)/shard_map/ppermute | solution.py:273
  2.2 21.9 %collective-permute-start.8 = (bf16[384,2048]{1,0:T(8,128)(2,1)}, bf16[384,2048]{1,0:T(8,128)(2,1)S(1)}, u32[]{:S(2)}, u32[]{:S(2)}) collective-permute-start(bf16[384,2048]{1,0:T(8,128)(2,1)} %bitcast.76), channel_id=1, source_target_pairs={{0,16},{16,0},{1,17},{17,1},{2,18},{18,2},{3,19},{19,3},{4,20},{20... | collective-permute-start | bytes 4718600 | tf_op jit(solution)/shard_map/ppermute | solution.py:273
  2.6 0.9 copy-start
  3.6 0.9 copy-start.1
  4.5 0.7 copy-start.2
  5.2 0.7 copy-start.4
  5.9 0.7 copy-start.5
  6.5 20.8 %copy-start.6 = (bf16[1,384,2048]{2,1,0:T(8,128)(2,1)S(1)}, bf16[1,384,2048]{2,1,0:T(8,128)(2,1)}, u32[]{:S(2)}) copy-start(bf16[1,384,2048]{2,1,0:T(8,128)(2,1)} %param.14) | copy-start | bytes 4718596
  6.8 17.2 %collective-permute-start.5 = (bf16[272,1024]{1,0:T(8,128)(2,1)S(1)}, bf16[272,1024]{1,0:T(8,128)(2,1)S(1)}, u32[]{:S(2)}, u32[]{:S(2)}) collective-permute-start(bf16[272,1024]{1,0:T(8,128)(2,1)S(1)} %get-tuple-element.71.own), channel_id=1, source_target_pairs={{0,2},{1,3},{2,6},{3,7},{4,0},{5,1},{6,4},{7,5},{8,10},{9,11},{10,... | collective-permute-start | bytes 1671176 | tf_op jit(solution)/shard_map/ppermute | solution.py:285
  9.5 8.4 %collective-permute-start = (bf16[128,1024]{1,0:T(8,128)(2,1)S(1)}, bf16[128,1024]{1,0:T(8,128)(2,1)S(1)}, u32[]{:S(2)}, u32[]{:S(2)}) collective-permute-start(bf16[128,1024]{1,0:T(8,128)(2,1)S(1)} %get-tuple-element.72), channel_id=1, source_target_pairs={{0,8},{8,0},{1,9},{9,1},{2,10},{10,2},{3,11},{11,3},{4,12},{12,4},... | collective-permute-start | bytes 786440 | tf_op jit(solution)/shard_map/ppermute | solution.py:270
  11.0 8.1 %collective-permute-start.2 = (bf16[128,1024]{1,0:T(8,128)(2,1)S(1)}, bf16[128,1024]{1,0:T(8,128)(2,1)S(1)}, u32[]{:S(2)}, u32[]{:S(2)}) collective-permute-start(bf16[128,1024]{1,0:T(8,128)(2,1)S(1)} %copy-done.1), channel_id=1, source_target_pairs={{0,1},{1,0},{2,3},{3,2},{4,5},{5,4},{6,7},{7,6},{8,9},{9,8},{10,11... | collective-permute-start | bytes 786440 | tf_op jit(solution)/shard_map/ppermute | solution.py:276
  19.2 15.8 %collective-permute-start.6 = (bf16[256,1024]{1,0:T(8,128)(2,1)S(1)}, bf16[256,1024]{1,0:T(8,128)(2,1)S(1)}, u32[]{:S(2)}, u32[]{:S(2)}) collective-permute-start(bf16[256,1024]{1,0:T(8,128)(2,1)S(1)} %shard_map.105.both), channel_id=1, source_target_pairs={{0,2},{1,3},{2,6},{3,7},{4,0},{5,1},{6,4},{7,5},{8,10},{9,11},{10,... | collective-permute-start | bytes 1572872 | tf_op jit(solution)/shard_map/ppermute | solution.py:285
  24.0 15.0 %collective-permute-start.3 = (bf16[272,1024]{1,0:T(8,128)(2,1)S(1)}, bf16[272,1024]{1,0:T(8,128)(2,1)S(1)}, u32[]{:S(2)}, u32[]{:S(2)}) collective-permute-start(bf16[272,1024]{1,0:T(8,128)(2,1)S(1)} %get-tuple-element.75.xs_ref), channel_id=1, source_target_pairs={{0,1},{1,0},{2,3},{3,2},{4,5},{5,4},{6,7},{7,6},{8,9},{9,8},{10,11... | collective-permute-start | bytes 1671176 | tf_op jit(solution)/shard_map/ppermute | solution.py:276
  25.8 3.5 %copy-start.7 = (bf16[1,384,2048]{2,1,0:T(8,128)(2,1)S(1)}, bf16[1,384,2048]{2,1,0:T(8,128)(2,1)}, u32[]{:S(2)}) copy-start(bf16[1,384,2048]{2,1,0:T(8,128)(2,1)} %param.16) | copy-start | bytes 4718596
  25.8 13.3 %collective-permute-start.4 = (bf16[256,1024]{1,0:T(8,128)(2,1)S(1)}, bf16[256,1024]{1,0:T(8,128)(2,1)S(1)}, u32[]{:S(2)}, u32[]{:S(2)}) collective-permute-start(bf16[256,1024]{1,0:T(8,128)(2,1)S(1)} %get-tuple-element.76.gs_ref), channel_id=1, source_target_pairs={{0,8},{8,0},{1,9},{9,1},{2,10},{10,2},{3,11},{11,3},{4,12},{12,4},... | collective-permute-start | bytes 1572872 | tf_op jit(solution)/shard_map/ppermute | solution.py:270
  35.2 26.6 %collective-permute-start.11 = (bf16[528,1024]{1,0:T(8,128)(2,1)S(1)}, bf16[528,1024]{1,0:T(8,128)(2,1)S(1)}, u32[]{:S(2)}, u32[]{:S(2)}) collective-permute-start(bf16[528,1024]{1,0:T(8,128)(2,1)S(1)} %get-tuple-element.85), channel_id=1, source_target_pairs={{0,2},{1,3},{2,6},{3,7},{4,0},{5,1},{6,4},{7,5},{8,10},{9,11},{10,... | collective-permute-start | bytes 3244040 | tf_op jit(solution)/shard_map/ppermute | solution.py:285
  36.1 29.5 %collective-permute-start.13 = (bf16[272,1024]{1,0:T(8,128)(2,1)S(1)}, bf16[272,1024]{1,0:T(8,128)(2,1)S(1)}, u32[]{:S(2)}, u32[]{:S(2)}) collective-permute-start(bf16[272,1024]{1,0:T(8,128)(2,1)S(1)} %get-tuple-element.86.xs_ref), channel_id=1, source_target_pairs={{0,1},{1,0},{2,3},{3,2},{4,5},{5,4},{6,7},{7,6},{8,9},{9,8},{10,11... | collective-permute-start | bytes 1671176 | tf_op jit(solution)/shard_map/ppermute | solution.py:276
  37.6 27.9 %collective-permute-start.14 = (bf16[256,1024]{1,0:T(8,128)(2,1)S(1)}, bf16[256,1024]{1,0:T(8,128)(2,1)S(1)}, u32[]{:S(2)}, u32[]{:S(2)}) collective-permute-start(bf16[256,1024]{1,0:T(8,128)(2,1)S(1)} %get-tuple-element.87.gs_ref), channel_id=1, source_target_pairs={{0,8},{8,0},{1,9},{9,1},{2,10},{10,2},{3,11},{11,3},{4,12},{12,4},... | collective-permute-start | bytes 1572872 | tf_op jit(solution)/shard_map/ppermute | solution.py:270
  44.3 11.4 %collective-permute-start.10 = (bf16[2,64,1024]{2,1,0:T(8,128)(2,1)S(1)}, bf16[2,64,1024]{2,1,0:T(8,128)(2,1)S(1)}, u32[]{:S(2)}, u32[]{:S(2)}) collective-permute-start(bf16[2,64,1024]{2,1,0:T(8,128)(2,1)S(1)} %get-tuple-element.95), channel_id=1, source_target_pairs={{0,1},{1,0},{2,3},{3,2},{4,5},{5,4},{6,7},{7,6},{8,9},{9,8},{10,11... | collective-permute-start | bytes 786440 | tf_op jit(solution)/shard_map/ppermute | solution.py:276
  44.9 11.3 %collective-permute-start.9 = (bf16[2,64,1024]{2,1,0:T(8,128)(2,1)S(1)}, bf16[2,64,1024]{2,1,0:T(8,128)(2,1)S(1)}, u32[]{:S(2)}, u32[]{:S(2)}) collective-permute-start(bf16[2,64,1024]{2,1,0:T(8,128)(2,1)S(1)} %get-tuple-element.94), channel_id=1, source_target_pairs={{0,8},{8,0},{1,9},{9,1},{2,10},{10,2},{3,11},{11,3},{4,12},{12,4},... | collective-permute-start | bytes 786440 | tf_op jit(solution)/shard_map/ppermute | solution.py:270
  61.8 25.7 %collective-permute-start.12 = (bf16[528,1024]{1,0:T(8,128)(2,1)S(1)}, bf16[528,1024]{1,0:T(8,128)(2,1)S(1)}, u32[]{:S(2)}, u32[]{:S(2)}) collective-permute-start(bf16[528,1024]{1,0:T(8,128)(2,1)S(1)} %collective-permute-done.11.um), channel_id=1, source_target_pairs={{0,2},{1,3},{2,6},{3,7},{4,0},{5,1},{6,4},{7,5},{8,10},{9,11},{10,... | collective-permute-start | bytes 3244040 | tf_op jit(solution)/shard_map/ppermute | solution.py:285
  62.5 19.2 %collective-permute-start.17 = (bf16[272,1024]{1,0:T(8,128)(2,1)S(1)}, bf16[272,1024]{1,0:T(8,128)(2,1)S(1)}, u32[]{:S(2)}, u32[]{:S(2)}) collective-permute-start(bf16[272,1024]{1,0:T(8,128)(2,1)S(1)} %get-tuple-element.102.xs_ref), channel_id=1, source_target_pairs={{0,1},{1,0},{2,3},{3,2},{4,5},{5,4},{6,7},{7,6},{8,9},{9,8},{10,11... | collective-permute-start | bytes 1671176 | tf_op jit(solution)/shard_map/ppermute | solution.py:276
  64.0 17.7 %collective-permute-start.18 = (bf16[256,1024]{1,0:T(8,128)(2,1)S(1)}, bf16[256,1024]{1,0:T(8,128)(2,1)S(1)}, u32[]{:S(2)}, u32[]{:S(2)}) collective-permute-start(bf16[256,1024]{1,0:T(8,128)(2,1)S(1)} %get-tuple-element.103.gs_ref), channel_id=1, source_target_pairs={{0,8},{8,0},{1,9},{9,1},{2,10},{10,2},{3,11},{11,3},{4,12},{12,4},... | collective-permute-start | bytes 1572872 | tf_op jit(solution)/shard_map/ppermute | solution.py:270
  70.7 11.0 %collective-permute-start.15 = (bf16[2,64,1024]{2,1,0:T(8,128)(2,1)S(1)}, bf16[2,64,1024]{2,1,0:T(8,128)(2,1)S(1)}, u32[]{:S(2)}, u32[]{:S(2)}) collective-permute-start(bf16[2,64,1024]{2,1,0:T(8,128)(2,1)S(1)} %get-tuple-element.98), channel_id=1, source_target_pairs={{0,8},{8,0},{1,9},{9,1},{2,10},{10,2},{3,11},{11,3},{4,12},{12,4},... | collective-permute-start | bytes 786440 | tf_op jit(solution)/shard_map/ppermute | solution.py:270
  71.3 10.4 %collective-permute-start.16 = (bf16[2,64,1024]{2,1,0:T(8,128)(2,1)S(1)}, bf16[2,64,1024]{2,1,0:T(8,128)(2,1)S(1)}, u32[]{:S(2)}, u32[]{:S(2)}) collective-permute-start(bf16[2,64,1024]{2,1,0:T(8,128)(2,1)S(1)} %get-tuple-element.100), channel_id=1, source_target_pairs={{0,1},{1,0},{2,3},{3,2},{4,5},{5,4},{6,7},{7,6},{8,9},{9,8},{10,11... | collective-permute-start | bytes 786440 | tf_op jit(solution)/shard_map/ppermute | solution.py:276
  87.6 18.3 %collective-permute-start.19 = (bf16[272,1024]{1,0:T(8,128)(2,1)S(1)}, bf16[272,1024]{1,0:T(8,128)(2,1)S(1)}, u32[]{:S(2)}, u32[]{:S(2)}) collective-permute-start(bf16[272,1024]{1,0:T(8,128)(2,1)S(1)} %get-tuple-element.107.xs_ref), channel_id=1, source_target_pairs={{0,1},{1,0},{2,3},{3,2},{4,5},{5,4},{6,7},{7,6},{8,9},{9,8},{10,11... | collective-permute-start | bytes 1671176 | tf_op jit(solution)/shard_map/ppermute | solution.py:276
  88.8 17.0 %collective-permute-start.20 = (bf16[256,1024]{1,0:T(8,128)(2,1)S(1)}, bf16[256,1024]{1,0:T(8,128)(2,1)S(1)}, u32[]{:S(2)}, u32[]{:S(2)}) collective-permute-start(bf16[256,1024]{1,0:T(8,128)(2,1)S(1)} %get-tuple-element.108.gs_ref), channel_id=1, source_target_pairs={{0,8},{8,0},{1,9},{9,1},{2,10},{10,2},{3,11},{11,3},{4,12},{12,4},... | collective-permute-start | bytes 1572872 | tf_op jit(solution)/shard_map/ppermute | solution.py:270
  90.3 15.5 %collective-permute-start.23 = (bf16[4,64,1024]{2,1,0:T(8,128)(2,1)S(1)}, bf16[4,64,1024]{2,1,0:T(8,128)(2,1)S(1)}, u32[]{:S(2)}, u32[]{:S(2)}) collective-permute-start(bf16[4,64,1024]{2,1,0:T(8,128)(2,1)S(1)} %pad_maximum_fusion.3), channel_id=1, source_target_pairs={{0,2},{1,3},{2,6},{3,7},{4,0},{5,1},{6,4},{7,5},{8,10},{9,11},{10,... | collective-permute-start | bytes 1572872 | tf_op jit(solution)/shard_map/ppermute | solution.py:285
  96.3 9.5 %collective-permute-start.21 = (bf16[2,64,1024]{2,1,0:T(8,128)(2,1)S(1)}, bf16[2,64,1024]{2,1,0:T(8,128)(2,1)S(1)}, u32[]{:S(2)}, u32[]{:S(2)}) collective-permute-start(bf16[2,64,1024]{2,1,0:T(8,128)(2,1)S(1)} %get-tuple-element.110), channel_id=1, source_target_pairs={{0,8},{8,0},{1,9},{9,1},{2,10},{10,2},{3,11},{11,3},{4,12},{12,4},... | collective-permute-start | bytes 786440 | tf_op jit(solution)/shard_map/ppermute | solution.py:270
  96.9 9.0 %collective-permute-start.22 = (bf16[2,64,1024]{2,1,0:T(8,128)(2,1)S(1)}, bf16[2,64,1024]{2,1,0:T(8,128)(2,1)S(1)}, u32[]{:S(2)}, u32[]{:S(2)}) collective-permute-start(bf16[2,64,1024]{2,1,0:T(8,128)(2,1)S(1)} %get-tuple-element.111), channel_id=1, source_target_pairs={{0,1},{1,0},{2,3},{3,2},{4,5},{5,4},{6,7},{7,6},{8,9},{9,8},{10,11... | collective-permute-start | bytes 786440 | tf_op jit(solution)/shard_map/ppermute | solution.py:276
  106.2 15.0 %collective-permute-start.27 = (bf16[4,64,1024]{2,1,0:T(8,128)(2,1)S(1)}, bf16[4,64,1024]{2,1,0:T(8,128)(2,1)S(1)}, u32[]{:S(2)}, u32[]{:S(2)}) collective-permute-start(bf16[4,64,1024]{2,1,0:T(8,128)(2,1)S(1)} %pad_maximum_fusion.4), channel_id=1, source_target_pairs={{0,2},{1,3},{2,6},{3,7},{4,0},{5,1},{6,4},{7,5},{8,10},{9,11},{10,... | collective-permute-start | bytes 1572872 | tf_op jit(solution)/shard_map/ppermute | solution.py:285
  112.2 25.2 %copy-start.3 = (s32[128,8]{0,1:T(8,128)S(1)}, s32[128,8]{0,1:T(8,128)}, u32[]{:S(2)}) copy-start(s32[128,8]{0,1:T(8,128)} %param.12) | copy-start | bytes 12292
  112.3 6.5 %collective-permute-start.24 = (bf16[2,64,1024]{2,1,0:T(8,128)(2,1)S(1)}, bf16[2,64,1024]{2,1,0:T(8,128)(2,1)S(1)}, u32[]{:S(2)}, u32[]{:S(2)}) collective-permute-start(bf16[2,64,1024]{2,1,0:T(8,128)(2,1)S(1)} %get-tuple-element.120), channel_id=1, source_target_pairs={{0,8},{8,0},{1,9},{9,1},{2,10},{10,2},{3,11},{11,3},{4,12},{12,4},... | collective-permute-start | bytes 786440 | tf_op jit(solution)/shard_map/ppermute | solution.py:270
  113.8 7.4 %collective-permute-start.25 = (bf16[2,64,1024]{2,1,0:T(8,128)(2,1)S(1)}, bf16[2,64,1024]{2,1,0:T(8,128)(2,1)S(1)}, u32[]{:S(2)}, u32[]{:S(2)}) collective-permute-start(bf16[2,64,1024]{2,1,0:T(8,128)(2,1)S(1)} %get-tuple-element.121), channel_id=1, source_target_pairs={{0,1},{1,0},{2,3},{3,2},{4,5},{5,4},{6,7},{7,6},{8,9},{9,8},{10,11... | collective-permute-start | bytes 786440 | tf_op jit(solution)/shard_map/ppermute | solution.py:276
  114.8 4.0 %collective-permute-start.26 = (f32[4,2,2,128]{3,1,2,0:T(2,128)S(1)}, f32[4,2,2,128]{3,1,2,0:T(2,128)S(1)}, u32[]{:S(2)}, u32[]{:S(2)}) collective-permute-start(f32[4,2,2,128]{3,1,2,0:T(2,128)S(1)} %constant_dynamic-update-slice_fusion), channel_id=1, source_target_pairs={{0,8},{8,0},{1,9},{9,1},{2,10},{10,2},{3,11},{11,3},{4,12},{12,4},... | collective-permute-start | bytes 24584 | tf_op jit(solution)/shard_map/ppermute | solution.py:270
  121.3 7.7 %collective-permute-start.28 = (bf16[64,1024]{1,0:T(8,128)(2,1)S(1)}, bf16[64,1024]{1,0:T(8,128)(2,1)S(1)}, u32[]{:S(2)}, u32[]{:S(2)}) collective-permute-start(bf16[64,1024]{1,0:T(8,128)(2,1)S(1)} %get-tuple-element.138), channel_id=1, source_target_pairs={{0,1},{1,0},{2,3},{3,2},{4,5},{5,4},{6,7},{7,6},{8,9},{9,8},{10,11... | collective-permute-start | bytes 393224 | tf_op jit(solution)/shard_map/ppermute | solution.py:276
  122.2 6.8 %collective-permute-start.29 = (bf16[64,1024]{1,0:T(8,128)(2,1)S(1)}, bf16[64,1024]{1,0:T(8,128)(2,1)S(1)}, u32[]{:S(2)}, u32[]{:S(2)}) collective-permute-start(bf16[64,1024]{1,0:T(8,128)(2,1)S(1)} %get-tuple-element.139), channel_id=1, source_target_pairs={{0,8},{8,0},{1,9},{9,1},{2,10},{10,2},{3,11},{11,3},{4,12},{12,4},... | collective-permute-start | bytes 393224 | tf_op jit(solution)/shard_map/ppermute | solution.py:270
  122.7 9.7 %collective-permute-start.33 = (f32[2,2,128]{2,0,1:T(2,128)S(1)}, f32[2,2,128]{2,0,1:T(2,128)S(1)}, u32[]{:S(2)}, u32[]{:S(2)}) collective-permute-start(f32[2,2,128]{2,0,1:T(2,128)S(1)} %get-tuple-element.148), channel_id=1, source_target_pairs={{0,4},{1,5},{2,0},{3,1},{4,6},{5,7},{6,2},{7,3},{8,12},{9,13},{10,... | collective-permute-start | bytes 6152 | tf_op jit(solution)/shard_map/ppermute | solution.py:285
  125.5 7.6 %collective-permute-start.34 = (f32[2,2,128]{2,0,1:T(2,128)S(1)}, f32[2,2,128]{2,0,1:T(2,128)S(1)}, u32[]{:S(2)}, u32[]{:S(2)}) collective-permute-start(f32[2,2,128]{2,0,1:T(2,128)S(1)} %get-tuple-element.147), channel_id=1, source_target_pairs={{0,6},{1,7},{2,4},{3,5},{4,2},{5,3},{6,0},{7,1},{8,14},{9,15},{10,... | collective-permute-start | bytes 6152 | tf_op jit(solution)/shard_map/ppermute | solution.py:285
  129.0 4.5 %collective-permute-start.35 = (f32[2,2,128]{2,0,1:T(2,128)S(1)}, f32[2,2,128]{2,0,1:T(2,128)S(1)}, u32[]{:S(2)}, u32[]{:S(2)}) collective-permute-start(f32[2,2,128]{2,0,1:T(2,128)S(1)} %get-tuple-element.146), channel_id=1, source_target_pairs={{0,2},{1,3},{2,6},{3,7},{4,0},{5,1},{6,4},{7,5},{8,10},{9,11},{10,... | collective-permute-start | bytes 6152 | tf_op jit(solution)/shard_map/ppermute | solution.py:285
  129.2 9.4 %collective-permute-start.31 = (bf16[128,1024]{1,0:T(8,128)(2,1)S(1)}, bf16[128,1024]{1,0:T(8,128)(2,1)S(1)}, u32[]{:S(2)}, u32[]{:S(2)}) collective-permute-start(bf16[128,1024]{1,0:T(8,128)(2,1)S(1)} %pad_maximum_fusion.5), channel_id=1, source_target_pairs={{0,2},{1,3},{2,6},{3,7},{4,0},{5,1},{6,4},{7,5},{8,10},{9,11},{10,... | collective-permute-start | bytes 786440 | tf_op jit(solution)/shard_map/ppermute | solution.py:285
  131.4 7.2 %collective-permute-start.32 = (bf16[64,1024]{1,0:T(8,128)(2,1)S(1)}, bf16[64,1024]{1,0:T(8,128)(2,1)S(1)}, u32[]{:S(2)}, u32[]{:S(2)}) collective-permute-start(bf16[64,1024]{1,0:T(8,128)(2,1)S(1)} %fusion.7), channel_id=1, source_target_pairs={{0,8},{8,0},{1,9},{9,1},{2,10},{10,2},{3,11},{11,3},{4,12},{12,4},... | collective-permute-start | bytes 393224 | tf_op jit(solution)/shard_map/ppermute | solution.py:270
  132.4 6.2 %collective-permute-start.30 = (bf16[64,1024]{1,0:T(8,128)(2,1)S(1)}, bf16[64,1024]{1,0:T(8,128)(2,1)S(1)}, u32[]{:S(2)}, u32[]{:S(2)}) collective-permute-start(bf16[64,1024]{1,0:T(8,128)(2,1)S(1)} %fusion.6), channel_id=1, source_target_pairs={{0,1},{1,0},{2,3},{3,2},{4,5},{5,4},{6,7},{7,6},{8,9},{9,8},{10,11... | collective-permute-start | bytes 393224 | tf_op jit(solution)/shard_map/ppermute | solution.py:276
  133.5 3.9 %collective-permute-start.36 = (f32[4,2,128]{2,1,0:T(2,128)S(1)}, f32[4,2,128]{2,1,0:T(2,128)S(1)}, u32[]{:S(2)}, u32[]{:S(2)}) collective-permute-start(f32[4,2,128]{2,1,0:T(2,128)S(1)} %get-tuple-element.144), channel_id=1, source_target_pairs={{0,1},{1,0},{2,3},{3,2},{4,5},{5,4},{6,7},{7,6},{8,9},{9,8},{10,11... | collective-permute-start | bytes 12296 | tf_op jit(solution)/shard_map/ppermute | solution.py:276

commit v3 on v2

--- a/solution.py
+++ b/solution.py
@@ -173,44 +173,34 @@
     )(info, xs, gs, v, n, wg, wu, wd)
 
 
-def prepare_kernel(*refs):
-    sources, (own, x), held, arrived = refs[:5], refs[5:7], refs[7:12], refs[12]
-    copies = [pltpu.make_async_copy(*pair, arrived.at[at]) for at, pair in enumerate(zip(sources, held))]
-    for copy in copies:
-        copy.start()
-    for copy in copies:
-        copy.wait()
-    checkpoint, scales, ids, gates, out_grad = held
+def stack_kernel(x_far, g_far, ids, gates, both):
     f32 = jnp.float32
-    token_rows, width = x.shape
-    scale = jnp.broadcast_to(scales[...], (128, token_rows)).T[:, :1]
-    value = (checkpoint[...].astype(f32) * scale).astype(jnp.bfloat16)
-    x[...] = value
-    own[:token_rows] = value
+    token_rows, width = x_far.shape
+    both[:token_rows] = x_far[...]
+    both[token_rows : 2 * token_rows] = g_far[...]
     high = gates[...].astype(jnp.bfloat16).astype(f32)
     parts = [ids[...].astype(f32), high, gates[...] - high]
     flat = [part[k : k + 1] for part in parts for k in range(part.shape[0])]
-    count = own.shape[0] - 2 * token_rows
+    count = both.shape[0] - 2 * token_rows
     flat += [jnp.zeros((1, token_rows), f32)] * (count * width // token_rows - len(flat))
     per = width // token_rows
     rows = [jnp.concatenate(flat[row * per : (row + 1) * per], axis=1) for row in range(count)]
-    own[token_rows : token_rows + count] = jnp.concatenate(rows, axis=0).astype(jnp.bfloat16)
-    own[token_rows + count :] = out_grad[...]
-
-
-def stack_kernel(first, second, both):
-    rows = first.shape[0]
-    both[:rows] = first[...]
-    both[rows:] = second[...]
+    both[2 * token_rows :] = jnp.concatenate(rows, axis=0).astype(jnp.bfloat16)
 
 
 def merge_kernel(own, both, xs, gs):
-    token_rows = both.shape[0] // 2
-    split = own.shape[0] - token_rows
+    token_rows = own.shape[0] // 2
     xs[:token_rows] = both[:token_rows]
-    xs[token_rows:] = own[:split]
-    gs[:token_rows] = own[split:]
-    gs[token_rows:] = both[token_rows:]
+    xs[token_rows : 2 * token_rows] = own[:token_rows]
+    xs[2 * token_rows :] = both[2 * token_rows :]
+    gs[:token_rows] = own[token_rows:]
+    gs[token_rows:] = both[token_rows : 2 * token_rows]
+
+
+def join_kernel(own, both, um, xs, gs):
+    merge_kernel(own, both, xs, gs)
+    split = xs.shape[0]
+    merge_kernel(own, both, um.at[:split], um.at[split:])
 
 
 def pick_kernel(owners, ids, *refs):
@@ -223,16 +213,6 @@
                 owner = owners[(step * len(terms) + way) * which_count + which]
                 total = total + jnp.where(ids[...] == owner, ref[step, which : which + 1], 0.0)
     out[...] = total
-
-
-def join_kernel(own, both, um, xs, gs):
-    token_rows = both.shape[0] // 2
-    split = own.shape[0] - token_rows
-    count = xs.shape[0]
-    um[:token_rows] = xs[:token_rows] = both[:token_rows]
-    um[token_rows:count] = xs[token_rows:] = own[:split]
-    um[count : count + token_rows] = gs[:token_rows] = own[split:]
-    um[count + token_rows :] = gs[token_rows:] = both[token_rows:]
 
 
 def split_kernel(um, xs, gs):
@@ -291,27 +271,24 @@
     x_count, g_count = 2 * token_rows + pick_rows, 2 * token_rows
 
     info = jnp.stack([side, core * experts + place, (1 - core) * experts + place])
-    places = [[moved(e, step) ^ way for step in range(ring) for way in range(2)] for e in range(experts)]
-    places = lax.dynamic_index_in_dim(jnp.array(places, jnp.int32), place, keepdims=False)
-    owners = (places[:, None] + jnp.stack([core, 1 - core])[None, :] * experts).reshape(-1)
+    mine = sum(jnp.where(place // 2 == slow, at, 0) for at, slow in enumerate(order))
+    owners = []
+    for step in range(ring):
+        spot_there = (mine + step) % ring
+        there = sum(jnp.where(spot_there == at, slow, 0) for at, slow in enumerate(order))
+        for way in range(2):
+            for which in range(2):
+                owners.append((core ^ which) * experts + there * 2 + (place % 2 ^ way))
+    owners = jnp.stack(owners)
     checkpoint, out_grad, w_gate, w_up, w_down = after((checkpoint, out_grad, w_gate, w_up, w_down), info, owners)
 
-    others = [over_core(w[0]) for w in (w_gate, w_up, w_down)]
+    x = (checkpoint.astype(jnp.float32) * scales[:, None]).astype(jnp.bfloat16)
+    own = lax.optimization_barrier(jnp.concatenate([x, out_grad]))
+    near, x_other = over_z(own, 1), over_x(x)
+    others = [over_core(w[0]) for w in after((w_gate, w_up, w_down), own)]
     g_other = over_y(after(out_grad, others[0]))
-    operands = checkpoint, scales[None, :], expert_ids.T, gates.T, out_grad
-    own, x = pl.pallas_call(
-        prepare_kernel,
-        in_specs=[pl.BlockSpec(memory_space=pltpu.HBM)] * len(operands),
-        out_specs=[pl.BlockSpec(memory_space=pltpu.VMEM)] * 2,
-        out_shape=[jax.ShapeDtypeStruct((rows, width), jnp.bfloat16) for rows in (x_count, token_rows)],
-        scratch_shapes=[
-            *[pltpu.VMEM(value.shape, value.dtype) for value in operands],
-            pltpu.SemaphoreType.DMA((len(operands),)),
-        ],
-        compiler_params=pltpu.CompilerParams(vmem_limit_bytes=4 * 1024 * 1024),
-    )(*operands)
-    near, x_other = over_z(own, 1), over_x(x)
-    (both,) = move_rows(stack_kernel, (g_count,), x_other, g_other)
+    ids_t, gates_t = after((expert_ids.T, gates.T), x_other)
+    (both,) = move_rows(stack_kernel, (x_count,), x_other, g_other, ids_t, gates_t)
     both_near = over_z(both, 1)
     near = after(near, both)
     terms, shares, tokens, hops, outs = [[None] * ring for _ in range(5)]

time: 140 us -> 133 us (0.950)
  local copies, waits for them, and re-layouts: 4.77 us -> 2.12 us
  starting transfers between devices: 44.6 us -> 42.3 us
  waiting for transfers between devices: 62.4 us -> 60.2 us
    unnamed x19 -> x15, local copies, waits for them, and re-layouts: 3.96 us -> 2 us
    ppermute x12, starting transfers between devices: 13.8 us -> 12.2 us  [over_x(): return lax.ppermute(value, 'tensor', [(0, 1), (1, 0)])]
    ppermute x12, waiting for transfers between devices: 27.5 us -> 25.9 us  [over_x(): return lax.ppermute(value, 'tensor', [(0, 1), (1, 0)])]
  transfers between devices with their start and end apart: 37 -> 37, of which waited for: 14 -> 16; matrix products, arithmetic and copies ran while one was open for 2% -> 1% of each run, Pallas kernels for 16% -> 17%
where the time goes in v3:
time: 133 us
  waiting for transfers between devices  60.2 us (45%)
  starting transfers between devices  42.3 us (32%)
  Pallas kernels  22.3 us (17%)
  other arithmetic  5.28 us (4%)
  local copies, waits for them, and re-layouts  2.12 us (2%)
    ppermute x12, waiting for transfers between devices, over_x(): return lax.ppermute(value, 'tensor', [(0, 1), (1, 0)])  25.9 us
    pallas_call x4, Pallas kernels, run_expert(): pl.pallas_call(functools.partial(expert_kernel, tops), in_specs=[pl.Block...  20.7 us
    ppermute x10, waiting for transfers between devices, over_z(): lax.ppermute(value, 'expert', [(e, moved(e, shift)) for e in range(expert...  19.1 us
    ppermute x10, starting transfers between devices, over_z(): lax.ppermute(value, 'expert', [(e, moved(e, shift)) for e in range(expert...  16.8 us
    ppermute x12, waiting for transfers between devices, over_y(): return lax.ppermute(value, 'expert', [(e, e ^ 1) for e in range(experts)])  15.2 us
    ppermute x12, starting transfers between devices, over_y(): return lax.ppermute(value, 'expert', [(e, e ^ 1) for e in range(experts)])  12.2 us
    ppermute x12, starting transfers between devices, over_x(): return lax.ppermute(value, 'tensor', [(0, 1), (1, 0)])  12.2 us
  transfers between devices with their start and end apart: 37, of which 16 were waited for; matrix products, arithmetic and copies ran while one was open for 1% of the time, Pallas kernels for 17%

profile of v3, /device:TPU:0, one launch (start us, length us, event | category | flops | bytes accessed | tf_op | source)
XLA Modules:
  0.0 133.2 jit_solution(823891779099510582)
XLA Ops:
  0.9 1.2 multiply_convert_fusion
  2.2 1.0 pad_maximum_fusion.3.own
  4.2 2.7 %collective-permute-start.5 = (bf16[256,1024]{1,0:T(8,128)(2,1)S(1)}, bf16[256,1024]{1,0:T(8,128)(2,1)S(1)}, u32[]{:S(2)}, u32[]{:S(2)}) collective-permute-start(bf16[256,1024]{1,0:T(8,128)(2,1)S(1)} %pad_maximum_fusion.3.own), channel_id=1, source_target_pairs={{0,2},{1,3},{2,6},{3,7},{4,0},{5,1},{6,4},{7,5},{8,10},{9,11},{10,... | collective-permute-start | bytes 1572872 | tf_op jit(solution)/shard_map/ppermute | solution.py:265
  6.8 1.5 %collective-permute-start = (bf16[128,1024]{1,0:T(8,128)(2,1)S(1)}, bf16[128,1024]{1,0:T(8,128)(2,1)S(1)}, u32[]{:S(2)}, u32[]{:S(2)}) collective-permute-start(bf16[128,1024]{1,0:T(8,128)(2,1)S(1)} %multiply_convert_fusion), channel_id=1, source_target_pairs={{0,8},{8,0},{1,9},{9,1},{2,10},{10,2},{3,11},{11,3},{4,12},{12,4},... | collective-permute-start | bytes 786440 | tf_op jit(solution)/shard_map/ppermute | solution.py:250
  8.3 1.5 %collective-permute-start.2 = (bf16[128,1024]{1,0:T(8,128)(2,1)}, bf16[128,1024]{1,0:T(8,128)(2,1)S(1)}, u32[]{:S(2)}, u32[]{:S(2)}) collective-permute-start(bf16[128,1024]{1,0:T(8,128)(2,1)} %param.10), channel_id=1, source_target_pairs={{0,1},{1,0},{2,3},{3,2},{4,5},{5,4},{6,7},{7,6},{8,9},{9,8},{10,11... | collective-permute-start | bytes 786440 | tf_op jit(solution)/shard_map/ppermute | solution.py:256
  9.9 5.4 %collective-permute-done.x_far = bf16[128,1024]{1,0:T(8,128)(2,1)S(1)} collective-permute-done((bf16[128,1024]{1,0:T(8,128)(2,1)S(1)}, bf16[128,1024]{1,0:T(8,128)(2,1)S(1)}, u32[]{:S(2)}, u32[]{:S(2)}) %collective-permute-start) | collective-permute-done | bytes 262176 | tf_op jit(solution)/shard_map/ppermute | solution.py:250
  15.2 1.4 %collective-permute-done.2.g_far = bf16[128,1024]{1,0:T(8,128)(2,1)S(1)} collective-permute-done((bf16[128,1024]{1,0:T(8,128)(2,1)}, bf16[128,1024]{1,0:T(8,128)(2,1)S(1)}, u32[]{:S(2)}, u32[]{:S(2)}) %collective-permute-start.2) | collective-permute-done | bytes 262176 | tf_op jit(solution)/shard_map/ppermute | solution.py:256
  16.6 0.7 copy-done
  17.3 0.7 copy-done.2
  18.1 2.6 %collective-permute-start.6 = (bf16[272,1024]{1,0:T(8,128)(2,1)S(1)}, bf16[272,1024]{1,0:T(8,128)(2,1)S(1)}, u32[]{:S(2)}, u32[]{:S(2)}) collective-permute-start(bf16[272,1024]{1,0:T(8,128)(2,1)S(1)} %shard_map.95.both), channel_id=1, source_target_pairs={{0,2},{1,3},{2,6},{3,7},{4,0},{5,1},{6,4},{7,5},{8,10},{9,11},{10,... | collective-permute-start | bytes 1671176 | tf_op jit(solution)/shard_map/ppermute | solution.py:265
  20.8 1.6 %collective-permute-start.3 = (bf16[272,1024]{1,0:T(8,128)(2,1)S(1)}, bf16[272,1024]{1,0:T(8,128)(2,1)S(1)}, u32[]{:S(2)}, u32[]{:S(2)}) collective-permute-start(bf16[272,1024]{1,0:T(8,128)(2,1)S(1)} %get-tuple-element.81.xs_ref), channel_id=1, source_target_pairs={{0,1},{1,0},{2,3},{3,2},{4,5},{5,4},{6,7},{7,6},{8,9},{9,8},{10,11... | collective-permute-start | bytes 1671176 | tf_op jit(solution)/shard_map/ppermute | solution.py:256
  22.4 1.1 collective-permute-start.4
  23.5 0.8 pad_maximum_fusion
  25.3 7.7 %collective-permute-done.6.both = bf16[272,1024]{1,0:T(8,128)(2,1)S(1)} collective-permute-done((bf16[272,1024]{1,0:T(8,128)(2,1)S(1)}, bf16[272,1024]{1,0:T(8,128)(2,1)S(1)}, u32[]{:S(2)}, u32[]{:S(2)}) %collective-permute-start.6) | collective-permute-done | bytes 557088 | tf_op jit(solution)/shard_map/ppermute | solution.py:265
  33.2 1.3 collective-permute-start.11
  34.5 1.5 %collective-permute-start.13 = (bf16[272,1024]{1,0:T(8,128)(2,1)S(1)}, bf16[272,1024]{1,0:T(8,128)(2,1)S(1)}, u32[]{:S(2)}, u32[]{:S(2)}) collective-permute-start(bf16[272,1024]{1,0:T(8,128)(2,1)S(1)} %get-tuple-element.92.xs_ref), channel_id=1, source_target_pairs={{0,1},{1,0},{2,3},{3,2},{4,5},{5,4},{6,7},{7,6},{8,9},{9,8},{10,11... | collective-permute-start | bytes 1671176 | tf_op jit(solution)/shard_map/ppermute | solution.py:256
  36.0 1.1 collective-permute-start.14
  37.1 5.2 %shard_map.98 = (bf16[2,64,1024]{2,1,0:T(8,128)(2,1)S(1)}, bf16[2,64,1024]{2,1,0:T(8,128)(2,1)S(1)}, bf16[2,64,1024]{2,1,0:T(8,128)(2,1)S(1)}, bf16[2,64,1024]{2,1,0:T(8,128)(2,1)S(1)}, f32[2,8,256]{2,1,0:T(8,128)S(1)}) custom-call(s32[3]{0:T(128)S(1)} %pad_add_fusion.info_ref, bf16[272,1024]{1,0:T(8,128)(2,1)S(1)} %get-tuple-element.81.xs_ref, ...), custom_call_target="tpu_custom_call" | custom-call | flops 4026531840 | bytes 12582912 | tf_op jit(solution)/shard_map/pallas_call | solution.py:162
  42.8 0.9 collective-permute-start.9
  43.7 8.7 %collective-permute-done.10 = bf16[2,64,1024]{2,1,0:T(8,128)(2,1)S(1)} collective-permute-done((bf16[2,64,1024]{2,1,0:T(8,128)(2,1)S(1)}, bf16[2,64,1024]{2,1,0:T(8,128)(2,1)S(1)}, u32[]{:S(2)}, u32[]{:S(2)}) %collective-permute-start.10) | collective-permute-done | bytes 262176 | tf_op jit(solution)/shard_map/ppermute | solution.py:256
  53.0 5.5 %collective-permute-done.11.um = bf16[528,1024]{1,0:T(8,128)(2,1)S(1)} collective-permute-done((bf16[528,1024]{1,0:T(8,128)(2,1)S(1)}, bf16[528,1024]{1,0:T(8,128)(2,1)S(1)}, u32[]{:S(2)}, u32[]{:S(2)}) %collective-permute-start.11) | collective-permute-done | bytes 1081376 | tf_op jit(solution)/shard_map/ppermute | solution.py:265
  58.5 0.7 collective-permute-start.12
  59.2 1.5 %collective-permute-start.17 = (bf16[272,1024]{1,0:T(8,128)(2,1)S(1)}, bf16[272,1024]{1,0:T(8,128)(2,1)S(1)}, u32[]{:S(2)}, u32[]{:S(2)}) collective-permute-start(bf16[272,1024]{1,0:T(8,128)(2,1)S(1)} %get-tuple-element.108.xs_ref), channel_id=1, source_target_pairs={{0,1},{1,0},{2,3},{3,2},{4,5},{5,4},{6,7},{7,6},{8,9},{9,8},{10,11... | collective-permute-start | bytes 1671176 | tf_op jit(solution)/shard_map/ppermute | solution.py:256
  60.8 1.5 %collective-permute-start.18 = (bf16[256,1024]{1,0:T(8,128)(2,1)S(1)}, bf16[256,1024]{1,0:T(8,128)(2,1)S(1)}, u32[]{:S(2)}, u32[]{:S(2)}) collective-permute-start(bf16[256,1024]{1,0:T(8,128)(2,1)S(1)} %get-tuple-element.109.gs_ref), channel_id=1, source_target_pairs={{0,8},{8,0},{1,9},{9,1},{2,10},{10,2},{3,11},{11,3},{4,12},{12,4},... | collective-permute-start | bytes 1572872 | tf_op jit(solution)/shard_map/ppermute | solution.py:250
  62.3 5.2 %shard_map.99 = (bf16[2,64,1024]{2,1,0:T(8,128)(2,1)S(1)}, bf16[2,64,1024]{2,1,0:T(8,128)(2,1)S(1)}, bf16[2,64,1024]{2,1,0:T(8,128)(2,1)S(1)}, bf16[2,64,1024]{2,1,0:T(8,128)(2,1)S(1)}, f32[2,8,256]{2,1,0:T(8,128)S(1)}) custom-call(s32[3]{0:T(128)S(1)} %pad_add_fusion.info_ref, bf16[272,1024]{1,0:T(8,128)(2,1)S(1)} %get-tuple-element.92.xs_ref, ...), custom_call_target="tpu_custom_call" | custom-call | flops 4026531840 | bytes 12582912 | tf_op jit(solution)/shard_map/pallas_call | solution.py:162
  67.4 0.6 collective-permute-start.15
  68.6 8.6 %collective-permute-done.15 = bf16[2,64,1024]{2,1,0:T(8,128)(2,1)S(1)} collective-permute-done((bf16[2,64,1024]{2,1,0:T(8,128)(2,1)S(1)}, bf16[2,64,1024]{2,1,0:T(8,128)(2,1)S(1)}, u32[]{:S(2)}, u32[]{:S(2)}) %collective-permute-start.15) | collective-permute-done | bytes 262176 | tf_op jit(solution)/shard_map/ppermute | solution.py:250
  77.3 5.5 %collective-permute-done.12.um = bf16[528,1024]{1,0:T(8,128)(2,1)S(1)} collective-permute-done((bf16[528,1024]{1,0:T(8,128)(2,1)S(1)}, bf16[528,1024]{1,0:T(8,128)(2,1)S(1)}, u32[]{:S(2)}, u32[]{:S(2)}) %collective-permute-start.12) | collective-permute-done | bytes 1081376 | tf_op jit(solution)/shard_map/ppermute | solution.py:265
  82.9 1.2 collective-permute-start.19
  84.1 1.6 %collective-permute-start.20 = (bf16[256,1024]{1,0:T(8,128)(2,1)S(1)}, bf16[256,1024]{1,0:T(8,128)(2,1)S(1)}, u32[]{:S(2)}, u32[]{:S(2)}) collective-permute-start(bf16[256,1024]{1,0:T(8,128)(2,1)S(1)} %get-tuple-element.114.gs_ref), channel_id=1, source_target_pairs={{0,8},{8,0},{1,9},{9,1},{2,10},{10,2},{3,11},{11,3},{4,12},{12,4},... | collective-permute-start | bytes 1572872 | tf_op jit(solution)/shard_map/ppermute | solution.py:250
  85.7 0.8 collective-permute-start.23
  86.5 5.2 %shard_map.102 = (bf16[2,64,1024]{2,1,0:T(8,128)(2,1)S(1)}, bf16[2,64,1024]{2,1,0:T(8,128)(2,1)S(1)}, bf16[2,64,1024]{2,1,0:T(8,128)(2,1)S(1)}, bf16[2,64,1024]{2,1,0:T(8,128)(2,1)S(1)}, f32[2,8,256]{2,1,0:T(8,128)S(1)}) custom-call(s32[3]{0:T(128)S(1)} %pad_add_fusion.info_ref, bf16[272,1024]{1,0:T(8,128)(2,1)S(1)} %get-tuple-element.108.xs_ref, ...), custom_call_target="tpu_custom_call" | custom-call | flops 4026531840 | bytes 12582912 | tf_op jit(solution)/shard_map/pallas_call | solution.py:162
  91.7 0.6 collective-permute-start.21
  92.8 6.9 %collective-permute-done.21 = bf16[2,64,1024]{2,1,0:T(8,128)(2,1)S(1)} collective-permute-done((bf16[2,64,1024]{2,1,0:T(8,128)(2,1)S(1)}, bf16[2,64,1024]{2,1,0:T(8,128)(2,1)S(1)}, u32[]{:S(2)}, u32[]{:S(2)}) %collective-permute-start.21) | collective-permute-done | bytes 262176 | tf_op jit(solution)/shard_map/ppermute | solution.py:250
  100.2 2.3 %collective-permute-start.27 = (bf16[4,64,1024]{2,1,0:T(8,128)(2,1)S(1)}, bf16[4,64,1024]{2,1,0:T(8,128)(2,1)S(1)}, u32[]{:S(2)}, u32[]{:S(2)}) collective-permute-start(bf16[4,64,1024]{2,1,0:T(8,128)(2,1)S(1)} %pad_maximum_fusion.5), channel_id=1, source_target_pairs={{0,2},{1,3},{2,6},{3,7},{4,0},{5,1},{6,4},{7,5},{8,10},{9,11},{10,... | collective-permute-start | bytes 1572872 | tf_op jit(solution)/shard_map/ppermute | solution.py:265
  102.5 5.2 %shard_map.103 = (bf16[2,64,1024]{2,1,0:T(8,128)(2,1)S(1)}, bf16[2,64,1024]{2,1,0:T(8,128)(2,1)S(1)}, bf16[2,64,1024]{2,1,0:T(8,128)(2,1)S(1)}, bf16[2,64,1024]{2,1,0:T(8,128)(2,1)S(1)}, f32[2,8,256]{2,1,0:T(8,128)S(1)}) custom-call(s32[3]{0:T(128)S(1)} %pad_add_fusion.info_ref, bf16[272,1024]{1,0:T(8,128)(2,1)S(1)} %get-tuple-element.113.xs_ref, ...), custom_call_target="tpu_custom_call" | custom-call | flops 4026531840 | bytes 12582912 | tf_op jit(solution)/shard_map/pallas_call | solution.py:162
  107.6 1.6 %collective-permute-start.24 = (bf16[2,64,1024]{2,1,0:T(8,128)(2,1)S(1)}, bf16[2,64,1024]{2,1,0:T(8,128)(2,1)S(1)}, u32[]{:S(2)}, u32[]{:S(2)}) collective-permute-start(bf16[2,64,1024]{2,1,0:T(8,128)(2,1)S(1)} %get-tuple-element.126), channel_id=1, source_target_pairs={{0,8},{8,0},{1,9},{9,1},{2,10},{10,2},{3,11},{11,3},{4,12},{12,4},... | collective-permute-start | bytes 786440 | tf_op jit(solution)/shard_map/ppermute | solution.py:250
  110.3 4.3 %collective-permute-done.26 = f32[4,2,2,128]{3,1,2,0:T(2,128)S(1)} collective-permute-done((f32[4,2,2,128]{3,1,2,0:T(2,128)S(1)}, f32[4,2,2,128]{3,1,2,0:T(2,128)S(1)}, u32[]{:S(2)}, u32[]{:S(2)}) %collective-permute-start.26) | collective-permute-done | bytes 8224 | tf_op jit(solution)/shard_map/ppermute | solution.py:250
  114.7 2.3 %collective-permute-done.25 = bf16[2,64,1024]{2,1,0:T(8,128)(2,1)S(1)} collective-permute-done((bf16[2,64,1024]{2,1,0:T(8,128)(2,1)S(1)}, bf16[2,64,1024]{2,1,0:T(8,128)(2,1)S(1)}, u32[]{:S(2)}, u32[]{:S(2)}) %collective-permute-start.25) | collective-permute-done | bytes 262176 | tf_op jit(solution)/shard_map/ppermute | solution.py:256
  118.2 1.2 collective-permute-start.33
  119.4 3.5 %collective-permute-start.34 = (f32[2,2,128]{2,0,1:T(2,128)S(1)}, f32[2,2,128]{2,0,1:T(2,128)S(1)}, u32[]{:S(2)}, u32[]{:S(2)}) collective-permute-start(f32[2,2,128]{2,0,1:T(2,128)S(1)} %get-tuple-element.153), channel_id=1, source_target_pairs={{0,6},{1,7},{2,4},{3,5},{4,2},{5,3},{6,0},{7,1},{8,14},{9,15},{10,... | collective-permute-start | bytes 6152 | tf_op jit(solution)/shard_map/ppermute | solution.py:265
  123.5 1.7 %collective-permute-start.31 = (bf16[128,1024]{1,0:T(8,128)(2,1)S(1)}, bf16[128,1024]{1,0:T(8,128)(2,1)S(1)}, u32[]{:S(2)}, u32[]{:S(2)}) collective-permute-start(bf16[128,1024]{1,0:T(8,128)(2,1)S(1)} %pad_maximum_fusion.6), channel_id=1, source_target_pairs={{0,2},{1,3},{2,6},{3,7},{4,0},{5,1},{6,4},{7,5},{8,10},{9,11},{10,... | collective-permute-start | bytes 786440 | tf_op jit(solution)/shard_map/ppermute | solution.py:265
  125.3 0.6 collective-permute-start.32
  125.9 1.1 collective-permute-start.30
  127.4 1.2 collective-permute-start.36
  128.6 2.5 %collective-permute-done.36.refs_1_ = f32[4,2,128]{2,1,0:T(2,128)S(1)} collective-permute-done((f32[4,2,128]{2,1,0:T(2,128)S(1)}, f32[4,2,128]{2,1,0:T(2,128)S(1)}, u32[]{:S(2)}, u32[]{:S(2)}) %collective-permute-start.36) | collective-permute-done | bytes 4128 | tf_op jit(solution)/shard_map/ppermute | solution.py:256
  131.1 1.2 shard_map.104
  132.4 0.7 pad_maximum_fusion.7
  (78 shorter events, 8.9 us)
Async XLA Ops:
  0.6 22.8 %copy-start.3 = (bf16[1,384,2048]{2,1,0:T(8,128)(2,1)S(1)}, bf16[1,384,2048]{2,1,0:T(8,128)(2,1)}, u32[]{:S(2)}) copy-start(bf16[1,384,2048]{2,1,0:T(8,128)(2,1)} %param.13) | copy-start | bytes 4718596
  3.2 5.2 %collective-permute-start.1 = (bf16[384,2048]{1,0:T(8,128)(2,1)}, bf16[384,2048]{1,0:T(8,128)(2,1)S(1)}, u32[]{:S(2)}, u32[]{:S(2)}) collective-permute-start(bf16[384,2048]{1,0:T(8,128)(2,1)} %bitcast.85), channel_id=1, source_target_pairs={{0,16},{16,0},{1,17},{17,1},{2,18},{18,2},{3,19},{19,3},{4,20},{20... | collective-permute-start | bytes 4718600 | tf_op jit(solution)/shard_map/ppermute | solution.py:253
  3.7 17.1 %collective-permute-start.7 = (bf16[384,2048]{1,0:T(8,128)(2,1)}, bf16[384,2048]{1,0:T(8,128)(2,1)S(1)}, u32[]{:S(2)}, u32[]{:S(2)}) collective-permute-start(bf16[384,2048]{1,0:T(8,128)(2,1)} %bitcast.87), channel_id=1, source_target_pairs={{0,16},{16,0},{1,17},{17,1},{2,18},{18,2},{3,19},{19,3},{4,20},{20... | collective-permute-start | bytes 4718600 | tf_op jit(solution)/shard_map/ppermute | solution.py:253
  3.8 17.1 %collective-permute-start.8 = (bf16[384,2048]{1,0:T(8,128)(2,1)}, bf16[384,2048]{1,0:T(8,128)(2,1)S(1)}, u32[]{:S(2)}, u32[]{:S(2)}) collective-permute-start(bf16[384,2048]{1,0:T(8,128)(2,1)} %bitcast.89), channel_id=1, source_target_pairs={{0,16},{16,0},{1,17},{17,1},{2,18},{18,2},{3,19},{19,3},{4,20},{20... | collective-permute-start | bytes 4718600 | tf_op jit(solution)/shard_map/ppermute | solution.py:253
  4.2 16.6 %collective-permute-start.5 = (bf16[256,1024]{1,0:T(8,128)(2,1)S(1)}, bf16[256,1024]{1,0:T(8,128)(2,1)S(1)}, u32[]{:S(2)}, u32[]{:S(2)}) collective-permute-start(bf16[256,1024]{1,0:T(8,128)(2,1)S(1)} %pad_maximum_fusion.3.own), channel_id=1, source_target_pairs={{0,2},{1,3},{2,6},{3,7},{4,0},{5,1},{6,4},{7,5},{8,10},{9,11},{10,... | collective-permute-start | bytes 1572872 | tf_op jit(solution)/shard_map/ppermute | solution.py:265
  6.8 8.4 %collective-permute-start = (bf16[128,1024]{1,0:T(8,128)(2,1)S(1)}, bf16[128,1024]{1,0:T(8,128)(2,1)S(1)}, u32[]{:S(2)}, u32[]{:S(2)}) collective-permute-start(bf16[128,1024]{1,0:T(8,128)(2,1)S(1)} %multiply_convert_fusion), channel_id=1, source_target_pairs={{0,8},{8,0},{1,9},{9,1},{2,10},{10,2},{3,11},{11,3},{4,12},{12,4},... | collective-permute-start | bytes 786440 | tf_op jit(solution)/shard_map/ppermute | solution.py:250
  8.3 8.3 %collective-permute-start.2 = (bf16[128,1024]{1,0:T(8,128)(2,1)}, bf16[128,1024]{1,0:T(8,128)(2,1)S(1)}, u32[]{:S(2)}, u32[]{:S(2)}) collective-permute-start(bf16[128,1024]{1,0:T(8,128)(2,1)} %param.10), channel_id=1, source_target_pairs={{0,1},{1,0},{2,3},{3,2},{4,5},{5,4},{6,7},{7,6},{8,9},{9,8},{10,11... | collective-permute-start | bytes 786440 | tf_op jit(solution)/shard_map/ppermute | solution.py:256
  16.6 0.7 copy-start
  17.3 0.7 copy-start.2
  18.0 5.4 %copy-start.4 = (bf16[1,384,2048]{2,1,0:T(8,128)(2,1)S(1)}, bf16[1,384,2048]{2,1,0:T(8,128)(2,1)}, u32[]{:S(2)}) copy-start(bf16[1,384,2048]{2,1,0:T(8,128)(2,1)} %param.14) | copy-start | bytes 4718596
  18.1 15.0 %collective-permute-start.6 = (bf16[272,1024]{1,0:T(8,128)(2,1)S(1)}, bf16[272,1024]{1,0:T(8,128)(2,1)S(1)}, u32[]{:S(2)}, u32[]{:S(2)}) collective-permute-start(bf16[272,1024]{1,0:T(8,128)(2,1)S(1)} %shard_map.95.both), channel_id=1, source_target_pairs={{0,2},{1,3},{2,6},{3,7},{4,0},{5,1},{6,4},{7,5},{8,10},{9,11},{10,... | collective-permute-start | bytes 1671176 | tf_op jit(solution)/shard_map/ppermute | solution.py:265
  20.8 16.3 %collective-permute-start.3 = (bf16[272,1024]{1,0:T(8,128)(2,1)S(1)}, bf16[272,1024]{1,0:T(8,128)(2,1)S(1)}, u32[]{:S(2)}, u32[]{:S(2)}) collective-permute-start(bf16[272,1024]{1,0:T(8,128)(2,1)S(1)} %get-tuple-element.81.xs_ref), channel_id=1, source_target_pairs={{0,1},{1,0},{2,3},{3,2},{4,5},{5,4},{6,7},{7,6},{8,9},{9,8},{10,11... | collective-permute-start | bytes 1671176 | tf_op jit(solution)/shard_map/ppermute | solution.py:256
  22.4 14.7 %collective-permute-start.4 = (bf16[256,1024]{1,0:T(8,128)(2,1)S(1)}, bf16[256,1024]{1,0:T(8,128)(2,1)S(1)}, u32[]{:S(2)}, u32[]{:S(2)}) collective-permute-start(bf16[256,1024]{1,0:T(8,128)(2,1)S(1)} %get-tuple-element.82.gs_ref), channel_id=1, source_target_pairs={{0,8},{8,0},{1,9},{9,1},{2,10},{10,2},{3,11},{11,3},{4,12},{12,4},... | collective-permute-start | bytes 1572872 | tf_op jit(solution)/shard_map/ppermute | solution.py:250
  23.5 1.4 %copy-start.5 = (bf16[1,384,2048]{2,1,0:T(8,128)(2,1)S(1)}, bf16[1,384,2048]{2,1,0:T(8,128)(2,1)}, u32[]{:S(2)}) copy-start(bf16[1,384,2048]{2,1,0:T(8,128)(2,1)} %param.15) | copy-start | bytes 4718596
  33.2 25.3 %collective-permute-start.11 = (bf16[528,1024]{1,0:T(8,128)(2,1)S(1)}, bf16[528,1024]{1,0:T(8,128)(2,1)S(1)}, u32[]{:S(2)}, u32[]{:S(2)}) collective-permute-start(bf16[528,1024]{1,0:T(8,128)(2,1)S(1)} %get-tuple-element.91), channel_id=1, source_target_pairs={{0,2},{1,3},{2,6},{3,7},{4,0},{5,1},{6,4},{7,5},{8,10},{9,11},{10,... | collective-permute-start | bytes 3244040 | tf_op jit(solution)/shard_map/ppermute | solution.py:265
  34.5 27.8 %collective-permute-start.13 = (bf16[272,1024]{1,0:T(8,128)(2,1)S(1)}, bf16[272,1024]{1,0:T(8,128)(2,1)S(1)}, u32[]{:S(2)}, u32[]{:S(2)}) collective-permute-start(bf16[272,1024]{1,0:T(8,128)(2,1)S(1)} %get-tuple-element.92.xs_ref), channel_id=1, source_target_pairs={{0,1},{1,0},{2,3},{3,2},{4,5},{5,4},{6,7},{7,6},{8,9},{9,8},{10,11... | collective-permute-start | bytes 1671176 | tf_op jit(solution)/shard_map/ppermute | solution.py:256
  36.0 26.3 %collective-permute-start.14 = (bf16[256,1024]{1,0:T(8,128)(2,1)S(1)}, bf16[256,1024]{1,0:T(8,128)(2,1)S(1)}, u32[]{:S(2)}, u32[]{:S(2)}) collective-permute-start(bf16[256,1024]{1,0:T(8,128)(2,1)S(1)} %get-tuple-element.93.gs_ref), channel_id=1, source_target_pairs={{0,8},{8,0},{1,9},{9,1},{2,10},{10,2},{3,11},{11,3},{4,12},{12,4},... | collective-permute-start | bytes 1572872 | tf_op jit(solution)/shard_map/ppermute | solution.py:250
  42.2 10.2 %collective-permute-start.10 = (bf16[2,64,1024]{2,1,0:T(8,128)(2,1)S(1)}, bf16[2,64,1024]{2,1,0:T(8,128)(2,1)S(1)}, u32[]{:S(2)}, u32[]{:S(2)}) collective-permute-start(bf16[2,64,1024]{2,1,0:T(8,128)(2,1)S(1)} %get-tuple-element.101), channel_id=1, source_target_pairs={{0,1},{1,0},{2,3},{3,2},{4,5},{5,4},{6,7},{7,6},{8,9},{9,8},{10,11... | collective-permute-start | bytes 786440 | tf_op jit(solution)/shard_map/ppermute | solution.py:256
  42.8 10.1 %collective-permute-start.9 = (bf16[2,64,1024]{2,1,0:T(8,128)(2,1)S(1)}, bf16[2,64,1024]{2,1,0:T(8,128)(2,1)S(1)}, u32[]{:S(2)}, u32[]{:S(2)}) collective-permute-start(bf16[2,64,1024]{2,1,0:T(8,128)(2,1)S(1)} %get-tuple-element.100), channel_id=1, source_target_pairs={{0,8},{8,0},{1,9},{9,1},{2,10},{10,2},{3,11},{11,3},{4,12},{12,4},... | collective-permute-start | bytes 786440 | tf_op jit(solution)/shard_map/ppermute | solution.py:250
  58.5 24.3 %collective-permute-start.12 = (bf16[528,1024]{1,0:T(8,128)(2,1)S(1)}, bf16[528,1024]{1,0:T(8,128)(2,1)S(1)}, u32[]{:S(2)}, u32[]{:S(2)}) collective-permute-start(bf16[528,1024]{1,0:T(8,128)(2,1)S(1)} %collective-permute-done.11.um), channel_id=1, source_target_pairs={{0,2},{1,3},{2,6},{3,7},{4,0},{5,1},{6,4},{7,5},{8,10},{9,11},{10,... | collective-permute-start | bytes 3244040 | tf_op jit(solution)/shard_map/ppermute | solution.py:265
  59.2 17.9 %collective-permute-start.17 = (bf16[272,1024]{1,0:T(8,128)(2,1)S(1)}, bf16[272,1024]{1,0:T(8,128)(2,1)S(1)}, u32[]{:S(2)}, u32[]{:S(2)}) collective-permute-start(bf16[272,1024]{1,0:T(8,128)(2,1)S(1)} %get-tuple-element.108.xs_ref), channel_id=1, source_target_pairs={{0,1},{1,0},{2,3},{3,2},{4,5},{5,4},{6,7},{7,6},{8,9},{9,8},{10,11... | collective-permute-start | bytes 1671176 | tf_op jit(solution)/shard_map/ppermute | solution.py:256
  60.8 16.4 %collective-permute-start.18 = (bf16[256,1024]{1,0:T(8,128)(2,1)S(1)}, bf16[256,1024]{1,0:T(8,128)(2,1)S(1)}, u32[]{:S(2)}, u32[]{:S(2)}) collective-permute-start(bf16[256,1024]{1,0:T(8,128)(2,1)S(1)} %get-tuple-element.109.gs_ref), channel_id=1, source_target_pairs={{0,8},{8,0},{1,9},{9,1},{2,10},{10,2},{3,11},{11,3},{4,12},{12,4},... | collective-permute-start | bytes 1572872 | tf_op jit(solution)/shard_map/ppermute | solution.py:250
  67.4 9.7 %collective-permute-start.15 = (bf16[2,64,1024]{2,1,0:T(8,128)(2,1)S(1)}, bf16[2,64,1024]{2,1,0:T(8,128)(2,1)S(1)}, u32[]{:S(2)}, u32[]{:S(2)}) collective-permute-start(bf16[2,64,1024]{2,1,0:T(8,128)(2,1)S(1)} %get-tuple-element.104), channel_id=1, source_target_pairs={{0,8},{8,0},{1,9},{9,1},{2,10},{10,2},{3,11},{11,3},{4,12},{12,4},... | collective-permute-start | bytes 786440 | tf_op jit(solution)/shard_map/ppermute | solution.py:250
  68.0 9.1 %collective-permute-start.16 = (bf16[2,64,1024]{2,1,0:T(8,128)(2,1)S(1)}, bf16[2,64,1024]{2,1,0:T(8,128)(2,1)S(1)}, u32[]{:S(2)}, u32[]{:S(2)}) collective-permute-start(bf16[2,64,1024]{2,1,0:T(8,128)(2,1)S(1)} %get-tuple-element.106), channel_id=1, source_target_pairs={{0,1},{1,0},{2,3},{3,2},{4,5},{5,4},{6,7},{7,6},{8,9},{9,8},{10,11... | collective-permute-start | bytes 786440 | tf_op jit(solution)/shard_map/ppermute | solution.py:256
  82.9 16.9 %collective-permute-start.19 = (bf16[272,1024]{1,0:T(8,128)(2,1)S(1)}, bf16[272,1024]{1,0:T(8,128)(2,1)S(1)}, u32[]{:S(2)}, u32[]{:S(2)}) collective-permute-start(bf16[272,1024]{1,0:T(8,128)(2,1)S(1)} %get-tuple-element.113.xs_ref), channel_id=1, source_target_pairs={{0,1},{1,0},{2,3},{3,2},{4,5},{5,4},{6,7},{7,6},{8,9},{9,8},{10,11... | collective-permute-start | bytes 1671176 | tf_op jit(solution)/shard_map/ppermute | solution.py:256
  84.1 15.8 %collective-permute-start.20 = (bf16[256,1024]{1,0:T(8,128)(2,1)S(1)}, bf16[256,1024]{1,0:T(8,128)(2,1)S(1)}, u32[]{:S(2)}, u32[]{:S(2)}) collective-permute-start(bf16[256,1024]{1,0:T(8,128)(2,1)S(1)} %get-tuple-element.114.gs_ref), channel_id=1, source_target_pairs={{0,8},{8,0},{1,9},{9,1},{2,10},{10,2},{3,11},{11,3},{4,12},{12,4},... | collective-permute-start | bytes 1572872 | tf_op jit(solution)/shard_map/ppermute | solution.py:250
  85.7 14.1 %collective-permute-start.23 = (bf16[4,64,1024]{2,1,0:T(8,128)(2,1)S(1)}, bf16[4,64,1024]{2,1,0:T(8,128)(2,1)S(1)}, u32[]{:S(2)}, u32[]{:S(2)}) collective-permute-start(bf16[4,64,1024]{2,1,0:T(8,128)(2,1)S(1)} %pad_maximum_fusion.4), channel_id=1, source_target_pairs={{0,2},{1,3},{2,6},{3,7},{4,0},{5,1},{6,4},{7,5},{8,10},{9,11},{10,... | collective-permute-start | bytes 1572872 | tf_op jit(solution)/shard_map/ppermute | solution.py:265
  91.7 8.0 %collective-permute-start.21 = (bf16[2,64,1024]{2,1,0:T(8,128)(2,1)S(1)}, bf16[2,64,1024]{2,1,0:T(8,128)(2,1)S(1)}, u32[]{:S(2)}, u32[]{:S(2)}) collective-permute-start(bf16[2,64,1024]{2,1,0:T(8,128)(2,1)S(1)} %get-tuple-element.116), channel_id=1, source_target_pairs={{0,8},{8,0},{1,9},{9,1},{2,10},{10,2},{3,11},{11,3},{4,12},{12,4},... | collective-permute-start | bytes 786440 | tf_op jit(solution)/shard_map/ppermute | solution.py:250
  92.3 7.5 %collective-permute-start.22 = (bf16[2,64,1024]{2,1,0:T(8,128)(2,1)S(1)}, bf16[2,64,1024]{2,1,0:T(8,128)(2,1)S(1)}, u32[]{:S(2)}, u32[]{:S(2)}) collective-permute-start(bf16[2,64,1024]{2,1,0:T(8,128)(2,1)S(1)} %get-tuple-element.117), channel_id=1, source_target_pairs={{0,1},{1,0},{2,3},{3,2},{4,5},{5,4},{6,7},{7,6},{8,9},{9,8},{10,11... | collective-permute-start | bytes 786440 | tf_op jit(solution)/shard_map/ppermute | solution.py:256
  100.2 16.8 %collective-permute-start.27 = (bf16[4,64,1024]{2,1,0:T(8,128)(2,1)S(1)}, bf16[4,64,1024]{2,1,0:T(8,128)(2,1)S(1)}, u32[]{:S(2)}, u32[]{:S(2)}) collective-permute-start(bf16[4,64,1024]{2,1,0:T(8,128)(2,1)S(1)} %pad_maximum_fusion.5), channel_id=1, source_target_pairs={{0,2},{1,3},{2,6},{3,7},{4,0},{5,1},{6,4},{7,5},{8,10},{9,11},{10,... | collective-permute-start | bytes 1572872 | tf_op jit(solution)/shard_map/ppermute | solution.py:265
  107.6 23.5 %copy-start.1 = (s32[128,8]{0,1:T(8,128)S(1)}, s32[128,8]{0,1:T(8,128)}, u32[]{:S(2)}) copy-start(s32[128,8]{0,1:T(8,128)} %param.11) | copy-start | bytes 12292
  107.6 7.0 %collective-permute-start.24 = (bf16[2,64,1024]{2,1,0:T(8,128)(2,1)S(1)}, bf16[2,64,1024]{2,1,0:T(8,128)(2,1)S(1)}, u32[]{:S(2)}, u32[]{:S(2)}) collective-permute-start(bf16[2,64,1024]{2,1,0:T(8,128)(2,1)S(1)} %get-tuple-element.126), channel_id=1, source_target_pairs={{0,8},{8,0},{1,9},{9,1},{2,10},{10,2},{3,11},{11,3},{4,12},{12,4},... | collective-permute-start | bytes 786440 | tf_op jit(solution)/shard_map/ppermute | solution.py:250
  109.2 7.8 %collective-permute-start.25 = (bf16[2,64,1024]{2,1,0:T(8,128)(2,1)S(1)}, bf16[2,64,1024]{2,1,0:T(8,128)(2,1)S(1)}, u32[]{:S(2)}, u32[]{:S(2)}) collective-permute-start(bf16[2,64,1024]{2,1,0:T(8,128)(2,1)S(1)} %get-tuple-element.127), channel_id=1, source_target_pairs={{0,1},{1,0},{2,3},{3,2},{4,5},{5,4},{6,7},{7,6},{8,9},{9,8},{10,11... | collective-permute-start | bytes 786440 | tf_op jit(solution)/shard_map/ppermute | solution.py:256
  109.7 4.9 %collective-permute-start.26 = (f32[4,2,2,128]{3,1,2,0:T(2,128)S(1)}, f32[4,2,2,128]{3,1,2,0:T(2,128)S(1)}, u32[]{:S(2)}, u32[]{:S(2)}) collective-permute-start(f32[4,2,2,128]{3,1,2,0:T(2,128)S(1)} %constant_dynamic-update-slice_fusion), channel_id=1, source_target_pairs={{0,8},{8,0},{1,9},{9,1},{2,10},{10,2},{3,11},{11,3},{4,12},{12,4},... | collective-permute-start | bytes 24584 | tf_op jit(solution)/shard_map/ppermute | solution.py:250
  117.1 6.0 %collective-permute-start.28 = (bf16[64,1024]{1,0:T(8,128)(2,1)S(1)}, bf16[64,1024]{1,0:T(8,128)(2,1)S(1)}, u32[]{:S(2)}, u32[]{:S(2)}) collective-permute-start(bf16[64,1024]{1,0:T(8,128)(2,1)S(1)} %get-tuple-element.144), channel_id=1, source_target_pairs={{0,1},{1,0},{2,3},{3,2},{4,5},{5,4},{6,7},{7,6},{8,9},{9,8},{10,11... | collective-permute-start | bytes 393224 | tf_op jit(solution)/shard_map/ppermute | solution.py:256
  117.7 5.6 %collective-permute-start.29 = (bf16[64,1024]{1,0:T(8,128)(2,1)S(1)}, bf16[64,1024]{1,0:T(8,128)(2,1)S(1)}, u32[]{:S(2)}, u32[]{:S(2)}) collective-permute-start(bf16[64,1024]{1,0:T(8,128)(2,1)S(1)} %get-tuple-element.145), channel_id=1, source_target_pairs={{0,8},{8,0},{1,9},{9,1},{2,10},{10,2},{3,11},{11,3},{4,12},{12,4},... | collective-permute-start | bytes 393224 | tf_op jit(solution)/shard_map/ppermute | solution.py:250
  118.2 7.7 %collective-permute-start.33 = (f32[2,2,128]{2,0,1:T(2,128)S(1)}, f32[2,2,128]{2,0,1:T(2,128)S(1)}, u32[]{:S(2)}, u32[]{:S(2)}) collective-permute-start(f32[2,2,128]{2,0,1:T(2,128)S(1)} %get-tuple-element.154), channel_id=1, source_target_pairs={{0,4},{1,5},{2,0},{3,1},{4,6},{5,7},{6,2},{7,3},{8,12},{9,13},{10,... | collective-permute-start | bytes 6152 | tf_op jit(solution)/shard_map/ppermute | solution.py:265
  119.4 7.6 %collective-permute-start.34 = (f32[2,2,128]{2,0,1:T(2,128)S(1)}, f32[2,2,128]{2,0,1:T(2,128)S(1)}, u32[]{:S(2)}, u32[]{:S(2)}) collective-permute-start(f32[2,2,128]{2,0,1:T(2,128)S(1)} %get-tuple-element.153), channel_id=1, source_target_pairs={{0,6},{1,7},{2,4},{3,5},{4,2},{5,3},{6,0},{7,1},{8,14},{9,15},{10,... | collective-permute-start | bytes 6152 | tf_op jit(solution)/shard_map/ppermute | solution.py:265
  122.9 4.5 %collective-permute-start.35 = (f32[2,2,128]{2,0,1:T(2,128)S(1)}, f32[2,2,128]{2,0,1:T(2,128)S(1)}, u32[]{:S(2)}, u32[]{:S(2)}) collective-permute-start(f32[2,2,128]{2,0,1:T(2,128)S(1)} %get-tuple-element.152), channel_id=1, source_target_pairs={{0,2},{1,3},{2,6},{3,7},{4,0},{5,1},{6,4},{7,5},{8,10},{9,11},{10,... | collective-permute-start | bytes 6152 | tf_op jit(solution)/shard_map/ppermute | solution.py:265
  123.5 8.8 %collective-permute-start.31 = (bf16[128,1024]{1,0:T(8,128)(2,1)S(1)}, bf16[128,1024]{1,0:T(8,128)(2,1)S(1)}, u32[]{:S(2)}, u32[]{:S(2)}) collective-permute-start(bf16[128,1024]{1,0:T(8,128)(2,1)S(1)} %pad_maximum_fusion.6), channel_id=1, source_target_pairs={{0,2},{1,3},{2,6},{3,7},{4,0},{5,1},{6,4},{7,5},{8,10},{9,11},{10,... | collective-permute-start | bytes 786440 | tf_op jit(solution)/shard_map/ppermute | solution.py:265
  125.3 6.9 %collective-permute-start.32 = (bf16[64,1024]{1,0:T(8,128)(2,1)S(1)}, bf16[64,1024]{1,0:T(8,128)(2,1)S(1)}, u32[]{:S(2)}, u32[]{:S(2)}) collective-permute-start(bf16[64,1024]{1,0:T(8,128)(2,1)S(1)} %fusion.7), channel_id=1, source_target_pairs={{0,8},{8,0},{1,9},{9,1},{2,10},{10,2},{3,11},{11,3},{4,12},{12,4},... | collective-permute-start | bytes 393224 | tf_op jit(solution)/shard_map/ppermute | solution.py:250
  125.9 6.3 %collective-permute-start.30 = (bf16[64,1024]{1,0:T(8,128)(2,1)S(1)}, bf16[64,1024]{1,0:T(8,128)(2,1)S(1)}, u32[]{:S(2)}, u32[]{:S(2)}) collective-permute-start(bf16[64,1024]{1,0:T(8,128)(2,1)S(1)} %fusion.6), channel_id=1, source_target_pairs={{0,1},{1,0},{2,3},{3,2},{4,5},{5,4},{6,7},{7,6},{8,9},{9,8},{10,11... | collective-permute-start | bytes 393224 | tf_op jit(solution)/shard_map/ppermute | solution.py:256
  127.4 3.7 %collective-permute-start.36 = (f32[4,2,128]{2,1,0:T(2,128)S(1)}, f32[4,2,128]{2,1,0:T(2,128)S(1)}, u32[]{:S(2)}, u32[]{:S(2)}) collective-permute-start(f32[4,2,128]{2,1,0:T(2,128)S(1)} %get-tuple-element.150), channel_id=1, source_target_pairs={{0,1},{1,0},{2,3},{3,2},{4,5},{5,4},{6,7},{7,6},{8,9},{9,8},{10,11... | collective-permute-start | bytes 12296 | tf_op jit(solution)/shard_map/ppermute | solution.py:256

commit v4 on v3

--- a/solution.py
+++ b/solution.py
@@ -173,19 +173,24 @@
     )(info, xs, gs, v, n, wg, wu, wd)
 
 
-def stack_kernel(x_far, g_far, ids, gates, both):
+def picks_kernel(ids, gates, picks):
     f32 = jnp.float32
-    token_rows, width = x_far.shape
-    both[:token_rows] = x_far[...]
-    both[token_rows : 2 * token_rows] = g_far[...]
+    count, width = picks.shape
+    token_rows = ids.shape[1]
     high = gates[...].astype(jnp.bfloat16).astype(f32)
     parts = [ids[...].astype(f32), high, gates[...] - high]
     flat = [part[k : k + 1] for part in parts for k in range(part.shape[0])]
-    count = both.shape[0] - 2 * token_rows
     flat += [jnp.zeros((1, token_rows), f32)] * (count * width // token_rows - len(flat))
     per = width // token_rows
     rows = [jnp.concatenate(flat[row * per : (row + 1) * per], axis=1) for row in range(count)]
-    both[2 * token_rows :] = jnp.concatenate(rows, axis=0).astype(jnp.bfloat16)
+    picks[...] = jnp.concatenate(rows, axis=0).astype(jnp.bfloat16)
+
+
+def stack_kernel(x_far, g_far, picks, both):
+    token_rows = x_far.shape[0]
+    both[:token_rows] = x_far[...]
+    both[token_rows : 2 * token_rows] = g_far[...]
+    both[2 * token_rows :] = picks[...]
 
 
 def merge_kernel(own, both, xs, gs):
@@ -220,9 +225,8 @@
     gs[...] = um[xs.shape[0] :]
 
 
-def move_rows(kernel, rows, *values):
+def move_rows(kernel, rows, width, *values):
     vmem = pl.BlockSpec(memory_space=pltpu.VMEM)
-    width = values[0].shape[1]
     return pl.pallas_call(
         kernel,
         in_specs=[vmem] * len(values),
@@ -287,8 +291,10 @@
     near, x_other = over_z(own, 1), over_x(x)
     others = [over_core(w[0]) for w in after((w_gate, w_up, w_down), own)]
     g_other = over_y(after(out_grad, others[0]))
-    ids_t, gates_t = after((expert_ids.T, gates.T), x_other)
-    (both,) = move_rows(stack_kernel, (x_count,), x_other, g_other, ids_t, gates_t)
+    ids_t, gates_t = after((expert_ids.T, gates.T), others[0])
+    (picks,) = move_rows(picks_kernel, (pick_rows,), width, ids_t, gates_t)
+    picks, x_other = lax.optimization_barrier((picks, x_other))
+    (both,) = move_rows(stack_kernel, (x_count,), width, x_other, g_other, picks)
     both_near = over_z(both, 1)
     near = after(near, both)
     terms, shares, tokens, hops, outs = [[None] * ring for _ in range(5)]
@@ -297,12 +303,12 @@
         xs, gs = shares[step]
         tokens[step] = over_y(xs), over_x(gs)
 
-    shares[0] = move_rows(merge_kernel, (x_count, g_count), own, both)
+    shares[0] = move_rows(merge_kernel, (x_count, g_count), width, own, both)
     hop(0)
     others = after(others, near)
     wg, wu, wd = [jnp.concatenate([w[0], far], axis=0) for w, far in zip((w_gate, w_up, w_down), others)]
     near, both_near, wg, wu, wd = lax.optimization_barrier((near, both_near, wg, wu, wd))
-    um, *shares[1] = move_rows(join_kernel, (x_count + g_count, x_count, g_count), near, both_near)
+    um, *shares[1] = move_rows(join_kernel, (x_count + g_count, x_count, g_count), width, near, both_near)
 
     def expert(step):
         *outs, term = run_expert(tops, token_rows, info, *shares[step], *tokens[step], wg, wu, wd)
@@ -316,7 +322,7 @@
     moving = None
     for step in range(1, ring):
         if step > 1:
-            shares[step] = move_rows(split_kernel, (x_count, g_count), um)
+            shares[step] = move_rows(split_kernel, (x_count, g_count), width, um)
         hop(step)
         if step < ring - 1:
             following = over_z(um, 1)

time: 133 us -> 135 us (1.015)
  transfers between devices with their start and end apart: 37 -> 37, of which waited for: 16 -> 15; matrix products, arithmetic and copies ran while one was open for 1% -> 1% of each run, Pallas kernels for 17% -> 16%
where the time goes in v4:
time: 135 us
  waiting for transfers between devices  61 us (45%)
  starting transfers between devices  43 us (32%)
  Pallas kernels  22.2 us (16%)
  other arithmetic  5.28 us (4%)
  local copies, waits for them, and re-layouts  2.12 us (2%)
    ppermute x12, waiting for transfers between devices, over_x(): return lax.ppermute(value, 'tensor', [(0, 1), (1, 0)])  25.6 us
    pallas_call x4, Pallas kernels, run_expert(): pl.pallas_call(functools.partial(expert_kernel, tops), in_specs=[pl.Block...  20.7 us
    ppermute x10, waiting for transfers between devices, over_z(): lax.ppermute(value, 'expert', [(e, moved(e, shift)) for e in range(expert...  19.2 us
    ppermute x10, starting transfers between devices, over_z(): lax.ppermute(value, 'expert', [(e, moved(e, shift)) for e in range(expert...  16.7 us
    ppermute x12, waiting for transfers between devices, over_y(): return lax.ppermute(value, 'expert', [(e, e ^ 1) for e in range(experts)])  16.2 us
    ppermute x12, starting transfers between devices, over_x(): return lax.ppermute(value, 'tensor', [(0, 1), (1, 0)])  12.7 us
    ppermute x12, starting transfers between devices, over_y(): return lax.ppermute(value, 'expert', [(e, e ^ 1) for e in range(experts)])  12.6 us
  transfers between devices with their start and end apart: 37, of which 15 were waited for; matrix products, arithmetic and copies ran while one was open for 1% of the time, Pallas kernels for 16%

profile of v4, /device:TPU:0, one launch (start us, length us, event | category | flops | bytes accessed | tf_op | source)
XLA Modules:
  0.0 134.7 jit_solution(7748508422842553022)
XLA Ops:
  0.9 1.2 multiply_convert_fusion
  2.2 1.0 pad_maximum_fusion.3.own
  4.2 2.7 %collective-permute-start.5 = (bf16[256,1024]{1,0:T(8,128)(2,1)S(1)}, bf16[256,1024]{1,0:T(8,128)(2,1)S(1)}, u32[]{:S(2)}, u32[]{:S(2)}) collective-permute-start(bf16[256,1024]{1,0:T(8,128)(2,1)S(1)} %pad_maximum_fusion.3.own), channel_id=1, source_target_pairs={{0,2},{1,3},{2,6},{3,7},{4,0},{5,1},{6,4},{7,5},{8,10},{9,11},{10,... | collective-permute-start | bytes 1572872 | tf_op jit(solution)/shard_map/ppermute | solution.py:269
  6.8 1.5 %collective-permute-start.1 = (bf16[128,1024]{1,0:T(8,128)(2,1)S(1)}, bf16[128,1024]{1,0:T(8,128)(2,1)S(1)}, u32[]{:S(2)}, u32[]{:S(2)}) collective-permute-start(bf16[128,1024]{1,0:T(8,128)(2,1)S(1)} %multiply_convert_fusion), channel_id=1, source_target_pairs={{0,8},{8,0},{1,9},{9,1},{2,10},{10,2},{3,11},{11,3},{4,12},{12,4},... | collective-permute-start | bytes 786440 | tf_op jit(solution)/shard_map/ppermute | solution.py:254
  8.3 1.5 %collective-permute-start.2 = (bf16[128,1024]{1,0:T(8,128)(2,1)}, bf16[128,1024]{1,0:T(8,128)(2,1)S(1)}, u32[]{:S(2)}, u32[]{:S(2)}) collective-permute-start(bf16[128,1024]{1,0:T(8,128)(2,1)} %param.10), channel_id=1, source_target_pairs={{0,1},{1,0},{2,3},{3,2},{4,5},{5,4},{6,7},{7,6},{8,9},{9,8},{10,11... | collective-permute-start | bytes 786440 | tf_op jit(solution)/shard_map/ppermute | solution.py:260
  9.9 0.7 copy-done
  10.5 0.7 copy-done.2
  11.3 4.0 %collective-permute-done.1.x_far = bf16[128,1024]{1,0:T(8,128)(2,1)S(1)} collective-permute-done((bf16[128,1024]{1,0:T(8,128)(2,1)S(1)}, bf16[128,1024]{1,0:T(8,128)(2,1)S(1)}, u32[]{:S(2)}, u32[]{:S(2)}) %collective-permute-start.1) | collective-permute-done | bytes 262176 | tf_op jit(solution)/shard_map/ppermute | solution.py:254
  15.2 1.4 %collective-permute-done.2.g_far = bf16[128,1024]{1,0:T(8,128)(2,1)S(1)} collective-permute-done((bf16[128,1024]{1,0:T(8,128)(2,1)}, bf16[128,1024]{1,0:T(8,128)(2,1)S(1)}, u32[]{:S(2)}, u32[]{:S(2)}) %collective-permute-start.2) | collective-permute-done | bytes 262176 | tf_op jit(solution)/shard_map/ppermute | solution.py:260
  16.7 2.6 %collective-permute-start.6 = (bf16[272,1024]{1,0:T(8,128)(2,1)S(1)}, bf16[272,1024]{1,0:T(8,128)(2,1)S(1)}, u32[]{:S(2)}, u32[]{:S(2)}) collective-permute-start(bf16[272,1024]{1,0:T(8,128)(2,1)S(1)} %shard_map.96.both), channel_id=1, source_target_pairs={{0,2},{1,3},{2,6},{3,7},{4,0},{5,1},{6,4},{7,5},{8,10},{9,11},{10,... | collective-permute-start | bytes 1671176 | tf_op jit(solution)/shard_map/ppermute | solution.py:269
  19.4 1.2 collective-permute-done.5.own
  20.6 1.8 %collective-permute-start.3 = (bf16[272,1024]{1,0:T(8,128)(2,1)S(1)}, bf16[272,1024]{1,0:T(8,128)(2,1)S(1)}, u32[]{:S(2)}, u32[]{:S(2)}) collective-permute-start(bf16[272,1024]{1,0:T(8,128)(2,1)S(1)} %get-tuple-element.85.xs_ref), channel_id=1, source_target_pairs={{0,1},{1,0},{2,3},{3,2},{4,5},{5,4},{6,7},{7,6},{8,9},{9,8},{10,11... | collective-permute-start | bytes 1671176 | tf_op jit(solution)/shard_map/ppermute | solution.py:260
  22.4 1.5 %collective-permute-start.4 = (bf16[256,1024]{1,0:T(8,128)(2,1)S(1)}, bf16[256,1024]{1,0:T(8,128)(2,1)S(1)}, u32[]{:S(2)}, u32[]{:S(2)}) collective-permute-start(bf16[256,1024]{1,0:T(8,128)(2,1)S(1)} %get-tuple-element.86.gs_ref), channel_id=1, source_target_pairs={{0,8},{8,0},{1,9},{9,1},{2,10},{10,2},{3,11},{11,3},{4,12},{12,4},... | collective-permute-start | bytes 1572872 | tf_op jit(solution)/shard_map/ppermute | solution.py:254
  23.9 0.8 pad_maximum_fusion
  25.7 6.6 %collective-permute-done.6.both = bf16[272,1024]{1,0:T(8,128)(2,1)S(1)} collective-permute-done((bf16[272,1024]{1,0:T(8,128)(2,1)S(1)}, bf16[272,1024]{1,0:T(8,128)(2,1)S(1)}, u32[]{:S(2)}, u32[]{:S(2)}) %collective-permute-start.6) | collective-permute-done | bytes 557088 | tf_op jit(solution)/shard_map/ppermute | solution.py:269
  32.5 0.9 collective-permute-start.11
  33.4 1.5 %collective-permute-start.13 = (bf16[272,1024]{1,0:T(8,128)(2,1)S(1)}, bf16[272,1024]{1,0:T(8,128)(2,1)S(1)}, u32[]{:S(2)}, u32[]{:S(2)}) collective-permute-start(bf16[272,1024]{1,0:T(8,128)(2,1)S(1)} %get-tuple-element.96.xs_ref), channel_id=1, source_target_pairs={{0,1},{1,0},{2,3},{3,2},{4,5},{5,4},{6,7},{7,6},{8,9},{9,8},{10,11... | collective-permute-start | bytes 1671176 | tf_op jit(solution)/shard_map/ppermute | solution.py:260
  34.9 1.5 %collective-permute-start.14 = (bf16[256,1024]{1,0:T(8,128)(2,1)S(1)}, bf16[256,1024]{1,0:T(8,128)(2,1)S(1)}, u32[]{:S(2)}, u32[]{:S(2)}) collective-permute-start(bf16[256,1024]{1,0:T(8,128)(2,1)S(1)} %get-tuple-element.97.gs_ref), channel_id=1, source_target_pairs={{0,8},{8,0},{1,9},{9,1},{2,10},{10,2},{3,11},{11,3},{4,12},{12,4},... | collective-permute-start | bytes 1572872 | tf_op jit(solution)/shard_map/ppermute | solution.py:254
  36.4 5.2 %shard_map.99 = (bf16[2,64,1024]{2,1,0:T(8,128)(2,1)S(1)}, bf16[2,64,1024]{2,1,0:T(8,128)(2,1)S(1)}, bf16[2,64,1024]{2,1,0:T(8,128)(2,1)S(1)}, bf16[2,64,1024]{2,1,0:T(8,128)(2,1)S(1)}, f32[2,8,256]{2,1,0:T(8,128)S(1)}) custom-call(s32[3]{0:T(128)S(1)} %pad_add_fusion.info_ref, bf16[272,1024]{1,0:T(8,128)(2,1)S(1)} %get-tuple-element.85.xs_ref, ...), custom_call_target="tpu_custom_call" | custom-call | flops 4026531840 | bytes 12582912 | tf_op jit(solution)/shard_map/pallas_call | solution.py:162
  42.1 0.8 collective-permute-start.9
  42.9 9.4 %collective-permute-done.10 = bf16[2,64,1024]{2,1,0:T(8,128)(2,1)S(1)} collective-permute-done((bf16[2,64,1024]{2,1,0:T(8,128)(2,1)S(1)}, bf16[2,64,1024]{2,1,0:T(8,128)(2,1)S(1)}, u32[]{:S(2)}, u32[]{:S(2)}) %collective-permute-start.10) | collective-permute-done | bytes 262176 | tf_op jit(solution)/shard_map/ppermute | solution.py:260
  52.8 5.5 %collective-permute-done.11.um = bf16[528,1024]{1,0:T(8,128)(2,1)S(1)} collective-permute-done((bf16[528,1024]{1,0:T(8,128)(2,1)S(1)}, bf16[528,1024]{1,0:T(8,128)(2,1)S(1)}, u32[]{:S(2)}, u32[]{:S(2)}) %collective-permute-start.11) | collective-permute-done | bytes 1081376 | tf_op jit(solution)/shard_map/ppermute | solution.py:269
  58.5 0.8 collective-permute-start.12
  59.2 1.5 %collective-permute-start.17 = (bf16[272,1024]{1,0:T(8,128)(2,1)S(1)}, bf16[272,1024]{1,0:T(8,128)(2,1)S(1)}, u32[]{:S(2)}, u32[]{:S(2)}) collective-permute-start(bf16[272,1024]{1,0:T(8,128)(2,1)S(1)} %get-tuple-element.112.xs_ref), channel_id=1, source_target_pairs={{0,1},{1,0},{2,3},{3,2},{4,5},{5,4},{6,7},{7,6},{8,9},{9,8},{10,11... | collective-permute-start | bytes 1671176 | tf_op jit(solution)/shard_map/ppermute | solution.py:260
  60.7 1.5 %collective-permute-start.18 = (bf16[256,1024]{1,0:T(8,128)(2,1)S(1)}, bf16[256,1024]{1,0:T(8,128)(2,1)S(1)}, u32[]{:S(2)}, u32[]{:S(2)}) collective-permute-start(bf16[256,1024]{1,0:T(8,128)(2,1)S(1)} %get-tuple-element.113.gs_ref), channel_id=1, source_target_pairs={{0,8},{8,0},{1,9},{9,1},{2,10},{10,2},{3,11},{11,3},{4,12},{12,4},... | collective-permute-start | bytes 1572872 | tf_op jit(solution)/shard_map/ppermute | solution.py:254
  62.2 5.2 %shard_map.100 = (bf16[2,64,1024]{2,1,0:T(8,128)(2,1)S(1)}, bf16[2,64,1024]{2,1,0:T(8,128)(2,1)S(1)}, bf16[2,64,1024]{2,1,0:T(8,128)(2,1)S(1)}, bf16[2,64,1024]{2,1,0:T(8,128)(2,1)S(1)}, f32[2,8,256]{2,1,0:T(8,128)S(1)}) custom-call(s32[3]{0:T(128)S(1)} %pad_add_fusion.info_ref, bf16[272,1024]{1,0:T(8,128)(2,1)S(1)} %get-tuple-element.96.xs_ref, ...), custom_call_target="tpu_custom_call" | custom-call | flops 4026531840 | bytes 12582912 | tf_op jit(solution)/shard_map/pallas_call | solution.py:162
  67.4 0.6 collective-permute-start.15
  68.5 9.2 %collective-permute-done.15 = bf16[2,64,1024]{2,1,0:T(8,128)(2,1)S(1)} collective-permute-done((bf16[2,64,1024]{2,1,0:T(8,128)(2,1)S(1)}, bf16[2,64,1024]{2,1,0:T(8,128)(2,1)S(1)}, u32[]{:S(2)}, u32[]{:S(2)}) %collective-permute-start.15) | collective-permute-done | bytes 262176 | tf_op jit(solution)/shard_map/ppermute | solution.py:254
  78.0 5.5 %collective-permute-done.12.um = bf16[528,1024]{1,0:T(8,128)(2,1)S(1)} collective-permute-done((bf16[528,1024]{1,0:T(8,128)(2,1)S(1)}, bf16[528,1024]{1,0:T(8,128)(2,1)S(1)}, u32[]{:S(2)}, u32[]{:S(2)}) %collective-permute-start.12) | collective-permute-done | bytes 1081376 | tf_op jit(solution)/shard_map/ppermute | solution.py:269
  83.5 1.4 %collective-permute-start.19 = (bf16[272,1024]{1,0:T(8,128)(2,1)S(1)}, bf16[272,1024]{1,0:T(8,128)(2,1)S(1)}, u32[]{:S(2)}, u32[]{:S(2)}) collective-permute-start(bf16[272,1024]{1,0:T(8,128)(2,1)S(1)} %get-tuple-element.117.xs_ref), channel_id=1, source_target_pairs={{0,1},{1,0},{2,3},{3,2},{4,5},{5,4},{6,7},{7,6},{8,9},{9,8},{10,11... | collective-permute-start | bytes 1671176 | tf_op jit(solution)/shard_map/ppermute | solution.py:260
  84.9 1.5 %collective-permute-start.20 = (bf16[256,1024]{1,0:T(8,128)(2,1)S(1)}, bf16[256,1024]{1,0:T(8,128)(2,1)S(1)}, u32[]{:S(2)}, u32[]{:S(2)}) collective-permute-start(bf16[256,1024]{1,0:T(8,128)(2,1)S(1)} %get-tuple-element.118.gs_ref), channel_id=1, source_target_pairs={{0,8},{8,0},{1,9},{9,1},{2,10},{10,2},{3,11},{11,3},{4,12},{12,4},... | collective-permute-start | bytes 1572872 | tf_op jit(solution)/shard_map/ppermute | solution.py:254
  86.4 0.8 collective-permute-start.23
  87.2 5.2 %shard_map.103 = (bf16[2,64,1024]{2,1,0:T(8,128)(2,1)S(1)}, bf16[2,64,1024]{2,1,0:T(8,128)(2,1)S(1)}, bf16[2,64,1024]{2,1,0:T(8,128)(2,1)S(1)}, bf16[2,64,1024]{2,1,0:T(8,128)(2,1)S(1)}, f32[2,8,256]{2,1,0:T(8,128)S(1)}) custom-call(s32[3]{0:T(128)S(1)} %pad_add_fusion.info_ref, bf16[272,1024]{1,0:T(8,128)(2,1)S(1)} %get-tuple-element.112.xs_ref, ...), custom_call_target="tpu_custom_call" | custom-call | flops 4026531840 | bytes 12582912 | tf_op jit(solution)/shard_map/pallas_call | solution.py:162
  92.4 0.6 collective-permute-start.21
  93.5 7.8 %collective-permute-done.21 = bf16[2,64,1024]{2,1,0:T(8,128)(2,1)S(1)} collective-permute-done((bf16[2,64,1024]{2,1,0:T(8,128)(2,1)S(1)}, bf16[2,64,1024]{2,1,0:T(8,128)(2,1)S(1)}, u32[]{:S(2)}, u32[]{:S(2)}) %collective-permute-start.21) | collective-permute-done | bytes 262176 | tf_op jit(solution)/shard_map/ppermute | solution.py:254
  101.7 1.5 %collective-permute-start.27 = (bf16[4,64,1024]{2,1,0:T(8,128)(2,1)S(1)}, bf16[4,64,1024]{2,1,0:T(8,128)(2,1)S(1)}, u32[]{:S(2)}, u32[]{:S(2)}) collective-permute-start(bf16[4,64,1024]{2,1,0:T(8,128)(2,1)S(1)} %pad_maximum_fusion.5), channel_id=1, source_target_pairs={{0,2},{1,3},{2,6},{3,7},{4,0},{5,1},{6,4},{7,5},{8,10},{9,11},{10,... | collective-permute-start | bytes 1572872 | tf_op jit(solution)/shard_map/ppermute | solution.py:269
  103.1 5.2 %shard_map.104 = (bf16[2,64,1024]{2,1,0:T(8,128)(2,1)S(1)}, bf16[2,64,1024]{2,1,0:T(8,128)(2,1)S(1)}, bf16[2,64,1024]{2,1,0:T(8,128)(2,1)S(1)}, bf16[2,64,1024]{2,1,0:T(8,128)(2,1)S(1)}, f32[2,8,256]{2,1,0:T(8,128)S(1)}) custom-call(s32[3]{0:T(128)S(1)} %pad_add_fusion.info_ref, bf16[272,1024]{1,0:T(8,128)(2,1)S(1)} %get-tuple-element.117.xs_ref, ...), custom_call_target="tpu_custom_call" | custom-call | flops 4026531840 | bytes 12582912 | tf_op jit(solution)/shard_map/pallas_call | solution.py:162
  108.3 1.6 %collective-permute-start.24 = (bf16[2,64,1024]{2,1,0:T(8,128)(2,1)S(1)}, bf16[2,64,1024]{2,1,0:T(8,128)(2,1)S(1)}, u32[]{:S(2)}, u32[]{:S(2)}) collective-permute-start(bf16[2,64,1024]{2,1,0:T(8,128)(2,1)S(1)} %get-tuple-element.130), channel_id=1, source_target_pairs={{0,8},{8,0},{1,9},{9,1},{2,10},{10,2},{3,11},{11,3},{4,12},{12,4},... | collective-permute-start | bytes 786440 | tf_op jit(solution)/shard_map/ppermute | solution.py:254
  111.0 3.8 %collective-permute-done.26 = f32[4,2,2,128]{3,1,2,0:T(2,128)S(1)} collective-permute-done((f32[4,2,2,128]{3,1,2,0:T(2,128)S(1)}, f32[4,2,2,128]{3,1,2,0:T(2,128)S(1)}, u32[]{:S(2)}, u32[]{:S(2)}) %collective-permute-start.26) | collective-permute-done | bytes 8224 | tf_op jit(solution)/shard_map/ppermute | solution.py:254
  114.9 2.8 %collective-permute-done.25 = bf16[2,64,1024]{2,1,0:T(8,128)(2,1)S(1)} collective-permute-done((bf16[2,64,1024]{2,1,0:T(8,128)(2,1)S(1)}, bf16[2,64,1024]{2,1,0:T(8,128)(2,1)S(1)}, u32[]{:S(2)}, u32[]{:S(2)}) %collective-permute-start.25) | collective-permute-done | bytes 262176 | tf_op jit(solution)/shard_map/ppermute | solution.py:260
  118.9 2.0 %collective-permute-start.33 = (f32[2,2,128]{2,0,1:T(2,128)S(1)}, f32[2,2,128]{2,0,1:T(2,128)S(1)}, u32[]{:S(2)}, u32[]{:S(2)}) collective-permute-start(f32[2,2,128]{2,0,1:T(2,128)S(1)} %get-tuple-element.158), channel_id=1, source_target_pairs={{0,4},{1,5},{2,0},{3,1},{4,6},{5,7},{6,2},{7,3},{8,12},{9,13},{10,... | collective-permute-start | bytes 6152 | tf_op jit(solution)/shard_map/ppermute | solution.py:269
  120.9 3.6 %collective-permute-start.34 = (f32[2,2,128]{2,0,1:T(2,128)S(1)}, f32[2,2,128]{2,0,1:T(2,128)S(1)}, u32[]{:S(2)}, u32[]{:S(2)}) collective-permute-start(f32[2,2,128]{2,0,1:T(2,128)S(1)} %get-tuple-element.157), channel_id=1, source_target_pairs={{0,6},{1,7},{2,4},{3,5},{4,2},{5,3},{6,0},{7,1},{8,14},{9,15},{10,... | collective-permute-start | bytes 6152 | tf_op jit(solution)/shard_map/ppermute | solution.py:269
  124.9 1.9 %collective-permute-start.31 = (bf16[128,1024]{1,0:T(8,128)(2,1)S(1)}, bf16[128,1024]{1,0:T(8,128)(2,1)S(1)}, u32[]{:S(2)}, u32[]{:S(2)}) collective-permute-start(bf16[128,1024]{1,0:T(8,128)(2,1)S(1)} %pad_maximum_fusion.6), channel_id=1, source_target_pairs={{0,2},{1,3},{2,6},{3,7},{4,0},{5,1},{6,4},{7,5},{8,10},{9,11},{10,... | collective-permute-start | bytes 786440 | tf_op jit(solution)/shard_map/ppermute | solution.py:269
  127.5 1.1 collective-permute-start.30
  129.0 1.1 collective-permute-start.36
  130.1 2.5 %collective-permute-done.36.refs_1_ = f32[4,2,128]{2,1,0:T(2,128)S(1)} collective-permute-done((f32[4,2,128]{2,1,0:T(2,128)S(1)}, f32[4,2,128]{2,1,0:T(2,128)S(1)}, u32[]{:S(2)}, u32[]{:S(2)}) %collective-permute-start.36) | collective-permute-done | bytes 4128 | tf_op jit(solution)/shard_map/ppermute | solution.py:260
  132.6 1.2 shard_map.105
  134.0 0.7 pad_maximum_fusion.7
  (79 shorter events, 9.3 us)
Async XLA Ops:
  0.6 23.3 %copy-start.3 = (bf16[1,384,2048]{2,1,0:T(8,128)(2,1)S(1)}, bf16[1,384,2048]{2,1,0:T(8,128)(2,1)}, u32[]{:S(2)}) copy-start(bf16[1,384,2048]{2,1,0:T(8,128)(2,1)} %param.13) | copy-start | bytes 4718596
  3.2 5.2 %collective-permute-start = (bf16[384,2048]{1,0:T(8,128)(2,1)}, bf16[384,2048]{1,0:T(8,128)(2,1)S(1)}, u32[]{:S(2)}, u32[]{:S(2)}) collective-permute-start(bf16[384,2048]{1,0:T(8,128)(2,1)} %bitcast.85), channel_id=1, source_target_pairs={{0,16},{16,0},{1,17},{17,1},{2,18},{18,2},{3,19},{19,3},{4,20},{20... | collective-permute-start | bytes 4718600 | tf_op jit(solution)/shard_map/ppermute | solution.py:257
  3.7 17.0 %collective-permute-start.7 = (bf16[384,2048]{1,0:T(8,128)(2,1)}, bf16[384,2048]{1,0:T(8,128)(2,1)S(1)}, u32[]{:S(2)}, u32[]{:S(2)}) collective-permute-start(bf16[384,2048]{1,0:T(8,128)(2,1)} %bitcast.87), channel_id=1, source_target_pairs={{0,16},{16,0},{1,17},{17,1},{2,18},{18,2},{3,19},{19,3},{4,20},{20... | collective-permute-start | bytes 4718600 | tf_op jit(solution)/shard_map/ppermute | solution.py:257
  3.8 16.9 %collective-permute-start.8 = (bf16[384,2048]{1,0:T(8,128)(2,1)}, bf16[384,2048]{1,0:T(8,128)(2,1)S(1)}, u32[]{:S(2)}, u32[]{:S(2)}) collective-permute-start(bf16[384,2048]{1,0:T(8,128)(2,1)} %bitcast.89), channel_id=1, source_target_pairs={{0,16},{16,0},{1,17},{17,1},{2,18},{18,2},{3,19},{19,3},{4,20},{20... | collective-permute-start | bytes 4718600 | tf_op jit(solution)/shard_map/ppermute | solution.py:257
  4.2 16.4 %collective-permute-start.5 = (bf16[256,1024]{1,0:T(8,128)(2,1)S(1)}, bf16[256,1024]{1,0:T(8,128)(2,1)S(1)}, u32[]{:S(2)}, u32[]{:S(2)}) collective-permute-start(bf16[256,1024]{1,0:T(8,128)(2,1)S(1)} %pad_maximum_fusion.3.own), channel_id=1, source_target_pairs={{0,2},{1,3},{2,6},{3,7},{4,0},{5,1},{6,4},{7,5},{8,10},{9,11},{10,... | collective-permute-start | bytes 1572872 | tf_op jit(solution)/shard_map/ppermute | solution.py:269
  6.8 8.4 %collective-permute-start.1 = (bf16[128,1024]{1,0:T(8,128)(2,1)S(1)}, bf16[128,1024]{1,0:T(8,128)(2,1)S(1)}, u32[]{:S(2)}, u32[]{:S(2)}) collective-permute-start(bf16[128,1024]{1,0:T(8,128)(2,1)S(1)} %multiply_convert_fusion), channel_id=1, source_target_pairs={{0,8},{8,0},{1,9},{9,1},{2,10},{10,2},{3,11},{11,3},{4,12},{12,4},... | collective-permute-start | bytes 786440 | tf_op jit(solution)/shard_map/ppermute | solution.py:254
  8.3 8.3 %collective-permute-start.2 = (bf16[128,1024]{1,0:T(8,128)(2,1)}, bf16[128,1024]{1,0:T(8,128)(2,1)S(1)}, u32[]{:S(2)}, u32[]{:S(2)}) collective-permute-start(bf16[128,1024]{1,0:T(8,128)(2,1)} %param.10), channel_id=1, source_target_pairs={{0,1},{1,0},{2,3},{3,2},{4,5},{5,4},{6,7},{7,6},{8,9},{9,8},{10,11... | collective-permute-start | bytes 786440 | tf_op jit(solution)/shard_map/ppermute | solution.py:260
  9.9 0.7 copy-start
  10.5 0.7 copy-start.2
  11.2 12.7 %copy-start.4 = (bf16[1,384,2048]{2,1,0:T(8,128)(2,1)S(1)}, bf16[1,384,2048]{2,1,0:T(8,128)(2,1)}, u32[]{:S(2)}) copy-start(bf16[1,384,2048]{2,1,0:T(8,128)(2,1)} %param.14) | copy-start | bytes 4718596
  16.7 15.6 %collective-permute-start.6 = (bf16[272,1024]{1,0:T(8,128)(2,1)S(1)}, bf16[272,1024]{1,0:T(8,128)(2,1)S(1)}, u32[]{:S(2)}, u32[]{:S(2)}) collective-permute-start(bf16[272,1024]{1,0:T(8,128)(2,1)S(1)} %shard_map.96.both), channel_id=1, source_target_pairs={{0,2},{1,3},{2,6},{3,7},{4,0},{5,1},{6,4},{7,5},{8,10},{9,11},{10,... | collective-permute-start | bytes 1671176 | tf_op jit(solution)/shard_map/ppermute | solution.py:269
  20.6 15.7 %collective-permute-start.3 = (bf16[272,1024]{1,0:T(8,128)(2,1)S(1)}, bf16[272,1024]{1,0:T(8,128)(2,1)S(1)}, u32[]{:S(2)}, u32[]{:S(2)}) collective-permute-start(bf16[272,1024]{1,0:T(8,128)(2,1)S(1)} %get-tuple-element.85.xs_ref), channel_id=1, source_target_pairs={{0,1},{1,0},{2,3},{3,2},{4,5},{5,4},{6,7},{7,6},{8,9},{9,8},{10,11... | collective-permute-start | bytes 1671176 | tf_op jit(solution)/shard_map/ppermute | solution.py:260
  22.4 14.0 %collective-permute-start.4 = (bf16[256,1024]{1,0:T(8,128)(2,1)S(1)}, bf16[256,1024]{1,0:T(8,128)(2,1)S(1)}, u32[]{:S(2)}, u32[]{:S(2)}) collective-permute-start(bf16[256,1024]{1,0:T(8,128)(2,1)S(1)} %get-tuple-element.86.gs_ref), channel_id=1, source_target_pairs={{0,8},{8,0},{1,9},{9,1},{2,10},{10,2},{3,11},{11,3},{4,12},{12,4},... | collective-permute-start | bytes 1572872 | tf_op jit(solution)/shard_map/ppermute | solution.py:254
  23.9 1.4 %copy-start.5 = (bf16[1,384,2048]{2,1,0:T(8,128)(2,1)S(1)}, bf16[1,384,2048]{2,1,0:T(8,128)(2,1)}, u32[]{:S(2)}) copy-start(bf16[1,384,2048]{2,1,0:T(8,128)(2,1)} %param.15) | copy-start | bytes 4718596
  32.5 25.9 %collective-permute-start.11 = (bf16[528,1024]{1,0:T(8,128)(2,1)S(1)}, bf16[528,1024]{1,0:T(8,128)(2,1)S(1)}, u32[]{:S(2)}, u32[]{:S(2)}) collective-permute-start(bf16[528,1024]{1,0:T(8,128)(2,1)S(1)} %get-tuple-element.95), channel_id=1, source_target_pairs={{0,2},{1,3},{2,6},{3,7},{4,0},{5,1},{6,4},{7,5},{8,10},{9,11},{10,... | collective-permute-start | bytes 3244040 | tf_op jit(solution)/shard_map/ppermute | solution.py:269
  33.4 28.9 %collective-permute-start.13 = (bf16[272,1024]{1,0:T(8,128)(2,1)S(1)}, bf16[272,1024]{1,0:T(8,128)(2,1)S(1)}, u32[]{:S(2)}, u32[]{:S(2)}) collective-permute-start(bf16[272,1024]{1,0:T(8,128)(2,1)S(1)} %get-tuple-element.96.xs_ref), channel_id=1, source_target_pairs={{0,1},{1,0},{2,3},{3,2},{4,5},{5,4},{6,7},{7,6},{8,9},{9,8},{10,11... | collective-permute-start | bytes 1671176 | tf_op jit(solution)/shard_map/ppermute | solution.py:260
  34.9 27.4 %collective-permute-start.14 = (bf16[256,1024]{1,0:T(8,128)(2,1)S(1)}, bf16[256,1024]{1,0:T(8,128)(2,1)S(1)}, u32[]{:S(2)}, u32[]{:S(2)}) collective-permute-start(bf16[256,1024]{1,0:T(8,128)(2,1)S(1)} %get-tuple-element.97.gs_ref), channel_id=1, source_target_pairs={{0,8},{8,0},{1,9},{9,1},{2,10},{10,2},{3,11},{11,3},{4,12},{12,4},... | collective-permute-start | bytes 1572872 | tf_op jit(solution)/shard_map/ppermute | solution.py:254
  41.5 10.8 %collective-permute-start.10 = (bf16[2,64,1024]{2,1,0:T(8,128)(2,1)S(1)}, bf16[2,64,1024]{2,1,0:T(8,128)(2,1)S(1)}, u32[]{:S(2)}, u32[]{:S(2)}) collective-permute-start(bf16[2,64,1024]{2,1,0:T(8,128)(2,1)S(1)} %get-tuple-element.105), channel_id=1, source_target_pairs={{0,1},{1,0},{2,3},{3,2},{4,5},{5,4},{6,7},{7,6},{8,9},{9,8},{10,11... | collective-permute-start | bytes 786440 | tf_op jit(solution)/shard_map/ppermute | solution.py:260
  42.1 10.7 %collective-permute-start.9 = (bf16[2,64,1024]{2,1,0:T(8,128)(2,1)S(1)}, bf16[2,64,1024]{2,1,0:T(8,128)(2,1)S(1)}, u32[]{:S(2)}, u32[]{:S(2)}) collective-permute-start(bf16[2,64,1024]{2,1,0:T(8,128)(2,1)S(1)} %get-tuple-element.104), channel_id=1, source_target_pairs={{0,8},{8,0},{1,9},{9,1},{2,10},{10,2},{3,11},{11,3},{4,12},{12,4},... | collective-permute-start | bytes 786440 | tf_op jit(solution)/shard_map/ppermute | solution.py:254
  58.5 25.0 %collective-permute-start.12 = (bf16[528,1024]{1,0:T(8,128)(2,1)S(1)}, bf16[528,1024]{1,0:T(8,128)(2,1)S(1)}, u32[]{:S(2)}, u32[]{:S(2)}) collective-permute-start(bf16[528,1024]{1,0:T(8,128)(2,1)S(1)} %collective-permute-done.11.um), channel_id=1, source_target_pairs={{0,2},{1,3},{2,6},{3,7},{4,0},{5,1},{6,4},{7,5},{8,10},{9,11},{10,... | collective-permute-start | bytes 3244040 | tf_op jit(solution)/shard_map/ppermute | solution.py:269
  59.2 18.6 %collective-permute-start.17 = (bf16[272,1024]{1,0:T(8,128)(2,1)S(1)}, bf16[272,1024]{1,0:T(8,128)(2,1)S(1)}, u32[]{:S(2)}, u32[]{:S(2)}) collective-permute-start(bf16[272,1024]{1,0:T(8,128)(2,1)S(1)} %get-tuple-element.112.xs_ref), channel_id=1, source_target_pairs={{0,1},{1,0},{2,3},{3,2},{4,5},{5,4},{6,7},{7,6},{8,9},{9,8},{10,11... | collective-permute-start | bytes 1671176 | tf_op jit(solution)/shard_map/ppermute | solution.py:260
  60.7 17.0 %collective-permute-start.18 = (bf16[256,1024]{1,0:T(8,128)(2,1)S(1)}, bf16[256,1024]{1,0:T(8,128)(2,1)S(1)}, u32[]{:S(2)}, u32[]{:S(2)}) collective-permute-start(bf16[256,1024]{1,0:T(8,128)(2,1)S(1)} %get-tuple-element.113.gs_ref), channel_id=1, source_target_pairs={{0,8},{8,0},{1,9},{9,1},{2,10},{10,2},{3,11},{11,3},{4,12},{12,4},... | collective-permute-start | bytes 1572872 | tf_op jit(solution)/shard_map/ppermute | solution.py:254
  67.4 10.4 %collective-permute-start.15 = (bf16[2,64,1024]{2,1,0:T(8,128)(2,1)S(1)}, bf16[2,64,1024]{2,1,0:T(8,128)(2,1)S(1)}, u32[]{:S(2)}, u32[]{:S(2)}) collective-permute-start(bf16[2,64,1024]{2,1,0:T(8,128)(2,1)S(1)} %get-tuple-element.108), channel_id=1, source_target_pairs={{0,8},{8,0},{1,9},{9,1},{2,10},{10,2},{3,11},{11,3},{4,12},{12,4},... | collective-permute-start | bytes 786440 | tf_op jit(solution)/shard_map/ppermute | solution.py:254
  68.0 9.8 %collective-permute-start.16 = (bf16[2,64,1024]{2,1,0:T(8,128)(2,1)S(1)}, bf16[2,64,1024]{2,1,0:T(8,128)(2,1)S(1)}, u32[]{:S(2)}, u32[]{:S(2)}) collective-permute-start(bf16[2,64,1024]{2,1,0:T(8,128)(2,1)S(1)} %get-tuple-element.110), channel_id=1, source_target_pairs={{0,1},{1,0},{2,3},{3,2},{4,5},{5,4},{6,7},{7,6},{8,9},{9,8},{10,11... | collective-permute-start | bytes 786440 | tf_op jit(solution)/shard_map/ppermute | solution.py:260
  83.5 17.8 %collective-permute-start.19 = (bf16[272,1024]{1,0:T(8,128)(2,1)S(1)}, bf16[272,1024]{1,0:T(8,128)(2,1)S(1)}, u32[]{:S(2)}, u32[]{:S(2)}) collective-permute-start(bf16[272,1024]{1,0:T(8,128)(2,1)S(1)} %get-tuple-element.117.xs_ref), channel_id=1, source_target_pairs={{0,1},{1,0},{2,3},{3,2},{4,5},{5,4},{6,7},{7,6},{8,9},{9,8},{10,11... | collective-permute-start | bytes 1671176 | tf_op jit(solution)/shard_map/ppermute | solution.py:260
  84.9 16.4 %collective-permute-start.20 = (bf16[256,1024]{1,0:T(8,128)(2,1)S(1)}, bf16[256,1024]{1,0:T(8,128)(2,1)S(1)}, u32[]{:S(2)}, u32[]{:S(2)}) collective-permute-start(bf16[256,1024]{1,0:T(8,128)(2,1)S(1)} %get-tuple-element.118.gs_ref), channel_id=1, source_target_pairs={{0,8},{8,0},{1,9},{9,1},{2,10},{10,2},{3,11},{11,3},{4,12},{12,4},... | collective-permute-start | bytes 1572872 | tf_op jit(solution)/shard_map/ppermute | solution.py:254
  86.4 14.9 %collective-permute-start.23 = (bf16[4,64,1024]{2,1,0:T(8,128)(2,1)S(1)}, bf16[4,64,1024]{2,1,0:T(8,128)(2,1)S(1)}, u32[]{:S(2)}, u32[]{:S(2)}) collective-permute-start(bf16[4,64,1024]{2,1,0:T(8,128)(2,1)S(1)} %pad_maximum_fusion.4), channel_id=1, source_target_pairs={{0,2},{1,3},{2,6},{3,7},{4,0},{5,1},{6,4},{7,5},{8,10},{9,11},{10,... | collective-permute-start | bytes 1572872 | tf_op jit(solution)/shard_map/ppermute | solution.py:269
  92.4 8.9 %collective-permute-start.21 = (bf16[2,64,1024]{2,1,0:T(8,128)(2,1)S(1)}, bf16[2,64,1024]{2,1,0:T(8,128)(2,1)S(1)}, u32[]{:S(2)}, u32[]{:S(2)}) collective-permute-start(bf16[2,64,1024]{2,1,0:T(8,128)(2,1)S(1)} %get-tuple-element.120), channel_id=1, source_target_pairs={{0,8},{8,0},{1,9},{9,1},{2,10},{10,2},{3,11},{11,3},{4,12},{12,4},... | collective-permute-start | bytes 786440 | tf_op jit(solution)/shard_map/ppermute | solution.py:254
  93.0 8.3 %collective-permute-start.22 = (bf16[2,64,1024]{2,1,0:T(8,128)(2,1)S(1)}, bf16[2,64,1024]{2,1,0:T(8,128)(2,1)S(1)}, u32[]{:S(2)}, u32[]{:S(2)}) collective-permute-start(bf16[2,64,1024]{2,1,0:T(8,128)(2,1)S(1)} %get-tuple-element.121), channel_id=1, source_target_pairs={{0,1},{1,0},{2,3},{3,2},{4,5},{5,4},{6,7},{7,6},{8,9},{9,8},{10,11... | collective-permute-start | bytes 786440 | tf_op jit(solution)/shard_map/ppermute | solution.py:260
  101.7 16.0 %collective-permute-start.27 = (bf16[4,64,1024]{2,1,0:T(8,128)(2,1)S(1)}, bf16[4,64,1024]{2,1,0:T(8,128)(2,1)S(1)}, u32[]{:S(2)}, u32[]{:S(2)}) collective-permute-start(bf16[4,64,1024]{2,1,0:T(8,128)(2,1)S(1)} %pad_maximum_fusion.5), channel_id=1, source_target_pairs={{0,2},{1,3},{2,6},{3,7},{4,0},{5,1},{6,4},{7,5},{8,10},{9,11},{10,... | collective-permute-start | bytes 1572872 | tf_op jit(solution)/shard_map/ppermute | solution.py:269
  108.3 24.3 %copy-start.1 = (s32[128,8]{0,1:T(8,128)S(1)}, s32[128,8]{0,1:T(8,128)}, u32[]{:S(2)}) copy-start(s32[128,8]{0,1:T(8,128)} %param.11) | copy-start | bytes 12292
  108.3 6.5 %collective-permute-start.24 = (bf16[2,64,1024]{2,1,0:T(8,128)(2,1)S(1)}, bf16[2,64,1024]{2,1,0:T(8,128)(2,1)S(1)}, u32[]{:S(2)}, u32[]{:S(2)}) collective-permute-start(bf16[2,64,1024]{2,1,0:T(8,128)(2,1)S(1)} %get-tuple-element.130), channel_id=1, source_target_pairs={{0,8},{8,0},{1,9},{9,1},{2,10},{10,2},{3,11},{11,3},{4,12},{12,4},... | collective-permute-start | bytes 786440 | tf_op jit(solution)/shard_map/ppermute | solution.py:254
  109.9 7.8 %collective-permute-start.25 = (bf16[2,64,1024]{2,1,0:T(8,128)(2,1)S(1)}, bf16[2,64,1024]{2,1,0:T(8,128)(2,1)S(1)}, u32[]{:S(2)}, u32[]{:S(2)}) collective-permute-start(bf16[2,64,1024]{2,1,0:T(8,128)(2,1)S(1)} %get-tuple-element.131), channel_id=1, source_target_pairs={{0,1},{1,0},{2,3},{3,2},{4,5},{5,4},{6,7},{7,6},{8,9},{9,8},{10,11... | collective-permute-start | bytes 786440 | tf_op jit(solution)/shard_map/ppermute | solution.py:260
  110.4 4.4 %collective-permute-start.26 = (f32[4,2,2,128]{3,1,2,0:T(2,128)S(1)}, f32[4,2,2,128]{3,1,2,0:T(2,128)S(1)}, u32[]{:S(2)}, u32[]{:S(2)}) collective-permute-start(f32[4,2,2,128]{3,1,2,0:T(2,128)S(1)} %constant_dynamic-update-slice_fusion), channel_id=1, source_target_pairs={{0,8},{8,0},{1,9},{9,1},{2,10},{10,2},{3,11},{11,3},{4,12},{12,4},... | collective-permute-start | bytes 24584 | tf_op jit(solution)/shard_map/ppermute | solution.py:254
  117.8 6.7 %collective-permute-start.28 = (bf16[64,1024]{1,0:T(8,128)(2,1)S(1)}, bf16[64,1024]{1,0:T(8,128)(2,1)S(1)}, u32[]{:S(2)}, u32[]{:S(2)}) collective-permute-start(bf16[64,1024]{1,0:T(8,128)(2,1)S(1)} %get-tuple-element.148), channel_id=1, source_target_pairs={{0,1},{1,0},{2,3},{3,2},{4,5},{5,4},{6,7},{7,6},{8,9},{9,8},{10,11... | collective-permute-start | bytes 393224 | tf_op jit(solution)/shard_map/ppermute | solution.py:260
  118.4 6.3 %collective-permute-start.29 = (bf16[64,1024]{1,0:T(8,128)(2,1)S(1)}, bf16[64,1024]{1,0:T(8,128)(2,1)S(1)}, u32[]{:S(2)}, u32[]{:S(2)}) collective-permute-start(bf16[64,1024]{1,0:T(8,128)(2,1)S(1)} %get-tuple-element.149), channel_id=1, source_target_pairs={{0,8},{8,0},{1,9},{9,1},{2,10},{10,2},{3,11},{11,3},{4,12},{12,4},... | collective-permute-start | bytes 393224 | tf_op jit(solution)/shard_map/ppermute | solution.py:254
  118.9 8.6 %collective-permute-start.33 = (f32[2,2,128]{2,0,1:T(2,128)S(1)}, f32[2,2,128]{2,0,1:T(2,128)S(1)}, u32[]{:S(2)}, u32[]{:S(2)}) collective-permute-start(f32[2,2,128]{2,0,1:T(2,128)S(1)} %get-tuple-element.158), channel_id=1, source_target_pairs={{0,4},{1,5},{2,0},{3,1},{4,6},{5,7},{6,2},{7,3},{8,12},{9,13},{10,... | collective-permute-start | bytes 6152 | tf_op jit(solution)/shard_map/ppermute | solution.py:269
  120.9 7.7 %collective-permute-start.34 = (f32[2,2,128]{2,0,1:T(2,128)S(1)}, f32[2,2,128]{2,0,1:T(2,128)S(1)}, u32[]{:S(2)}, u32[]{:S(2)}) collective-permute-start(f32[2,2,128]{2,0,1:T(2,128)S(1)} %get-tuple-element.157), channel_id=1, source_target_pairs={{0,6},{1,7},{2,4},{3,5},{4,2},{5,3},{6,0},{7,1},{8,14},{9,15},{10,... | collective-permute-start | bytes 6152 | tf_op jit(solution)/shard_map/ppermute | solution.py:269
  124.5 4.5 %collective-permute-start.35 = (f32[2,2,128]{2,0,1:T(2,128)S(1)}, f32[2,2,128]{2,0,1:T(2,128)S(1)}, u32[]{:S(2)}, u32[]{:S(2)}) collective-permute-start(f32[2,2,128]{2,0,1:T(2,128)S(1)} %get-tuple-element.156), channel_id=1, source_target_pairs={{0,2},{1,3},{2,6},{3,7},{4,0},{5,1},{6,4},{7,5},{8,10},{9,11},{10,... | collective-permute-start | bytes 6152 | tf_op jit(solution)/shard_map/ppermute | solution.py:269
  124.9 8.9 %collective-permute-start.31 = (bf16[128,1024]{1,0:T(8,128)(2,1)S(1)}, bf16[128,1024]{1,0:T(8,128)(2,1)S(1)}, u32[]{:S(2)}, u32[]{:S(2)}) collective-permute-start(bf16[128,1024]{1,0:T(8,128)(2,1)S(1)} %pad_maximum_fusion.6), channel_id=1, source_target_pairs={{0,2},{1,3},{2,6},{3,7},{4,0},{5,1},{6,4},{7,5},{8,10},{9,11},{10,... | collective-permute-start | bytes 786440 | tf_op jit(solution)/shard_map/ppermute | solution.py:269
  126.9 6.9 %collective-permute-start.32 = (bf16[64,1024]{1,0:T(8,128)(2,1)S(1)}, bf16[64,1024]{1,0:T(8,128)(2,1)S(1)}, u32[]{:S(2)}, u32[]{:S(2)}) collective-permute-start(bf16[64,1024]{1,0:T(8,128)(2,1)S(1)} %fusion.7), channel_id=1, source_target_pairs={{0,8},{8,0},{1,9},{9,1},{2,10},{10,2},{3,11},{11,3},{4,12},{12,4},... | collective-permute-start | bytes 393224 | tf_op jit(solution)/shard_map/ppermute | solution.py:254
  127.5 6.3 %collective-permute-start.30 = (bf16[64,1024]{1,0:T(8,128)(2,1)S(1)}, bf16[64,1024]{1,0:T(8,128)(2,1)S(1)}, u32[]{:S(2)}, u32[]{:S(2)}) collective-permute-start(bf16[64,1024]{1,0:T(8,128)(2,1)S(1)} %fusion.6), channel_id=1, source_target_pairs={{0,1},{1,0},{2,3},{3,2},{4,5},{5,4},{6,7},{7,6},{8,9},{9,8},{10,11... | collective-permute-start | bytes 393224 | tf_op jit(solution)/shard_map/ppermute | solution.py:260
  129.0 3.7 %collective-permute-start.36 = (f32[4,2,128]{2,1,0:T(2,128)S(1)}, f32[4,2,128]{2,1,0:T(2,128)S(1)}, u32[]{:S(2)}, u32[]{:S(2)}) collective-permute-start(f32[4,2,128]{2,1,0:T(2,128)S(1)} %get-tuple-element.154), channel_id=1, source_target_pairs={{0,1},{1,0},{2,3},{3,2},{4,5},{5,4},{6,7},{7,6},{8,9},{9,8},{10,11... | collective-permute-start | bytes 12296 | tf_op jit(solution)/shard_map/ppermute | solution.py:260

commit v5 on v4

--- a/solution.py
+++ b/solution.py
@@ -193,19 +193,19 @@
     both[2 * token_rows :] = picks[...]
 
 
-def merge_kernel(own, both, xs, gs):
-    token_rows = own.shape[0] // 2
+def merge_kernel(x, g, both, xs, gs):
+    token_rows = x.shape[0]
     xs[:token_rows] = both[:token_rows]
-    xs[token_rows : 2 * token_rows] = own[:token_rows]
+    xs[token_rows : 2 * token_rows] = x[...]
     xs[2 * token_rows :] = both[2 * token_rows :]
-    gs[:token_rows] = own[token_rows:]
+    gs[:token_rows] = g[...]
     gs[token_rows:] = both[token_rows : 2 * token_rows]
 
 
-def join_kernel(own, both, um, xs, gs):
-    merge_kernel(own, both, xs, gs)
+def join_kernel(x, g, both, um, xs, gs):
+    merge_kernel(x, g, both, xs, gs)
     split = xs.shape[0]
-    merge_kernel(own, both, um.at[:split], um.at[split:])
+    merge_kernel(x, g, both, um.at[:split], um.at[split:])
 
 
 def pick_kernel(owners, ids, *refs):
@@ -287,9 +287,9 @@
     checkpoint, out_grad, w_gate, w_up, w_down = after((checkpoint, out_grad, w_gate, w_up, w_down), info, owners)
 
     x = (checkpoint.astype(jnp.float32) * scales[:, None]).astype(jnp.bfloat16)
-    own = lax.optimization_barrier(jnp.concatenate([x, out_grad]))
-    near, x_other = over_z(own, 1), over_x(x)
-    others = [over_core(w[0]) for w in after((w_gate, w_up, w_down), own)]
+    x = lax.optimization_barrier(x)
+    near, x_other = (over_z(x, 1), over_z(out_grad, 1)), over_x(x)
+    others = [over_core(w[0]) for w in after((w_gate, w_up, w_down), x)]
     g_other = over_y(after(out_grad, others[0]))
     ids_t, gates_t = after((expert_ids.T, gates.T), others[0])
     (picks,) = move_rows(picks_kernel, (pick_rows,), width, ids_t, gates_t)
@@ -303,12 +303,12 @@
         xs, gs = shares[step]
         tokens[step] = over_y(xs), over_x(gs)
 
-    shares[0] = move_rows(merge_kernel, (x_count, g_count), width, own, both)
+    shares[0] = move_rows(merge_kernel, (x_count, g_count), width, x, out_grad, both)
     hop(0)
     others = after(others, near)
     wg, wu, wd = [jnp.concatenate([w[0], far], axis=0) for w, far in zip((w_gate, w_up, w_down), others)]
     near, both_near, wg, wu, wd = lax.optimization_barrier((near, both_near, wg, wu, wd))
-    um, *shares[1] = move_rows(join_kernel, (x_count + g_count, x_count, g_count), width, near, both_near)
+    um, *shares[1] = move_rows(join_kernel, (x_count + g_count, x_count, g_count), width, *near, both_near)
 
     def expert(step):
         *outs, term = run_expert(tops, token_rows, info, *shares[step], *tokens[step], wg, wu, wd)

time: 135 us -> 137 us (1.015)
  starting transfers between devices: 43 us -> 45.5 us
    ppermute x12, waiting for transfers between devices: 16.2 us -> 5.6 us  [over_y(): return lax.ppermute(value, 'expert', [(e, e ^ 1) for e in range(experts)])]
    ppermute x12, waiting for transfers between devices: 25.6 us -> 31.2 us  [over_x(): return lax.ppermute(value, 'tensor', [(0, 1), (1, 0)])]
    ppermute x10 -> x11, waiting for transfers between devices: 19.2 us -> 23.1 us  [over_z(): lax.ppermute(value, 'expert', [(e, moved(e, shift)) for e in range(expert...]
    concatenate x2, other arithmetic: 1.21 us -> 2.78 us  [body_dense(): jnp.concatenate([w[0], far], axis=0)]
    ppermute x10 -> x11, starting transfers between devices: 16.7 us -> 17.1 us  [over_z(): lax.ppermute(value, 'expert', [(e, moved(e, shift)) for e in range(expert...]
  transfers between devices with their start and end apart: 37 -> 38, of which waited for: 15 -> 15; matrix products, arithmetic and copies ran while one was open for 1% -> 2% of each run, Pallas kernels for 16% -> 16%
where the time goes in v5:
time: 137 us
  waiting for transfers between devices  60 us (44%)
  starting transfers between devices  45.5 us (33%)
  Pallas kernels  22.3 us (16%)
  other arithmetic  5.71 us (4%)
  local copies, waits for them, and re-layouts  2.47 us (2%)
    ppermute x12, waiting for transfers between devices, over_x(): return lax.ppermute(value, 'tensor', [(0, 1), (1, 0)])  31.2 us
    ppermute x11, waiting for transfers between devices, over_z(): lax.ppermute(value, 'expert', [(e, moved(e, shift)) for e in range(expert...  23.1 us
    pallas_call x4, Pallas kernels, run_expert(): pl.pallas_call(functools.partial(expert_kernel, tops), in_specs=[pl.Block...  20.7 us
    ppermute x11, starting transfers between devices, over_z(): lax.ppermute(value, 'expert', [(e, moved(e, shift)) for e in range(expert...  17.1 us
    ppermute x12, starting transfers between devices, over_x(): return lax.ppermute(value, 'tensor', [(0, 1), (1, 0)])  13.8 us
    ppermute x12, starting transfers between devices, over_y(): return lax.ppermute(value, 'expert', [(e, e ^ 1) for e in range(experts)])  13.6 us
    ppermute x12, waiting for transfers between devices, over_y(): return lax.ppermute(value, 'expert', [(e, e ^ 1) for e in range(experts)])  5.6 us
    concatenate x2, other arithmetic, body_dense(): jnp.concatenate([w[0], far], axis=0)  2.78 us
  transfers between devices with their start and end apart: 38, of which 15 were waited for; matrix products, arithmetic and copies ran while one was open for 2% of the time, Pallas kernels for 16%

profile of v5, /device:TPU:0, one launch (start us, length us, event | category | flops | bytes accessed | tf_op | source)
XLA Modules:
  0.0 137.0 jit_solution(5918286495644450637)
XLA Ops:
  0.9 1.1 multiply_convert_fusion.x
  3.0 2.6 %collective-permute-start.1 = (bf16[128,1024]{1,0:T(8,128)(2,1)S(1)}, bf16[128,1024]{1,0:T(8,128)(2,1)S(1)}, u32[]{:S(2)}, u32[]{:S(2)}) collective-permute-start(bf16[128,1024]{1,0:T(8,128)(2,1)S(1)} %multiply_convert_fusion.x), channel_id=1, source_target_pairs={{0,8},{8,0},{1,9},{9,1},{2,10},{10,2},{3,11},{11,3},{4,12},{12,4},... | collective-permute-start | bytes 786440 | tf_op jit(solution)/shard_map/ppermute | solution.py:254
  5.8 2.9 %collective-permute-start.2 = (bf16[128,1024]{1,0:T(8,128)(2,1)}, bf16[128,1024]{1,0:T(8,128)(2,1)S(1)}, u32[]{:S(2)}, u32[]{:S(2)}) collective-permute-start(bf16[128,1024]{1,0:T(8,128)(2,1)} %g), channel_id=1, source_target_pairs={{0,1},{1,0},{2,3},{3,2},{4,5},{5,4},{6,7},{7,6},{8,9},{9,8},{10,11... | collective-permute-start | bytes 786440 | tf_op jit(solution)/shard_map/ppermute | solution.py:260
  8.7 1.6 %collective-permute-start.5 = (bf16[128,1024]{1,0:T(8,128)(2,1)S(1)}, bf16[128,1024]{1,0:T(8,128)(2,1)S(1)}, u32[]{:S(2)}, u32[]{:S(2)}) collective-permute-start(bf16[128,1024]{1,0:T(8,128)(2,1)S(1)} %multiply_convert_fusion.x), channel_id=1, source_target_pairs={{0,2},{1,3},{2,6},{3,7},{4,0},{5,1},{6,4},{7,5},{8,10},{9,11},{10,... | collective-permute-start | bytes 786440 | tf_op jit(solution)/shard_map/ppermute | solution.py:269
  10.2 2.3 %collective-permute-done.1.x_far = bf16[128,1024]{1,0:T(8,128)(2,1)S(1)} collective-permute-done((bf16[128,1024]{1,0:T(8,128)(2,1)S(1)}, bf16[128,1024]{1,0:T(8,128)(2,1)S(1)}, u32[]{:S(2)}, u32[]{:S(2)}) %collective-permute-start.1) | collective-permute-done | bytes 262176 | tf_op jit(solution)/shard_map/ppermute | solution.py:254
  12.5 1.8 %collective-permute-start.6 = (bf16[128,1024]{1,0:T(8,128)(2,1)}, bf16[128,1024]{1,0:T(8,128)(2,1)S(1)}, u32[]{:S(2)}, u32[]{:S(2)}) collective-permute-start(bf16[128,1024]{1,0:T(8,128)(2,1)} %g), channel_id=1, source_target_pairs={{0,2},{1,3},{2,6},{3,7},{4,0},{5,1},{6,4},{7,5},{8,10},{9,11},{10,... | collective-permute-start | bytes 786440 | tf_op jit(solution)/shard_map/ppermute | solution.py:269
  14.3 0.7 copy-done.1
  15.0 0.7 copy-done.3
  15.8 2.6 %collective-permute-start.7 = (bf16[272,1024]{1,0:T(8,128)(2,1)S(1)}, bf16[272,1024]{1,0:T(8,128)(2,1)S(1)}, u32[]{:S(2)}, u32[]{:S(2)}) collective-permute-start(bf16[272,1024]{1,0:T(8,128)(2,1)S(1)} %shard_map.96.both), channel_id=1, source_target_pairs={{0,2},{1,3},{2,6},{3,7},{4,0},{5,1},{6,4},{7,5},{8,10},{9,11},{10,... | collective-permute-start | bytes 1671176 | tf_op jit(solution)/shard_map/ppermute | solution.py:269
  18.4 0.9 copy-done
  19.5 4.9 %collective-permute-done.6.g = bf16[128,1024]{1,0:T(8,128)(2,1)S(1)} collective-permute-done((bf16[128,1024]{1,0:T(8,128)(2,1)}, bf16[128,1024]{1,0:T(8,128)(2,1)S(1)}, u32[]{:S(2)}, u32[]{:S(2)}) %collective-permute-start.6) | collective-permute-done | bytes 262176 | tf_op jit(solution)/shard_map/ppermute | solution.py:269
  24.6 1.5 %collective-permute-start.4 = (bf16[256,1024]{1,0:T(8,128)(2,1)S(1)}, bf16[256,1024]{1,0:T(8,128)(2,1)S(1)}, u32[]{:S(2)}, u32[]{:S(2)}) collective-permute-start(bf16[256,1024]{1,0:T(8,128)(2,1)S(1)} %get-tuple-element.88.gs_ref), channel_id=1, source_target_pairs={{0,8},{8,0},{1,9},{9,1},{2,10},{10,2},{3,11},{11,3},{4,12},{12,4},... | collective-permute-start | bytes 1572872 | tf_op jit(solution)/shard_map/ppermute | solution.py:254
  26.1 2.4 %pad_maximum_fusion = (bf16[768,2048]{1,0:T(8,128)(2,1)S(1)}, bf16[768,2048]{1,0:T(8,128)(2,1)S(1)}) fusion(bf16[384,2048]{1,0:T(8,128)(2,1)S(1)} %collective-permute-done, bf16[384,2048]{1,0:T(8,128)(2,1)} %bitcast.86, bf16[384,2048]{1,0:T(8,128)(2,1)S(1)} %collective-permute-done.8, bf16[384,2048]{1,0:T(8,128)(2,1)} %bitcast.88), kind=kLoop, calls=%fused_computation | loop fusion | flops 12582912 | bytes 12582912 | tf_op jit(solution)/shard_map/concatenate | solution.py:309
  28.9 6.3 %collective-permute-done.7.both = bf16[272,1024]{1,0:T(8,128)(2,1)S(1)} collective-permute-done((bf16[272,1024]{1,0:T(8,128)(2,1)S(1)}, bf16[272,1024]{1,0:T(8,128)(2,1)S(1)}, u32[]{:S(2)}, u32[]{:S(2)}) %collective-permute-start.7) | collective-permute-done | bytes 557088 | tf_op jit(solution)/shard_map/ppermute | solution.py:269
  35.3 0.8 collective-permute-start.12
  36.7 1.5 %collective-permute-start.15 = (bf16[256,1024]{1,0:T(8,128)(2,1)S(1)}, bf16[256,1024]{1,0:T(8,128)(2,1)S(1)}, u32[]{:S(2)}, u32[]{:S(2)}) collective-permute-start(bf16[256,1024]{1,0:T(8,128)(2,1)S(1)} %get-tuple-element.101.gs_ref), channel_id=1, source_target_pairs={{0,8},{8,0},{1,9},{9,1},{2,10},{10,2},{3,11},{11,3},{4,12},{12,4},... | collective-permute-start | bytes 1572872 | tf_op jit(solution)/shard_map/ppermute | solution.py:254
  38.2 5.2 %shard_map.99 = (bf16[2,64,1024]{2,1,0:T(8,128)(2,1)S(1)}, bf16[2,64,1024]{2,1,0:T(8,128)(2,1)S(1)}, bf16[2,64,1024]{2,1,0:T(8,128)(2,1)S(1)}, bf16[2,64,1024]{2,1,0:T(8,128)(2,1)S(1)}, f32[2,8,256]{2,1,0:T(8,128)S(1)}) custom-call(s32[3]{0:T(128)S(1)} %pad_add_fusion.info_ref, bf16[272,1024]{1,0:T(8,128)(2,1)S(1)} %get-tuple-element.87.xs_ref, ...), custom_call_target="tpu_custom_call" | custom-call | flops 4026531840 | bytes 12582912 | tf_op jit(solution)/shard_map/pallas_call | solution.py:162
  43.9 1.5 %collective-permute-start.11 = (bf16[2,64,1024]{2,1,0:T(8,128)(2,1)S(1)}, bf16[2,64,1024]{2,1,0:T(8,128)(2,1)S(1)}, u32[]{:S(2)}, u32[]{:S(2)}) collective-permute-start(bf16[2,64,1024]{2,1,0:T(8,128)(2,1)S(1)} %get-tuple-element.109), channel_id=1, source_target_pairs={{0,1},{1,0},{2,3},{3,2},{4,5},{5,4},{6,7},{7,6},{8,9},{9,8},{10,11... | collective-permute-start | bytes 786440 | tf_op jit(solution)/shard_map/ppermute | solution.py:260
  45.5 9.3 %collective-permute-done.10 = bf16[2,64,1024]{2,1,0:T(8,128)(2,1)S(1)} collective-permute-done((bf16[2,64,1024]{2,1,0:T(8,128)(2,1)S(1)}, bf16[2,64,1024]{2,1,0:T(8,128)(2,1)S(1)}, u32[]{:S(2)}, u32[]{:S(2)}) %collective-permute-start.10) | collective-permute-done | bytes 262176 | tf_op jit(solution)/shard_map/ppermute | solution.py:254
  55.0 6.0 %collective-permute-done.12.um = bf16[528,1024]{1,0:T(8,128)(2,1)S(1)} collective-permute-done((bf16[528,1024]{1,0:T(8,128)(2,1)S(1)}, bf16[528,1024]{1,0:T(8,128)(2,1)S(1)}, u32[]{:S(2)}, u32[]{:S(2)}) %collective-permute-start.12) | collective-permute-done | bytes 1081376 | tf_op jit(solution)/shard_map/ppermute | solution.py:269
  61.1 0.8 collective-permute-start.13
  61.9 0.8 collective-permute-start.18
  62.7 1.5 %collective-permute-start.19 = (bf16[256,1024]{1,0:T(8,128)(2,1)S(1)}, bf16[256,1024]{1,0:T(8,128)(2,1)S(1)}, u32[]{:S(2)}, u32[]{:S(2)}) collective-permute-start(bf16[256,1024]{1,0:T(8,128)(2,1)S(1)} %get-tuple-element.117.gs_ref), channel_id=1, source_target_pairs={{0,8},{8,0},{1,9},{9,1},{2,10},{10,2},{3,11},{11,3},{4,12},{12,4},... | collective-permute-start | bytes 1572872 | tf_op jit(solution)/shard_map/ppermute | solution.py:254
  64.2 5.2 %shard_map.100 = (bf16[2,64,1024]{2,1,0:T(8,128)(2,1)S(1)}, bf16[2,64,1024]{2,1,0:T(8,128)(2,1)S(1)}, bf16[2,64,1024]{2,1,0:T(8,128)(2,1)S(1)}, bf16[2,64,1024]{2,1,0:T(8,128)(2,1)S(1)}, f32[2,8,256]{2,1,0:T(8,128)S(1)}) custom-call(s32[3]{0:T(128)S(1)} %pad_add_fusion.info_ref, bf16[272,1024]{1,0:T(8,128)(2,1)S(1)} %get-tuple-element.100.xs_ref, ...), custom_call_target="tpu_custom_call" | custom-call | flops 4026531840 | bytes 12582912 | tf_op jit(solution)/shard_map/pallas_call | solution.py:162
  70.0 1.3 collective-permute-start.17
  71.3 8.7 %collective-permute-done.16 = bf16[2,64,1024]{2,1,0:T(8,128)(2,1)S(1)} collective-permute-done((bf16[2,64,1024]{2,1,0:T(8,128)(2,1)S(1)}, bf16[2,64,1024]{2,1,0:T(8,128)(2,1)S(1)}, u32[]{:S(2)}, u32[]{:S(2)}) %collective-permute-start.16) | collective-permute-done | bytes 262176 | tf_op jit(solution)/shard_map/ppermute | solution.py:254
  80.1 5.7 %collective-permute-done.13.um = bf16[528,1024]{1,0:T(8,128)(2,1)S(1)} collective-permute-done((bf16[528,1024]{1,0:T(8,128)(2,1)S(1)}, bf16[528,1024]{1,0:T(8,128)(2,1)S(1)}, u32[]{:S(2)}, u32[]{:S(2)}) %collective-permute-start.13) | collective-permute-done | bytes 1081376 | tf_op jit(solution)/shard_map/ppermute | solution.py:269
  86.0 0.9 collective-permute-start.20
  86.9 1.7 %collective-permute-start.21 = (bf16[256,1024]{1,0:T(8,128)(2,1)S(1)}, bf16[256,1024]{1,0:T(8,128)(2,1)S(1)}, u32[]{:S(2)}, u32[]{:S(2)}) collective-permute-start(bf16[256,1024]{1,0:T(8,128)(2,1)S(1)} %get-tuple-element.122.gs_ref), channel_id=1, source_target_pairs={{0,8},{8,0},{1,9},{9,1},{2,10},{10,2},{3,11},{11,3},{4,12},{12,4},... | collective-permute-start | bytes 1572872 | tf_op jit(solution)/shard_map/ppermute | solution.py:254
  88.5 0.8 collective-permute-start.24
  89.3 5.2 %shard_map.103 = (bf16[2,64,1024]{2,1,0:T(8,128)(2,1)S(1)}, bf16[2,64,1024]{2,1,0:T(8,128)(2,1)S(1)}, bf16[2,64,1024]{2,1,0:T(8,128)(2,1)S(1)}, bf16[2,64,1024]{2,1,0:T(8,128)(2,1)S(1)}, f32[2,8,256]{2,1,0:T(8,128)S(1)}) custom-call(s32[3]{0:T(128)S(1)} %pad_add_fusion.info_ref, bf16[272,1024]{1,0:T(8,128)(2,1)S(1)} %get-tuple-element.116.xs_ref, ...), custom_call_target="tpu_custom_call" | custom-call | flops 4026531840 | bytes 12582912 | tf_op jit(solution)/shard_map/pallas_call | solution.py:162
  95.1 1.0 collective-permute-start.23
  96.2 7.3 %collective-permute-done.22 = bf16[2,64,1024]{2,1,0:T(8,128)(2,1)S(1)} collective-permute-done((bf16[2,64,1024]{2,1,0:T(8,128)(2,1)S(1)}, bf16[2,64,1024]{2,1,0:T(8,128)(2,1)S(1)}, u32[]{:S(2)}, u32[]{:S(2)}) %collective-permute-start.22) | collective-permute-done | bytes 262176 | tf_op jit(solution)/shard_map/ppermute | solution.py:254
  103.8 1.5 %collective-permute-start.28 = (bf16[4,64,1024]{2,1,0:T(8,128)(2,1)S(1)}, bf16[4,64,1024]{2,1,0:T(8,128)(2,1)S(1)}, u32[]{:S(2)}, u32[]{:S(2)}) collective-permute-start(bf16[4,64,1024]{2,1,0:T(8,128)(2,1)S(1)} %pad_maximum_fusion.4), channel_id=1, source_target_pairs={{0,2},{1,3},{2,6},{3,7},{4,0},{5,1},{6,4},{7,5},{8,10},{9,11},{10,... | collective-permute-start | bytes 1572872 | tf_op jit(solution)/shard_map/ppermute | solution.py:269
  105.3 5.2 %shard_map.104 = (bf16[2,64,1024]{2,1,0:T(8,128)(2,1)S(1)}, bf16[2,64,1024]{2,1,0:T(8,128)(2,1)S(1)}, bf16[2,64,1024]{2,1,0:T(8,128)(2,1)S(1)}, bf16[2,64,1024]{2,1,0:T(8,128)(2,1)S(1)}, f32[2,8,256]{2,1,0:T(8,128)S(1)}) custom-call(s32[3]{0:T(128)S(1)} %pad_add_fusion.info_ref, bf16[272,1024]{1,0:T(8,128)(2,1)S(1)} %get-tuple-element.121.xs_ref, ...), custom_call_target="tpu_custom_call" | custom-call | flops 4026531840 | bytes 12582912 | tf_op jit(solution)/shard_map/pallas_call | solution.py:162
  110.5 1.6 %collective-permute-start.25 = (bf16[2,64,1024]{2,1,0:T(8,128)(2,1)S(1)}, bf16[2,64,1024]{2,1,0:T(8,128)(2,1)S(1)}, u32[]{:S(2)}, u32[]{:S(2)}) collective-permute-start(bf16[2,64,1024]{2,1,0:T(8,128)(2,1)S(1)} %get-tuple-element.134), channel_id=1, source_target_pairs={{0,8},{8,0},{1,9},{9,1},{2,10},{10,2},{3,11},{11,3},{4,12},{12,4},... | collective-permute-start | bytes 786440 | tf_op jit(solution)/shard_map/ppermute | solution.py:254
  112.0 1.0 collective-permute-start.26
  113.6 3.3 %collective-permute-done.27 = f32[4,2,2,128]{3,1,2,0:T(2,128)S(1)} collective-permute-done((f32[4,2,2,128]{3,1,2,0:T(2,128)S(1)}, f32[4,2,2,128]{3,1,2,0:T(2,128)S(1)}, u32[]{:S(2)}, u32[]{:S(2)}) %collective-permute-start.27) | collective-permute-done | bytes 8224 | tf_op jit(solution)/shard_map/ppermute | solution.py:254
  117.0 2.8 %collective-permute-done.26 = bf16[2,64,1024]{2,1,0:T(8,128)(2,1)S(1)} collective-permute-done((bf16[2,64,1024]{2,1,0:T(8,128)(2,1)S(1)}, bf16[2,64,1024]{2,1,0:T(8,128)(2,1)S(1)}, u32[]{:S(2)}, u32[]{:S(2)}) %collective-permute-start.26) | collective-permute-done | bytes 262176 | tf_op jit(solution)/shard_map/ppermute | solution.py:260
  119.9 1.1 collective-permute-start.29
  121.5 1.4 %collective-permute-start.34 = (f32[2,2,128]{2,0,1:T(2,128)S(1)}, f32[2,2,128]{2,0,1:T(2,128)S(1)}, u32[]{:S(2)}, u32[]{:S(2)}) collective-permute-start(f32[2,2,128]{2,0,1:T(2,128)S(1)} %get-tuple-element.162), channel_id=1, source_target_pairs={{0,4},{1,5},{2,0},{3,1},{4,6},{5,7},{6,2},{7,3},{8,12},{9,13},{10,... | collective-permute-start | bytes 6152 | tf_op jit(solution)/shard_map/ppermute | solution.py:269
  123.0 3.8 %collective-permute-start.35 = (f32[2,2,128]{2,0,1:T(2,128)S(1)}, f32[2,2,128]{2,0,1:T(2,128)S(1)}, u32[]{:S(2)}, u32[]{:S(2)}) collective-permute-start(f32[2,2,128]{2,0,1:T(2,128)S(1)} %get-tuple-element.161), channel_id=1, source_target_pairs={{0,6},{1,7},{2,4},{3,5},{4,2},{5,3},{6,0},{7,1},{8,14},{9,15},{10,... | collective-permute-start | bytes 6152 | tf_op jit(solution)/shard_map/ppermute | solution.py:269
  127.2 1.9 %collective-permute-start.32 = (bf16[128,1024]{1,0:T(8,128)(2,1)S(1)}, bf16[128,1024]{1,0:T(8,128)(2,1)S(1)}, u32[]{:S(2)}, u32[]{:S(2)}) collective-permute-start(bf16[128,1024]{1,0:T(8,128)(2,1)S(1)} %pad_maximum_fusion.5), channel_id=1, source_target_pairs={{0,2},{1,3},{2,6},{3,7},{4,0},{5,1},{6,4},{7,5},{8,10},{9,11},{10,... | collective-permute-start | bytes 786440 | tf_op jit(solution)/shard_map/ppermute | solution.py:269
  129.8 1.3 collective-permute-start.31
  131.3 1.1 collective-permute-start.37
  132.4 2.6 %collective-permute-done.37.refs_1_ = f32[4,2,128]{2,1,0:T(2,128)S(1)} collective-permute-done((f32[4,2,128]{2,1,0:T(2,128)S(1)}, f32[4,2,128]{2,1,0:T(2,128)S(1)}, u32[]{:S(2)}, u32[]{:S(2)}) %collective-permute-start.37) | collective-permute-done | bytes 4128 | tf_op jit(solution)/shard_map/ppermute | solution.py:260
  135.0 1.2 shard_map.105
  136.3 0.7 pad_maximum_fusion.6
  (78 shorter events, 8.3 us)
Async XLA Ops:
  2.0 3.8 %collective-permute-start = (bf16[384,2048]{1,0:T(8,128)(2,1)}, bf16[384,2048]{1,0:T(8,128)(2,1)S(1)}, u32[]{:S(2)}, u32[]{:S(2)}) collective-permute-start(bf16[384,2048]{1,0:T(8,128)(2,1)} %bitcast.85), channel_id=1, source_target_pairs={{0,16},{16,0},{1,17},{17,1},{2,18},{18,2},{3,19},{19,3},{4,20},{20... | collective-permute-start | bytes 4718600 | tf_op jit(solution)/shard_map/ppermute | solution.py:257
  2.5 21.8 %collective-permute-start.8 = (bf16[384,2048]{1,0:T(8,128)(2,1)}, bf16[384,2048]{1,0:T(8,128)(2,1)S(1)}, u32[]{:S(2)}, u32[]{:S(2)}) collective-permute-start(bf16[384,2048]{1,0:T(8,128)(2,1)} %bitcast.87), channel_id=1, source_target_pairs={{0,16},{16,0},{1,17},{17,1},{2,18},{18,2},{3,19},{19,3},{4,20},{20... | collective-permute-start | bytes 4718600 | tf_op jit(solution)/shard_map/ppermute | solution.py:257
  2.6 21.8 %collective-permute-start.9 = (bf16[384,2048]{1,0:T(8,128)(2,1)}, bf16[384,2048]{1,0:T(8,128)(2,1)S(1)}, u32[]{:S(2)}, u32[]{:S(2)}) collective-permute-start(bf16[384,2048]{1,0:T(8,128)(2,1)} %bitcast.89), channel_id=1, source_target_pairs={{0,16},{16,0},{1,17},{17,1},{2,18},{18,2},{3,19},{19,3},{4,20},{20... | collective-permute-start | bytes 4718600 | tf_op jit(solution)/shard_map/ppermute | solution.py:257
  3.0 9.5 %collective-permute-start.1 = (bf16[128,1024]{1,0:T(8,128)(2,1)S(1)}, bf16[128,1024]{1,0:T(8,128)(2,1)S(1)}, u32[]{:S(2)}, u32[]{:S(2)}) collective-permute-start(bf16[128,1024]{1,0:T(8,128)(2,1)S(1)} %multiply_convert_fusion.x), channel_id=1, source_target_pairs={{0,8},{8,0},{1,9},{9,1},{2,10},{10,2},{3,11},{11,3},{4,12},{12,4},... | collective-permute-start | bytes 786440 | tf_op jit(solution)/shard_map/ppermute | solution.py:254
  5.8 10.0 %collective-permute-start.2 = (bf16[128,1024]{1,0:T(8,128)(2,1)}, bf16[128,1024]{1,0:T(8,128)(2,1)S(1)}, u32[]{:S(2)}, u32[]{:S(2)}) collective-permute-start(bf16[128,1024]{1,0:T(8,128)(2,1)} %g), channel_id=1, source_target_pairs={{0,1},{1,0},{2,3},{3,2},{4,5},{5,4},{6,7},{7,6},{8,9},{9,8},{10,11... | collective-permute-start | bytes 786440 | tf_op jit(solution)/shard_map/ppermute | solution.py:260
  8.7 10.8 %collective-permute-start.5 = (bf16[128,1024]{1,0:T(8,128)(2,1)S(1)}, bf16[128,1024]{1,0:T(8,128)(2,1)S(1)}, u32[]{:S(2)}, u32[]{:S(2)}) collective-permute-start(bf16[128,1024]{1,0:T(8,128)(2,1)S(1)} %multiply_convert_fusion.x), channel_id=1, source_target_pairs={{0,2},{1,3},{2,6},{3,7},{4,0},{5,1},{6,4},{7,5},{8,10},{9,11},{10,... | collective-permute-start | bytes 786440 | tf_op jit(solution)/shard_map/ppermute | solution.py:269
  12.5 11.9 %collective-permute-start.6 = (bf16[128,1024]{1,0:T(8,128)(2,1)}, bf16[128,1024]{1,0:T(8,128)(2,1)S(1)}, u32[]{:S(2)}, u32[]{:S(2)}) collective-permute-start(bf16[128,1024]{1,0:T(8,128)(2,1)} %g), channel_id=1, source_target_pairs={{0,2},{1,3},{2,6},{3,7},{4,0},{5,1},{6,4},{7,5},{8,10},{9,11},{10,... | collective-permute-start | bytes 786440 | tf_op jit(solution)/shard_map/ppermute | solution.py:269
  14.3 0.7 copy-start.1
  15.0 0.7 copy-start.3
  15.8 19.4 %collective-permute-start.7 = (bf16[272,1024]{1,0:T(8,128)(2,1)S(1)}, bf16[272,1024]{1,0:T(8,128)(2,1)S(1)}, u32[]{:S(2)}, u32[]{:S(2)}) collective-permute-start(bf16[272,1024]{1,0:T(8,128)(2,1)S(1)} %shard_map.96.both), channel_id=1, source_target_pairs={{0,2},{1,3},{2,6},{3,7},{4,0},{5,1},{6,4},{7,5},{8,10},{9,11},{10,... | collective-permute-start | bytes 1671176 | tf_op jit(solution)/shard_map/ppermute | solution.py:269
  18.4 0.9 copy-start
  24.4 13.8 %collective-permute-start.3 = (bf16[272,1024]{1,0:T(8,128)(2,1)S(1)}, bf16[272,1024]{1,0:T(8,128)(2,1)S(1)}, u32[]{:S(2)}, u32[]{:S(2)}) collective-permute-start(bf16[272,1024]{1,0:T(8,128)(2,1)S(1)} %get-tuple-element.87.xs_ref), channel_id=1, source_target_pairs={{0,1},{1,0},{2,3},{3,2},{4,5},{5,4},{6,7},{7,6},{8,9},{9,8},{10,11... | collective-permute-start | bytes 1671176 | tf_op jit(solution)/shard_map/ppermute | solution.py:260
  24.6 13.5 %collective-permute-start.4 = (bf16[256,1024]{1,0:T(8,128)(2,1)S(1)}, bf16[256,1024]{1,0:T(8,128)(2,1)S(1)}, u32[]{:S(2)}, u32[]{:S(2)}) collective-permute-start(bf16[256,1024]{1,0:T(8,128)(2,1)S(1)} %get-tuple-element.88.gs_ref), channel_id=1, source_target_pairs={{0,8},{8,0},{1,9},{9,1},{2,10},{10,2},{3,11},{11,3},{4,12},{12,4},... | collective-permute-start | bytes 1572872 | tf_op jit(solution)/shard_map/ppermute | solution.py:254
  26.1 2.4 %copy-start.4 = (bf16[1,384,2048]{2,1,0:T(8,128)(2,1)S(1)}, bf16[1,384,2048]{2,1,0:T(8,128)(2,1)}, u32[]{:S(2)}) copy-start(bf16[1,384,2048]{2,1,0:T(8,128)(2,1)} %param.15) | copy-start | bytes 4718596
  35.3 25.7 %collective-permute-start.12 = (bf16[528,1024]{1,0:T(8,128)(2,1)S(1)}, bf16[528,1024]{1,0:T(8,128)(2,1)S(1)}, u32[]{:S(2)}, u32[]{:S(2)}) collective-permute-start(bf16[528,1024]{1,0:T(8,128)(2,1)S(1)} %get-tuple-element.99), channel_id=1, source_target_pairs={{0,2},{1,3},{2,6},{3,7},{4,0},{5,1},{6,4},{7,5},{8,10},{9,11},{10,... | collective-permute-start | bytes 3244040 | tf_op jit(solution)/shard_map/ppermute | solution.py:269
  36.2 28.0 %collective-permute-start.14 = (bf16[272,1024]{1,0:T(8,128)(2,1)S(1)}, bf16[272,1024]{1,0:T(8,128)(2,1)S(1)}, u32[]{:S(2)}, u32[]{:S(2)}) collective-permute-start(bf16[272,1024]{1,0:T(8,128)(2,1)S(1)} %get-tuple-element.100.xs_ref), channel_id=1, source_target_pairs={{0,1},{1,0},{2,3},{3,2},{4,5},{5,4},{6,7},{7,6},{8,9},{9,8},{10,11... | collective-permute-start | bytes 1671176 | tf_op jit(solution)/shard_map/ppermute | solution.py:260
  36.7 27.5 %collective-permute-start.15 = (bf16[256,1024]{1,0:T(8,128)(2,1)S(1)}, bf16[256,1024]{1,0:T(8,128)(2,1)S(1)}, u32[]{:S(2)}, u32[]{:S(2)}) collective-permute-start(bf16[256,1024]{1,0:T(8,128)(2,1)S(1)} %get-tuple-element.101.gs_ref), channel_id=1, source_target_pairs={{0,8},{8,0},{1,9},{9,1},{2,10},{10,2},{3,11},{11,3},{4,12},{12,4},... | collective-permute-start | bytes 1572872 | tf_op jit(solution)/shard_map/ppermute | solution.py:254
  43.3 11.5 %collective-permute-start.10 = (bf16[2,64,1024]{2,1,0:T(8,128)(2,1)S(1)}, bf16[2,64,1024]{2,1,0:T(8,128)(2,1)S(1)}, u32[]{:S(2)}, u32[]{:S(2)}) collective-permute-start(bf16[2,64,1024]{2,1,0:T(8,128)(2,1)S(1)} %get-tuple-element.108), channel_id=1, source_target_pairs={{0,8},{8,0},{1,9},{9,1},{2,10},{10,2},{3,11},{11,3},{4,12},{12,4},... | collective-permute-start | bytes 786440 | tf_op jit(solution)/shard_map/ppermute | solution.py:254
  43.9 11.1 %collective-permute-start.11 = (bf16[2,64,1024]{2,1,0:T(8,128)(2,1)S(1)}, bf16[2,64,1024]{2,1,0:T(8,128)(2,1)S(1)}, u32[]{:S(2)}, u32[]{:S(2)}) collective-permute-start(bf16[2,64,1024]{2,1,0:T(8,128)(2,1)S(1)} %get-tuple-element.109), channel_id=1, source_target_pairs={{0,1},{1,0},{2,3},{3,2},{4,5},{5,4},{6,7},{7,6},{8,9},{9,8},{10,11... | collective-permute-start | bytes 786440 | tf_op jit(solution)/shard_map/ppermute | solution.py:260
  61.1 24.8 %collective-permute-start.13 = (bf16[528,1024]{1,0:T(8,128)(2,1)S(1)}, bf16[528,1024]{1,0:T(8,128)(2,1)S(1)}, u32[]{:S(2)}, u32[]{:S(2)}) collective-permute-start(bf16[528,1024]{1,0:T(8,128)(2,1)S(1)} %collective-permute-done.12.um), channel_id=1, source_target_pairs={{0,2},{1,3},{2,6},{3,7},{4,0},{5,1},{6,4},{7,5},{8,10},{9,11},{10,... | collective-permute-start | bytes 3244040 | tf_op jit(solution)/shard_map/ppermute | solution.py:269
  61.9 18.0 %collective-permute-start.18 = (bf16[272,1024]{1,0:T(8,128)(2,1)S(1)}, bf16[272,1024]{1,0:T(8,128)(2,1)S(1)}, u32[]{:S(2)}, u32[]{:S(2)}) collective-permute-start(bf16[272,1024]{1,0:T(8,128)(2,1)S(1)} %get-tuple-element.116.xs_ref), channel_id=1, source_target_pairs={{0,1},{1,0},{2,3},{3,2},{4,5},{5,4},{6,7},{7,6},{8,9},{9,8},{10,11... | collective-permute-start | bytes 1671176 | tf_op jit(solution)/shard_map/ppermute | solution.py:260
  62.7 17.2 %collective-permute-start.19 = (bf16[256,1024]{1,0:T(8,128)(2,1)S(1)}, bf16[256,1024]{1,0:T(8,128)(2,1)S(1)}, u32[]{:S(2)}, u32[]{:S(2)}) collective-permute-start(bf16[256,1024]{1,0:T(8,128)(2,1)S(1)} %get-tuple-element.117.gs_ref), channel_id=1, source_target_pairs={{0,8},{8,0},{1,9},{9,1},{2,10},{10,2},{3,11},{11,3},{4,12},{12,4},... | collective-permute-start | bytes 1572872 | tf_op jit(solution)/shard_map/ppermute | solution.py:254
  69.4 10.5 %collective-permute-start.16 = (bf16[2,64,1024]{2,1,0:T(8,128)(2,1)S(1)}, bf16[2,64,1024]{2,1,0:T(8,128)(2,1)S(1)}, u32[]{:S(2)}, u32[]{:S(2)}) collective-permute-start(bf16[2,64,1024]{2,1,0:T(8,128)(2,1)S(1)} %get-tuple-element.112), channel_id=1, source_target_pairs={{0,8},{8,0},{1,9},{9,1},{2,10},{10,2},{3,11},{11,3},{4,12},{12,4},... | collective-permute-start | bytes 786440 | tf_op jit(solution)/shard_map/ppermute | solution.py:254
  70.0 9.9 %collective-permute-start.17 = (bf16[2,64,1024]{2,1,0:T(8,128)(2,1)S(1)}, bf16[2,64,1024]{2,1,0:T(8,128)(2,1)S(1)}, u32[]{:S(2)}, u32[]{:S(2)}) collective-permute-start(bf16[2,64,1024]{2,1,0:T(8,128)(2,1)S(1)} %get-tuple-element.114), channel_id=1, source_target_pairs={{0,1},{1,0},{2,3},{3,2},{4,5},{5,4},{6,7},{7,6},{8,9},{9,8},{10,11... | collective-permute-start | bytes 786440 | tf_op jit(solution)/shard_map/ppermute | solution.py:260
  86.0 17.5 %collective-permute-start.20 = (bf16[272,1024]{1,0:T(8,128)(2,1)S(1)}, bf16[272,1024]{1,0:T(8,128)(2,1)S(1)}, u32[]{:S(2)}, u32[]{:S(2)}) collective-permute-start(bf16[272,1024]{1,0:T(8,128)(2,1)S(1)} %get-tuple-element.121.xs_ref), channel_id=1, source_target_pairs={{0,1},{1,0},{2,3},{3,2},{4,5},{5,4},{6,7},{7,6},{8,9},{9,8},{10,11... | collective-permute-start | bytes 1671176 | tf_op jit(solution)/shard_map/ppermute | solution.py:260
  86.9 16.5 %collective-permute-start.21 = (bf16[256,1024]{1,0:T(8,128)(2,1)S(1)}, bf16[256,1024]{1,0:T(8,128)(2,1)S(1)}, u32[]{:S(2)}, u32[]{:S(2)}) collective-permute-start(bf16[256,1024]{1,0:T(8,128)(2,1)S(1)} %get-tuple-element.122.gs_ref), channel_id=1, source_target_pairs={{0,8},{8,0},{1,9},{9,1},{2,10},{10,2},{3,11},{11,3},{4,12},{12,4},... | collective-permute-start | bytes 1572872 | tf_op jit(solution)/shard_map/ppermute | solution.py:254
  88.5 14.9 %collective-permute-start.24 = (bf16[4,64,1024]{2,1,0:T(8,128)(2,1)S(1)}, bf16[4,64,1024]{2,1,0:T(8,128)(2,1)S(1)}, u32[]{:S(2)}, u32[]{:S(2)}) collective-permute-start(bf16[4,64,1024]{2,1,0:T(8,128)(2,1)S(1)} %pad_maximum_fusion.3), channel_id=1, source_target_pairs={{0,2},{1,3},{2,6},{3,7},{4,0},{5,1},{6,4},{7,5},{8,10},{9,11},{10,... | collective-permute-start | bytes 1572872 | tf_op jit(solution)/shard_map/ppermute | solution.py:269
  94.5 8.9 %collective-permute-start.22 = (bf16[2,64,1024]{2,1,0:T(8,128)(2,1)S(1)}, bf16[2,64,1024]{2,1,0:T(8,128)(2,1)S(1)}, u32[]{:S(2)}, u32[]{:S(2)}) collective-permute-start(bf16[2,64,1024]{2,1,0:T(8,128)(2,1)S(1)} %get-tuple-element.124), channel_id=1, source_target_pairs={{0,8},{8,0},{1,9},{9,1},{2,10},{10,2},{3,11},{11,3},{4,12},{12,4},... | collective-permute-start | bytes 786440 | tf_op jit(solution)/shard_map/ppermute | solution.py:254
  95.1 8.3 %collective-permute-start.23 = (bf16[2,64,1024]{2,1,0:T(8,128)(2,1)S(1)}, bf16[2,64,1024]{2,1,0:T(8,128)(2,1)S(1)}, u32[]{:S(2)}, u32[]{:S(2)}) collective-permute-start(bf16[2,64,1024]{2,1,0:T(8,128)(2,1)S(1)} %get-tuple-element.125), channel_id=1, source_target_pairs={{0,1},{1,0},{2,3},{3,2},{4,5},{5,4},{6,7},{7,6},{8,9},{9,8},{10,11... | collective-permute-start | bytes 786440 | tf_op jit(solution)/shard_map/ppermute | solution.py:260
  103.8 16.0 %collective-permute-start.28 = (bf16[4,64,1024]{2,1,0:T(8,128)(2,1)S(1)}, bf16[4,64,1024]{2,1,0:T(8,128)(2,1)S(1)}, u32[]{:S(2)}, u32[]{:S(2)}) collective-permute-start(bf16[4,64,1024]{2,1,0:T(8,128)(2,1)S(1)} %pad_maximum_fusion.4), channel_id=1, source_target_pairs={{0,2},{1,3},{2,6},{3,7},{4,0},{5,1},{6,4},{7,5},{8,10},{9,11},{10,... | collective-permute-start | bytes 1572872 | tf_op jit(solution)/shard_map/ppermute | solution.py:269
  110.4 24.5 %copy-start.2 = (s32[128,8]{0,1:T(8,128)S(1)}, s32[128,8]{0,1:T(8,128)}, u32[]{:S(2)}) copy-start(s32[128,8]{0,1:T(8,128)} %param.11) | copy-start | bytes 12292
  110.5 6.5 %collective-permute-start.25 = (bf16[2,64,1024]{2,1,0:T(8,128)(2,1)S(1)}, bf16[2,64,1024]{2,1,0:T(8,128)(2,1)S(1)}, u32[]{:S(2)}, u32[]{:S(2)}) collective-permute-start(bf16[2,64,1024]{2,1,0:T(8,128)(2,1)S(1)} %get-tuple-element.134), channel_id=1, source_target_pairs={{0,8},{8,0},{1,9},{9,1},{2,10},{10,2},{3,11},{11,3},{4,12},{12,4},... | collective-permute-start | bytes 786440 | tf_op jit(solution)/shard_map/ppermute | solution.py:254
  112.0 7.8 %collective-permute-start.26 = (bf16[2,64,1024]{2,1,0:T(8,128)(2,1)S(1)}, bf16[2,64,1024]{2,1,0:T(8,128)(2,1)S(1)}, u32[]{:S(2)}, u32[]{:S(2)}) collective-permute-start(bf16[2,64,1024]{2,1,0:T(8,128)(2,1)S(1)} %get-tuple-element.135), channel_id=1, source_target_pairs={{0,1},{1,0},{2,3},{3,2},{4,5},{5,4},{6,7},{7,6},{8,9},{9,8},{10,11... | collective-permute-start | bytes 786440 | tf_op jit(solution)/shard_map/ppermute | solution.py:260
  113.1 3.9 %collective-permute-start.27 = (f32[4,2,2,128]{3,1,2,0:T(2,128)S(1)}, f32[4,2,2,128]{3,1,2,0:T(2,128)S(1)}, u32[]{:S(2)}, u32[]{:S(2)}) collective-permute-start(f32[4,2,2,128]{3,1,2,0:T(2,128)S(1)} %constant_dynamic-update-slice_fusion), channel_id=1, source_target_pairs={{0,8},{8,0},{1,9},{9,1},{2,10},{10,2},{3,11},{11,3},{4,12},{12,4},... | collective-permute-start | bytes 24584 | tf_op jit(solution)/shard_map/ppermute | solution.py:254
  119.9 6.9 %collective-permute-start.29 = (bf16[64,1024]{1,0:T(8,128)(2,1)S(1)}, bf16[64,1024]{1,0:T(8,128)(2,1)S(1)}, u32[]{:S(2)}, u32[]{:S(2)}) collective-permute-start(bf16[64,1024]{1,0:T(8,128)(2,1)S(1)} %get-tuple-element.152), channel_id=1, source_target_pairs={{0,1},{1,0},{2,3},{3,2},{4,5},{5,4},{6,7},{7,6},{8,9},{9,8},{10,11... | collective-permute-start | bytes 393224 | tf_op jit(solution)/shard_map/ppermute | solution.py:260
  121.0 6.0 %collective-permute-start.30 = (bf16[64,1024]{1,0:T(8,128)(2,1)S(1)}, bf16[64,1024]{1,0:T(8,128)(2,1)S(1)}, u32[]{:S(2)}, u32[]{:S(2)}) collective-permute-start(bf16[64,1024]{1,0:T(8,128)(2,1)S(1)} %get-tuple-element.153), channel_id=1, source_target_pairs={{0,8},{8,0},{1,9},{9,1},{2,10},{10,2},{3,11},{11,3},{4,12},{12,4},... | collective-permute-start | bytes 393224 | tf_op jit(solution)/shard_map/ppermute | solution.py:254
  121.5 8.3 %collective-permute-start.34 = (f32[2,2,128]{2,0,1:T(2,128)S(1)}, f32[2,2,128]{2,0,1:T(2,128)S(1)}, u32[]{:S(2)}, u32[]{:S(2)}) collective-permute-start(f32[2,2,128]{2,0,1:T(2,128)S(1)} %get-tuple-element.162), channel_id=1, source_target_pairs={{0,4},{1,5},{2,0},{3,1},{4,6},{5,7},{6,2},{7,3},{8,12},{9,13},{10,... | collective-permute-start | bytes 6152 | tf_op jit(solution)/shard_map/ppermute | solution.py:269
  123.0 8.1 %collective-permute-start.35 = (f32[2,2,128]{2,0,1:T(2,128)S(1)}, f32[2,2,128]{2,0,1:T(2,128)S(1)}, u32[]{:S(2)}, u32[]{:S(2)}) collective-permute-start(f32[2,2,128]{2,0,1:T(2,128)S(1)} %get-tuple-element.161), channel_id=1, source_target_pairs={{0,6},{1,7},{2,4},{3,5},{4,2},{5,3},{6,0},{7,1},{8,14},{9,15},{10,... | collective-permute-start | bytes 6152 | tf_op jit(solution)/shard_map/ppermute | solution.py:269
  126.8 4.5 %collective-permute-start.36 = (f32[2,2,128]{2,0,1:T(2,128)S(1)}, f32[2,2,128]{2,0,1:T(2,128)S(1)}, u32[]{:S(2)}, u32[]{:S(2)}) collective-permute-start(f32[2,2,128]{2,0,1:T(2,128)S(1)} %get-tuple-element.160), channel_id=1, source_target_pairs={{0,2},{1,3},{2,6},{3,7},{4,0},{5,1},{6,4},{7,5},{8,10},{9,11},{10,... | collective-permute-start | bytes 6152 | tf_op jit(solution)/shard_map/ppermute | solution.py:269
  127.2 8.9 %collective-permute-start.32 = (bf16[128,1024]{1,0:T(8,128)(2,1)S(1)}, bf16[128,1024]{1,0:T(8,128)(2,1)S(1)}, u32[]{:S(2)}, u32[]{:S(2)}) collective-permute-start(bf16[128,1024]{1,0:T(8,128)(2,1)S(1)} %pad_maximum_fusion.5), channel_id=1, source_target_pairs={{0,2},{1,3},{2,6},{3,7},{4,0},{5,1},{6,4},{7,5},{8,10},{9,11},{10,... | collective-permute-start | bytes 786440 | tf_op jit(solution)/shard_map/ppermute | solution.py:269
  129.2 6.9 %collective-permute-start.33 = (bf16[64,1024]{1,0:T(8,128)(2,1)S(1)}, bf16[64,1024]{1,0:T(8,128)(2,1)S(1)}, u32[]{:S(2)}, u32[]{:S(2)}) collective-permute-start(bf16[64,1024]{1,0:T(8,128)(2,1)S(1)} %fusion.7), channel_id=1, source_target_pairs={{0,8},{8,0},{1,9},{9,1},{2,10},{10,2},{3,11},{11,3},{4,12},{12,4},... | collective-permute-start | bytes 393224 | tf_op jit(solution)/shard_map/ppermute | solution.py:254
  129.8 6.3 %collective-permute-start.31 = (bf16[64,1024]{1,0:T(8,128)(2,1)S(1)}, bf16[64,1024]{1,0:T(8,128)(2,1)S(1)}, u32[]{:S(2)}, u32[]{:S(2)}) collective-permute-start(bf16[64,1024]{1,0:T(8,128)(2,1)S(1)} %fusion.6), channel_id=1, source_target_pairs={{0,1},{1,0},{2,3},{3,2},{4,5},{5,4},{6,7},{7,6},{8,9},{9,8},{10,11... | collective-permute-start | bytes 393224 | tf_op jit(solution)/shard_map/ppermute | solution.py:260
  131.3 3.7 %collective-permute-start.37 = (f32[4,2,128]{2,1,0:T(2,128)S(1)}, f32[4,2,128]{2,1,0:T(2,128)S(1)}, u32[]{:S(2)}, u32[]{:S(2)}) collective-permute-start(f32[4,2,128]{2,1,0:T(2,128)S(1)} %get-tuple-element.158), channel_id=1, source_target_pairs={{0,1},{1,0},{2,3},{3,2},{4,5},{5,4},{6,7},{7,6},{8,9},{9,8},{10,11... | collective-permute-start | bytes 12296 | tf_op jit(solution)/shard_map/ppermute | solution.py:260

commit v6 on v3

--- a/solution.py
+++ b/solution.py
@@ -339,11 +339,11 @@
     (_, a_keep, _, b_keep), (a_got, b_got) = outs[-1], hops[-1]
     term = jnp.stack(terms).reshape(ring, 2, 2, token_rows)
     term_far = over_x(term)
-    a_got, b_got = after((a_got, b_got), term_far)
+    b_got = after(b_got, term_far)
     a_next, b_next = add(a_keep[1], a_got[1], moving[1]), add(b_keep[1], b_got[1], moving[3])
     term = after(term + term_far, a_next, b_next)
     term = [term[step] if step == 0 else over_z(term[step], -step) for step in range(ring)]
-    a = add(a_keep[0], a_got[0], moving[0], over_y(a_next))
+    a = add(a_keep[0], a_got[0], moving[0], after(over_y(a_next), b_next))
     b = add(b_keep[0], b_got[0], moving[2], over_x(b_next))
     last = lax.optimization_barrier(jnp.concatenate([a, b]))
     moving = over_z(last, 1)

time: 133 us -> 134 us (level)
  starting transfers between devices: 42.3 us -> 44 us
    ppermute x12, waiting for transfers between devices: 15.2 us -> 12.8 us  [over_y(): return lax.ppermute(value, 'expert', [(e, e ^ 1) for e in range(experts)])]
    ppermute x12, starting transfers between devices: 12.2 us -> 13.7 us  [over_x(): return lax.ppermute(value, 'tensor', [(0, 1), (1, 0)])]
  transfers between devices with their start and end apart: 37 -> 37, of which waited for: 16 -> 13; matrix products, arithmetic and copies ran while one was open for 1% -> 1% of each run, Pallas kernels for 17% -> 17%
where the time goes in v6:
time: 134 us
  waiting for transfers between devices  59.3 us (44%)
  starting transfers between devices  44 us (33%)
  Pallas kernels  22.3 us (17%)
  other arithmetic  5.29 us (4%)
  local copies, waits for them, and re-layouts  2.12 us (2%)
    ppermute x12, waiting for transfers between devices, over_x(): return lax.ppermute(value, 'tensor', [(0, 1), (1, 0)])  27.2 us
    pallas_call x4, Pallas kernels, run_expert(): pl.pallas_call(functools.partial(expert_kernel, tops), in_specs=[pl.Block...  20.7 us
    ppermute x10, waiting for transfers between devices, over_z(): lax.ppermute(value, 'expert', [(e, moved(e, shift)) for e in range(expert...  19.3 us
    ppermute x10, starting transfers between devices, over_z(): lax.ppermute(value, 'expert', [(e, moved(e, shift)) for e in range(expert...  16.3 us
    ppermute x12, starting transfers between devices, over_x(): return lax.ppermute(value, 'tensor', [(0, 1), (1, 0)])  13.7 us
    ppermute x12, starting transfers between devices, over_y(): return lax.ppermute(value, 'expert', [(e, e ^ 1) for e in range(experts)])  13.1 us
    ppermute x12, waiting for transfers between devices, over_y(): return lax.ppermute(value, 'expert', [(e, e ^ 1) for e in range(experts)])  12.8 us
  transfers between devices with their start and end apart: 37, of which 13 were waited for; matrix products, arithmetic and copies ran while one was open for 1% of the time, Pallas kernels for 17%

profile of v6, /device:TPU:0, one launch (start us, length us, event | category | flops | bytes accessed | tf_op | source)
XLA Modules:
  0.0 134.0 jit_solution(15823191073521658539)
XLA Ops:
  0.9 1.2 multiply_convert_fusion
  2.2 1.0 pad_maximum_fusion.3.own
  4.2 2.7 %collective-permute-start.5 = (bf16[256,1024]{1,0:T(8,128)(2,1)S(1)}, bf16[256,1024]{1,0:T(8,128)(2,1)S(1)}, u32[]{:S(2)}, u32[]{:S(2)}) collective-permute-start(bf16[256,1024]{1,0:T(8,128)(2,1)S(1)} %pad_maximum_fusion.3.own), channel_id=1, source_target_pairs={{0,2},{1,3},{2,6},{3,7},{4,0},{5,1},{6,4},{7,5},{8,10},{9,11},{10,... | collective-permute-start | bytes 1572872 | tf_op jit(solution)/shard_map/ppermute | solution.py:265
  6.8 1.5 %collective-permute-start = (bf16[128,1024]{1,0:T(8,128)(2,1)S(1)}, bf16[128,1024]{1,0:T(8,128)(2,1)S(1)}, u32[]{:S(2)}, u32[]{:S(2)}) collective-permute-start(bf16[128,1024]{1,0:T(8,128)(2,1)S(1)} %multiply_convert_fusion), channel_id=1, source_target_pairs={{0,8},{8,0},{1,9},{9,1},{2,10},{10,2},{3,11},{11,3},{4,12},{12,4},... | collective-permute-start | bytes 786440 | tf_op jit(solution)/shard_map/ppermute | solution.py:250
  8.3 1.5 %collective-permute-start.2 = (bf16[128,1024]{1,0:T(8,128)(2,1)}, bf16[128,1024]{1,0:T(8,128)(2,1)S(1)}, u32[]{:S(2)}, u32[]{:S(2)}) collective-permute-start(bf16[128,1024]{1,0:T(8,128)(2,1)} %param.10), channel_id=1, source_target_pairs={{0,1},{1,0},{2,3},{3,2},{4,5},{5,4},{6,7},{7,6},{8,9},{9,8},{10,11... | collective-permute-start | bytes 786440 | tf_op jit(solution)/shard_map/ppermute | solution.py:256
  9.9 5.4 %collective-permute-done.x_far = bf16[128,1024]{1,0:T(8,128)(2,1)S(1)} collective-permute-done((bf16[128,1024]{1,0:T(8,128)(2,1)S(1)}, bf16[128,1024]{1,0:T(8,128)(2,1)S(1)}, u32[]{:S(2)}, u32[]{:S(2)}) %collective-permute-start) | collective-permute-done | bytes 262176 | tf_op jit(solution)/shard_map/ppermute | solution.py:250
  15.2 1.4 %collective-permute-done.2.g_far = bf16[128,1024]{1,0:T(8,128)(2,1)S(1)} collective-permute-done((bf16[128,1024]{1,0:T(8,128)(2,1)}, bf16[128,1024]{1,0:T(8,128)(2,1)S(1)}, u32[]{:S(2)}, u32[]{:S(2)}) %collective-permute-start.2) | collective-permute-done | bytes 262176 | tf_op jit(solution)/shard_map/ppermute | solution.py:256
  16.6 0.7 copy-done
  17.3 0.7 copy-done.2
  18.1 2.6 %collective-permute-start.6 = (bf16[272,1024]{1,0:T(8,128)(2,1)S(1)}, bf16[272,1024]{1,0:T(8,128)(2,1)S(1)}, u32[]{:S(2)}, u32[]{:S(2)}) collective-permute-start(bf16[272,1024]{1,0:T(8,128)(2,1)S(1)} %shard_map.95.both), channel_id=1, source_target_pairs={{0,2},{1,3},{2,6},{3,7},{4,0},{5,1},{6,4},{7,5},{8,10},{9,11},{10,... | collective-permute-start | bytes 1671176 | tf_op jit(solution)/shard_map/ppermute | solution.py:265
  20.8 1.6 %collective-permute-start.3 = (bf16[272,1024]{1,0:T(8,128)(2,1)S(1)}, bf16[272,1024]{1,0:T(8,128)(2,1)S(1)}, u32[]{:S(2)}, u32[]{:S(2)}) collective-permute-start(bf16[272,1024]{1,0:T(8,128)(2,1)S(1)} %get-tuple-element.81.xs_ref), channel_id=1, source_target_pairs={{0,1},{1,0},{2,3},{3,2},{4,5},{5,4},{6,7},{7,6},{8,9},{9,8},{10,11... | collective-permute-start | bytes 1671176 | tf_op jit(solution)/shard_map/ppermute | solution.py:256
  22.4 1.1 collective-permute-start.4
  23.5 0.8 pad_maximum_fusion
  25.3 7.7 %collective-permute-done.6.both = bf16[272,1024]{1,0:T(8,128)(2,1)S(1)} collective-permute-done((bf16[272,1024]{1,0:T(8,128)(2,1)S(1)}, bf16[272,1024]{1,0:T(8,128)(2,1)S(1)}, u32[]{:S(2)}, u32[]{:S(2)}) %collective-permute-start.6) | collective-permute-done | bytes 557088 | tf_op jit(solution)/shard_map/ppermute | solution.py:265
  33.2 1.3 collective-permute-start.11
  34.5 1.5 %collective-permute-start.13 = (bf16[272,1024]{1,0:T(8,128)(2,1)S(1)}, bf16[272,1024]{1,0:T(8,128)(2,1)S(1)}, u32[]{:S(2)}, u32[]{:S(2)}) collective-permute-start(bf16[272,1024]{1,0:T(8,128)(2,1)S(1)} %get-tuple-element.92.xs_ref), channel_id=1, source_target_pairs={{0,1},{1,0},{2,3},{3,2},{4,5},{5,4},{6,7},{7,6},{8,9},{9,8},{10,11... | collective-permute-start | bytes 1671176 | tf_op jit(solution)/shard_map/ppermute | solution.py:256
  36.0 1.1 collective-permute-start.14
  37.1 5.2 %shard_map.98 = (bf16[2,64,1024]{2,1,0:T(8,128)(2,1)S(1)}, bf16[2,64,1024]{2,1,0:T(8,128)(2,1)S(1)}, bf16[2,64,1024]{2,1,0:T(8,128)(2,1)S(1)}, bf16[2,64,1024]{2,1,0:T(8,128)(2,1)S(1)}, f32[2,8,256]{2,1,0:T(8,128)S(1)}) custom-call(s32[3]{0:T(128)S(1)} %pad_add_fusion.info_ref, bf16[272,1024]{1,0:T(8,128)(2,1)S(1)} %get-tuple-element.81.xs_ref, ...), custom_call_target="tpu_custom_call" | custom-call | flops 4026531840 | bytes 12582912 | tf_op jit(solution)/shard_map/pallas_call | solution.py:162
  42.8 0.9 collective-permute-start.9
  43.7 8.7 %collective-permute-done.10 = bf16[2,64,1024]{2,1,0:T(8,128)(2,1)S(1)} collective-permute-done((bf16[2,64,1024]{2,1,0:T(8,128)(2,1)S(1)}, bf16[2,64,1024]{2,1,0:T(8,128)(2,1)S(1)}, u32[]{:S(2)}, u32[]{:S(2)}) %collective-permute-start.10) | collective-permute-done | bytes 262176 | tf_op jit(solution)/shard_map/ppermute | solution.py:256
  53.0 5.5 %collective-permute-done.11.um = bf16[528,1024]{1,0:T(8,128)(2,1)S(1)} collective-permute-done((bf16[528,1024]{1,0:T(8,128)(2,1)S(1)}, bf16[528,1024]{1,0:T(8,128)(2,1)S(1)}, u32[]{:S(2)}, u32[]{:S(2)}) %collective-permute-start.11) | collective-permute-done | bytes 1081376 | tf_op jit(solution)/shard_map/ppermute | solution.py:265
  58.5 0.7 collective-permute-start.12
  59.2 1.5 %collective-permute-start.17 = (bf16[272,1024]{1,0:T(8,128)(2,1)S(1)}, bf16[272,1024]{1,0:T(8,128)(2,1)S(1)}, u32[]{:S(2)}, u32[]{:S(2)}) collective-permute-start(bf16[272,1024]{1,0:T(8,128)(2,1)S(1)} %get-tuple-element.108.xs_ref), channel_id=1, source_target_pairs={{0,1},{1,0},{2,3},{3,2},{4,5},{5,4},{6,7},{7,6},{8,9},{9,8},{10,11... | collective-permute-start | bytes 1671176 | tf_op jit(solution)/shard_map/ppermute | solution.py:256
  60.8 1.5 %collective-permute-start.18 = (bf16[256,1024]{1,0:T(8,128)(2,1)S(1)}, bf16[256,1024]{1,0:T(8,128)(2,1)S(1)}, u32[]{:S(2)}, u32[]{:S(2)}) collective-permute-start(bf16[256,1024]{1,0:T(8,128)(2,1)S(1)} %get-tuple-element.109.gs_ref), channel_id=1, source_target_pairs={{0,8},{8,0},{1,9},{9,1},{2,10},{10,2},{3,11},{11,3},{4,12},{12,4},... | collective-permute-start | bytes 1572872 | tf_op jit(solution)/shard_map/ppermute | solution.py:250
  62.3 5.2 %shard_map.99 = (bf16[2,64,1024]{2,1,0:T(8,128)(2,1)S(1)}, bf16[2,64,1024]{2,1,0:T(8,128)(2,1)S(1)}, bf16[2,64,1024]{2,1,0:T(8,128)(2,1)S(1)}, bf16[2,64,1024]{2,1,0:T(8,128)(2,1)S(1)}, f32[2,8,256]{2,1,0:T(8,128)S(1)}) custom-call(s32[3]{0:T(128)S(1)} %pad_add_fusion.info_ref, bf16[272,1024]{1,0:T(8,128)(2,1)S(1)} %get-tuple-element.92.xs_ref, ...), custom_call_target="tpu_custom_call" | custom-call | flops 4026531840 | bytes 12582912 | tf_op jit(solution)/shard_map/pallas_call | solution.py:162
  67.4 0.6 collective-permute-start.15
  68.6 8.6 %collective-permute-done.15 = bf16[2,64,1024]{2,1,0:T(8,128)(2,1)S(1)} collective-permute-done((bf16[2,64,1024]{2,1,0:T(8,128)(2,1)S(1)}, bf16[2,64,1024]{2,1,0:T(8,128)(2,1)S(1)}, u32[]{:S(2)}, u32[]{:S(2)}) %collective-permute-start.15) | collective-permute-done | bytes 262176 | tf_op jit(solution)/shard_map/ppermute | solution.py:250
  77.3 5.5 %collective-permute-done.12.um = bf16[528,1024]{1,0:T(8,128)(2,1)S(1)} collective-permute-done((bf16[528,1024]{1,0:T(8,128)(2,1)S(1)}, bf16[528,1024]{1,0:T(8,128)(2,1)S(1)}, u32[]{:S(2)}, u32[]{:S(2)}) %collective-permute-start.12) | collective-permute-done | bytes 1081376 | tf_op jit(solution)/shard_map/ppermute | solution.py:265
  82.9 1.2 collective-permute-start.19
  84.1 1.6 %collective-permute-start.20 = (bf16[256,1024]{1,0:T(8,128)(2,1)S(1)}, bf16[256,1024]{1,0:T(8,128)(2,1)S(1)}, u32[]{:S(2)}, u32[]{:S(2)}) collective-permute-start(bf16[256,1024]{1,0:T(8,128)(2,1)S(1)} %get-tuple-element.114.gs_ref), channel_id=1, source_target_pairs={{0,8},{8,0},{1,9},{9,1},{2,10},{10,2},{3,11},{11,3},{4,12},{12,4},... | collective-permute-start | bytes 1572872 | tf_op jit(solution)/shard_map/ppermute | solution.py:250
  85.7 0.8 collective-permute-start.23
  86.5 5.2 %shard_map.102 = (bf16[2,64,1024]{2,1,0:T(8,128)(2,1)S(1)}, bf16[2,64,1024]{2,1,0:T(8,128)(2,1)S(1)}, bf16[2,64,1024]{2,1,0:T(8,128)(2,1)S(1)}, bf16[2,64,1024]{2,1,0:T(8,128)(2,1)S(1)}, f32[2,8,256]{2,1,0:T(8,128)S(1)}) custom-call(s32[3]{0:T(128)S(1)} %pad_add_fusion.info_ref, bf16[272,1024]{1,0:T(8,128)(2,1)S(1)} %get-tuple-element.108.xs_ref, ...), custom_call_target="tpu_custom_call" | custom-call | flops 4026531840 | bytes 12582912 | tf_op jit(solution)/shard_map/pallas_call | solution.py:162
  92.8 6.9 %collective-permute-done.21 = bf16[2,64,1024]{2,1,0:T(8,128)(2,1)S(1)} collective-permute-done((bf16[2,64,1024]{2,1,0:T(8,128)(2,1)S(1)}, bf16[2,64,1024]{2,1,0:T(8,128)(2,1)S(1)}, u32[]{:S(2)}, u32[]{:S(2)}) %collective-permute-start.21) | collective-permute-done | bytes 262176 | tf_op jit(solution)/shard_map/ppermute | solution.py:250
  100.2 2.3 %collective-permute-start.25 = (bf16[4,64,1024]{2,1,0:T(8,128)(2,1)S(1)}, bf16[4,64,1024]{2,1,0:T(8,128)(2,1)S(1)}, u32[]{:S(2)}, u32[]{:S(2)}) collective-permute-start(bf16[4,64,1024]{2,1,0:T(8,128)(2,1)S(1)} %pad_maximum_fusion.5), channel_id=1, source_target_pairs={{0,2},{1,3},{2,6},{3,7},{4,0},{5,1},{6,4},{7,5},{8,10},{9,11},{10,... | collective-permute-start | bytes 1572872 | tf_op jit(solution)/shard_map/ppermute | solution.py:265
  102.5 5.2 %shard_map.103 = (bf16[2,64,1024]{2,1,0:T(8,128)(2,1)S(1)}, bf16[2,64,1024]{2,1,0:T(8,128)(2,1)S(1)}, bf16[2,64,1024]{2,1,0:T(8,128)(2,1)S(1)}, bf16[2,64,1024]{2,1,0:T(8,128)(2,1)S(1)}, f32[2,8,256]{2,1,0:T(8,128)S(1)}) custom-call(s32[3]{0:T(128)S(1)} %pad_add_fusion.info_ref, bf16[272,1024]{1,0:T(8,128)(2,1)S(1)} %get-tuple-element.113.xs_ref, ...), custom_call_target="tpu_custom_call" | custom-call | flops 4026531840 | bytes 12582912 | tf_op jit(solution)/shard_map/pallas_call | solution.py:162
  108.2 1.5 %collective-permute-start.24 = (bf16[2,64,1024]{2,1,0:T(8,128)(2,1)S(1)}, bf16[2,64,1024]{2,1,0:T(8,128)(2,1)S(1)}, u32[]{:S(2)}, u32[]{:S(2)}) collective-permute-start(bf16[2,64,1024]{2,1,0:T(8,128)(2,1)S(1)} %get-tuple-element.126), channel_id=1, source_target_pairs={{0,8},{8,0},{1,9},{9,1},{2,10},{10,2},{3,11},{11,3},{4,12},{12,4},... | collective-permute-start | bytes 786440 | tf_op jit(solution)/shard_map/ppermute | solution.py:250
  110.3 5.8 %collective-permute-done.28 = f32[4,2,2,128]{3,1,2,0:T(2,128)S(1)} collective-permute-done((f32[4,2,2,128]{3,1,2,0:T(2,128)S(1)}, f32[4,2,2,128]{3,1,2,0:T(2,128)S(1)}, u32[]{:S(2)}, u32[]{:S(2)}) %collective-permute-start.28) | collective-permute-done | bytes 8224 | tf_op jit(solution)/shard_map/ppermute | solution.py:250
  116.3 1.6 %collective-permute-start.26 = (bf16[64,1024]{1,0:T(8,128)(2,1)S(1)}, bf16[64,1024]{1,0:T(8,128)(2,1)S(1)}, u32[]{:S(2)}, u32[]{:S(2)}) collective-permute-start(bf16[64,1024]{1,0:T(8,128)(2,1)S(1)} %get-tuple-element.144), channel_id=1, source_target_pairs={{0,1},{1,0},{2,3},{3,2},{4,5},{5,4},{6,7},{7,6},{8,9},{9,8},{10,11... | collective-permute-start | bytes 393224 | tf_op jit(solution)/shard_map/ppermute | solution.py:256
  117.8 1.5 %collective-permute-start.29 = (bf16[64,1024]{1,0:T(8,128)(2,1)S(1)}, bf16[64,1024]{1,0:T(8,128)(2,1)S(1)}, u32[]{:S(2)}, u32[]{:S(2)}) collective-permute-start(bf16[64,1024]{1,0:T(8,128)(2,1)S(1)} %get-tuple-element.145), channel_id=1, source_target_pairs={{0,8},{8,0},{1,9},{9,1},{2,10},{10,2},{3,11},{11,3},{4,12},{12,4},... | collective-permute-start | bytes 393224 | tf_op jit(solution)/shard_map/ppermute | solution.py:250
  119.3 0.8 collective-permute-start.33
  120.2 3.6 %collective-permute-start.34 = (f32[2,2,128]{2,0,1:T(2,128)S(1)}, f32[2,2,128]{2,0,1:T(2,128)S(1)}, u32[]{:S(2)}, u32[]{:S(2)}) collective-permute-start(f32[2,2,128]{2,0,1:T(2,128)S(1)} %get-tuple-element.153), channel_id=1, source_target_pairs={{0,6},{1,7},{2,4},{3,5},{4,2},{5,3},{6,0},{7,1},{8,14},{9,15},{10,... | collective-permute-start | bytes 6152 | tf_op jit(solution)/shard_map/ppermute | solution.py:265
  124.0 1.5 %collective-permute-start.31 = (bf16[128,1024]{1,0:T(8,128)(2,1)S(1)}, bf16[128,1024]{1,0:T(8,128)(2,1)S(1)}, u32[]{:S(2)}, u32[]{:S(2)}) collective-permute-start(bf16[128,1024]{1,0:T(8,128)(2,1)S(1)} %pad_maximum_fusion.6), channel_id=1, source_target_pairs={{0,2},{1,3},{2,6},{3,7},{4,0},{5,1},{6,4},{7,5},{8,10},{9,11},{10,... | collective-permute-start | bytes 786440 | tf_op jit(solution)/shard_map/ppermute | solution.py:265
  125.5 1.2 collective-permute-start.32
  126.8 1.0 collective-permute-start.30
  128.3 1.0 collective-permute-start.36
  129.3 2.6 %collective-permute-done.36.refs_1_ = f32[4,2,128]{2,1,0:T(2,128)S(1)} collective-permute-done((f32[4,2,128]{2,1,0:T(2,128)S(1)}, f32[4,2,128]{2,1,0:T(2,128)S(1)}, u32[]{:S(2)}, u32[]{:S(2)}) %collective-permute-start.36) | collective-permute-done | bytes 4128 | tf_op jit(solution)/shard_map/ppermute | solution.py:256
  131.9 1.2 shard_map.104
  133.3 0.7 pad_maximum_fusion.7
  (78 shorter events, 8.3 us)
Async XLA Ops:
  0.6 22.8 %copy-start.3 = (bf16[1,384,2048]{2,1,0:T(8,128)(2,1)S(1)}, bf16[1,384,2048]{2,1,0:T(8,128)(2,1)}, u32[]{:S(2)}) copy-start(bf16[1,384,2048]{2,1,0:T(8,128)(2,1)} %param.13) | copy-start | bytes 4718596
  3.2 5.2 %collective-permute-start.1 = (bf16[384,2048]{1,0:T(8,128)(2,1)}, bf16[384,2048]{1,0:T(8,128)(2,1)S(1)}, u32[]{:S(2)}, u32[]{:S(2)}) collective-permute-start(bf16[384,2048]{1,0:T(8,128)(2,1)} %bitcast.85), channel_id=1, source_target_pairs={{0,16},{16,0},{1,17},{17,1},{2,18},{18,2},{3,19},{19,3},{4,20},{20... | collective-permute-start | bytes 4718600 | tf_op jit(solution)/shard_map/ppermute | solution.py:253
  3.7 17.1 %collective-permute-start.7 = (bf16[384,2048]{1,0:T(8,128)(2,1)}, bf16[384,2048]{1,0:T(8,128)(2,1)S(1)}, u32[]{:S(2)}, u32[]{:S(2)}) collective-permute-start(bf16[384,2048]{1,0:T(8,128)(2,1)} %bitcast.87), channel_id=1, source_target_pairs={{0,16},{16,0},{1,17},{17,1},{2,18},{18,2},{3,19},{19,3},{4,20},{20... | collective-permute-start | bytes 4718600 | tf_op jit(solution)/shard_map/ppermute | solution.py:253
  3.8 17.1 %collective-permute-start.8 = (bf16[384,2048]{1,0:T(8,128)(2,1)}, bf16[384,2048]{1,0:T(8,128)(2,1)S(1)}, u32[]{:S(2)}, u32[]{:S(2)}) collective-permute-start(bf16[384,2048]{1,0:T(8,128)(2,1)} %bitcast.89), channel_id=1, source_target_pairs={{0,16},{16,0},{1,17},{17,1},{2,18},{18,2},{3,19},{19,3},{4,20},{20... | collective-permute-start | bytes 4718600 | tf_op jit(solution)/shard_map/ppermute | solution.py:253
  4.2 16.6 %collective-permute-start.5 = (bf16[256,1024]{1,0:T(8,128)(2,1)S(1)}, bf16[256,1024]{1,0:T(8,128)(2,1)S(1)}, u32[]{:S(2)}, u32[]{:S(2)}) collective-permute-start(bf16[256,1024]{1,0:T(8,128)(2,1)S(1)} %pad_maximum_fusion.3.own), channel_id=1, source_target_pairs={{0,2},{1,3},{2,6},{3,7},{4,0},{5,1},{6,4},{7,5},{8,10},{9,11},{10,... | collective-permute-start | bytes 1572872 | tf_op jit(solution)/shard_map/ppermute | solution.py:265
  6.8 8.4 %collective-permute-start = (bf16[128,1024]{1,0:T(8,128)(2,1)S(1)}, bf16[128,1024]{1,0:T(8,128)(2,1)S(1)}, u32[]{:S(2)}, u32[]{:S(2)}) collective-permute-start(bf16[128,1024]{1,0:T(8,128)(2,1)S(1)} %multiply_convert_fusion), channel_id=1, source_target_pairs={{0,8},{8,0},{1,9},{9,1},{2,10},{10,2},{3,11},{11,3},{4,12},{12,4},... | collective-permute-start | bytes 786440 | tf_op jit(solution)/shard_map/ppermute | solution.py:250
  8.3 8.3 %collective-permute-start.2 = (bf16[128,1024]{1,0:T(8,128)(2,1)}, bf16[128,1024]{1,0:T(8,128)(2,1)S(1)}, u32[]{:S(2)}, u32[]{:S(2)}) collective-permute-start(bf16[128,1024]{1,0:T(8,128)(2,1)} %param.10), channel_id=1, source_target_pairs={{0,1},{1,0},{2,3},{3,2},{4,5},{5,4},{6,7},{7,6},{8,9},{9,8},{10,11... | collective-permute-start | bytes 786440 | tf_op jit(solution)/shard_map/ppermute | solution.py:256
  16.6 0.7 copy-start
  17.3 0.7 copy-start.2
  18.0 5.4 %copy-start.4 = (bf16[1,384,2048]{2,1,0:T(8,128)(2,1)S(1)}, bf16[1,384,2048]{2,1,0:T(8,128)(2,1)}, u32[]{:S(2)}) copy-start(bf16[1,384,2048]{2,1,0:T(8,128)(2,1)} %param.14) | copy-start | bytes 4718596
  18.1 15.0 %collective-permute-start.6 = (bf16[272,1024]{1,0:T(8,128)(2,1)S(1)}, bf16[272,1024]{1,0:T(8,128)(2,1)S(1)}, u32[]{:S(2)}, u32[]{:S(2)}) collective-permute-start(bf16[272,1024]{1,0:T(8,128)(2,1)S(1)} %shard_map.95.both), channel_id=1, source_target_pairs={{0,2},{1,3},{2,6},{3,7},{4,0},{5,1},{6,4},{7,5},{8,10},{9,11},{10,... | collective-permute-start | bytes 1671176 | tf_op jit(solution)/shard_map/ppermute | solution.py:265
  20.8 16.3 %collective-permute-start.3 = (bf16[272,1024]{1,0:T(8,128)(2,1)S(1)}, bf16[272,1024]{1,0:T(8,128)(2,1)S(1)}, u32[]{:S(2)}, u32[]{:S(2)}) collective-permute-start(bf16[272,1024]{1,0:T(8,128)(2,1)S(1)} %get-tuple-element.81.xs_ref), channel_id=1, source_target_pairs={{0,1},{1,0},{2,3},{3,2},{4,5},{5,4},{6,7},{7,6},{8,9},{9,8},{10,11... | collective-permute-start | bytes 1671176 | tf_op jit(solution)/shard_map/ppermute | solution.py:256
  22.4 14.7 %collective-permute-start.4 = (bf16[256,1024]{1,0:T(8,128)(2,1)S(1)}, bf16[256,1024]{1,0:T(8,128)(2,1)S(1)}, u32[]{:S(2)}, u32[]{:S(2)}) collective-permute-start(bf16[256,1024]{1,0:T(8,128)(2,1)S(1)} %get-tuple-element.82.gs_ref), channel_id=1, source_target_pairs={{0,8},{8,0},{1,9},{9,1},{2,10},{10,2},{3,11},{11,3},{4,12},{12,4},... | collective-permute-start | bytes 1572872 | tf_op jit(solution)/shard_map/ppermute | solution.py:250
  23.5 1.4 %copy-start.5 = (bf16[1,384,2048]{2,1,0:T(8,128)(2,1)S(1)}, bf16[1,384,2048]{2,1,0:T(8,128)(2,1)}, u32[]{:S(2)}) copy-start(bf16[1,384,2048]{2,1,0:T(8,128)(2,1)} %param.15) | copy-start | bytes 4718596
  33.2 25.3 %collective-permute-start.11 = (bf16[528,1024]{1,0:T(8,128)(2,1)S(1)}, bf16[528,1024]{1,0:T(8,128)(2,1)S(1)}, u32[]{:S(2)}, u32[]{:S(2)}) collective-permute-start(bf16[528,1024]{1,0:T(8,128)(2,1)S(1)} %get-tuple-element.91), channel_id=1, source_target_pairs={{0,2},{1,3},{2,6},{3,7},{4,0},{5,1},{6,4},{7,5},{8,10},{9,11},{10,... | collective-permute-start | bytes 3244040 | tf_op jit(solution)/shard_map/ppermute | solution.py:265
  34.5 27.8 %collective-permute-start.13 = (bf16[272,1024]{1,0:T(8,128)(2,1)S(1)}, bf16[272,1024]{1,0:T(8,128)(2,1)S(1)}, u32[]{:S(2)}, u32[]{:S(2)}) collective-permute-start(bf16[272,1024]{1,0:T(8,128)(2,1)S(1)} %get-tuple-element.92.xs_ref), channel_id=1, source_target_pairs={{0,1},{1,0},{2,3},{3,2},{4,5},{5,4},{6,7},{7,6},{8,9},{9,8},{10,11... | collective-permute-start | bytes 1671176 | tf_op jit(solution)/shard_map/ppermute | solution.py:256
  36.0 26.3 %collective-permute-start.14 = (bf16[256,1024]{1,0:T(8,128)(2,1)S(1)}, bf16[256,1024]{1,0:T(8,128)(2,1)S(1)}, u32[]{:S(2)}, u32[]{:S(2)}) collective-permute-start(bf16[256,1024]{1,0:T(8,128)(2,1)S(1)} %get-tuple-element.93.gs_ref), channel_id=1, source_target_pairs={{0,8},{8,0},{1,9},{9,1},{2,10},{10,2},{3,11},{11,3},{4,12},{12,4},... | collective-permute-start | bytes 1572872 | tf_op jit(solution)/shard_map/ppermute | solution.py:250
  42.2 10.2 %collective-permute-start.10 = (bf16[2,64,1024]{2,1,0:T(8,128)(2,1)S(1)}, bf16[2,64,1024]{2,1,0:T(8,128)(2,1)S(1)}, u32[]{:S(2)}, u32[]{:S(2)}) collective-permute-start(bf16[2,64,1024]{2,1,0:T(8,128)(2,1)S(1)} %get-tuple-element.101), channel_id=1, source_target_pairs={{0,1},{1,0},{2,3},{3,2},{4,5},{5,4},{6,7},{7,6},{8,9},{9,8},{10,11... | collective-permute-start | bytes 786440 | tf_op jit(solution)/shard_map/ppermute | solution.py:256
  42.8 10.1 %collective-permute-start.9 = (bf16[2,64,1024]{2,1,0:T(8,128)(2,1)S(1)}, bf16[2,64,1024]{2,1,0:T(8,128)(2,1)S(1)}, u32[]{:S(2)}, u32[]{:S(2)}) collective-permute-start(bf16[2,64,1024]{2,1,0:T(8,128)(2,1)S(1)} %get-tuple-element.100), channel_id=1, source_target_pairs={{0,8},{8,0},{1,9},{9,1},{2,10},{10,2},{3,11},{11,3},{4,12},{12,4},... | collective-permute-start | bytes 786440 | tf_op jit(solution)/shard_map/ppermute | solution.py:250
  58.5 24.3 %collective-permute-start.12 = (bf16[528,1024]{1,0:T(8,128)(2,1)S(1)}, bf16[528,1024]{1,0:T(8,128)(2,1)S(1)}, u32[]{:S(2)}, u32[]{:S(2)}) collective-permute-start(bf16[528,1024]{1,0:T(8,128)(2,1)S(1)} %collective-permute-done.11.um), channel_id=1, source_target_pairs={{0,2},{1,3},{2,6},{3,7},{4,0},{5,1},{6,4},{7,5},{8,10},{9,11},{10,... | collective-permute-start | bytes 3244040 | tf_op jit(solution)/shard_map/ppermute | solution.py:265
  59.2 17.9 %collective-permute-start.17 = (bf16[272,1024]{1,0:T(8,128)(2,1)S(1)}, bf16[272,1024]{1,0:T(8,128)(2,1)S(1)}, u32[]{:S(2)}, u32[]{:S(2)}) collective-permute-start(bf16[272,1024]{1,0:T(8,128)(2,1)S(1)} %get-tuple-element.108.xs_ref), channel_id=1, source_target_pairs={{0,1},{1,0},{2,3},{3,2},{4,5},{5,4},{6,7},{7,6},{8,9},{9,8},{10,11... | collective-permute-start | bytes 1671176 | tf_op jit(solution)/shard_map/ppermute | solution.py:256
  60.8 16.4 %collective-permute-start.18 = (bf16[256,1024]{1,0:T(8,128)(2,1)S(1)}, bf16[256,1024]{1,0:T(8,128)(2,1)S(1)}, u32[]{:S(2)}, u32[]{:S(2)}) collective-permute-start(bf16[256,1024]{1,0:T(8,128)(2,1)S(1)} %get-tuple-element.109.gs_ref), channel_id=1, source_target_pairs={{0,8},{8,0},{1,9},{9,1},{2,10},{10,2},{3,11},{11,3},{4,12},{12,4},... | collective-permute-start | bytes 1572872 | tf_op jit(solution)/shard_map/ppermute | solution.py:250
  67.4 9.7 %collective-permute-start.15 = (bf16[2,64,1024]{2,1,0:T(8,128)(2,1)S(1)}, bf16[2,64,1024]{2,1,0:T(8,128)(2,1)S(1)}, u32[]{:S(2)}, u32[]{:S(2)}) collective-permute-start(bf16[2,64,1024]{2,1,0:T(8,128)(2,1)S(1)} %get-tuple-element.104), channel_id=1, source_target_pairs={{0,8},{8,0},{1,9},{9,1},{2,10},{10,2},{3,11},{11,3},{4,12},{12,4},... | collective-permute-start | bytes 786440 | tf_op jit(solution)/shard_map/ppermute | solution.py:250
  68.0 9.1 %collective-permute-start.16 = (bf16[2,64,1024]{2,1,0:T(8,128)(2,1)S(1)}, bf16[2,64,1024]{2,1,0:T(8,128)(2,1)S(1)}, u32[]{:S(2)}, u32[]{:S(2)}) collective-permute-start(bf16[2,64,1024]{2,1,0:T(8,128)(2,1)S(1)} %get-tuple-element.106), channel_id=1, source_target_pairs={{0,1},{1,0},{2,3},{3,2},{4,5},{5,4},{6,7},{7,6},{8,9},{9,8},{10,11... | collective-permute-start | bytes 786440 | tf_op jit(solution)/shard_map/ppermute | solution.py:256
  82.9 16.9 %collective-permute-start.19 = (bf16[272,1024]{1,0:T(8,128)(2,1)S(1)}, bf16[272,1024]{1,0:T(8,128)(2,1)S(1)}, u32[]{:S(2)}, u32[]{:S(2)}) collective-permute-start(bf16[272,1024]{1,0:T(8,128)(2,1)S(1)} %get-tuple-element.113.xs_ref), channel_id=1, source_target_pairs={{0,1},{1,0},{2,3},{3,2},{4,5},{5,4},{6,7},{7,6},{8,9},{9,8},{10,11... | collective-permute-start | bytes 1671176 | tf_op jit(solution)/shard_map/ppermute | solution.py:256
  84.1 15.8 %collective-permute-start.20 = (bf16[256,1024]{1,0:T(8,128)(2,1)S(1)}, bf16[256,1024]{1,0:T(8,128)(2,1)S(1)}, u32[]{:S(2)}, u32[]{:S(2)}) collective-permute-start(bf16[256,1024]{1,0:T(8,128)(2,1)S(1)} %get-tuple-element.114.gs_ref), channel_id=1, source_target_pairs={{0,8},{8,0},{1,9},{9,1},{2,10},{10,2},{3,11},{11,3},{4,12},{12,4},... | collective-permute-start | bytes 1572872 | tf_op jit(solution)/shard_map/ppermute | solution.py:250
  85.7 14.1 %collective-permute-start.23 = (bf16[4,64,1024]{2,1,0:T(8,128)(2,1)S(1)}, bf16[4,64,1024]{2,1,0:T(8,128)(2,1)S(1)}, u32[]{:S(2)}, u32[]{:S(2)}) collective-permute-start(bf16[4,64,1024]{2,1,0:T(8,128)(2,1)S(1)} %pad_maximum_fusion.4), channel_id=1, source_target_pairs={{0,2},{1,3},{2,6},{3,7},{4,0},{5,1},{6,4},{7,5},{8,10},{9,11},{10,... | collective-permute-start | bytes 1572872 | tf_op jit(solution)/shard_map/ppermute | solution.py:265
  91.7 8.0 %collective-permute-start.21 = (bf16[2,64,1024]{2,1,0:T(8,128)(2,1)S(1)}, bf16[2,64,1024]{2,1,0:T(8,128)(2,1)S(1)}, u32[]{:S(2)}, u32[]{:S(2)}) collective-permute-start(bf16[2,64,1024]{2,1,0:T(8,128)(2,1)S(1)} %get-tuple-element.116), channel_id=1, source_target_pairs={{0,8},{8,0},{1,9},{9,1},{2,10},{10,2},{3,11},{11,3},{4,12},{12,4},... | collective-permute-start | bytes 786440 | tf_op jit(solution)/shard_map/ppermute | solution.py:250
  92.3 7.5 %collective-permute-start.22 = (bf16[2,64,1024]{2,1,0:T(8,128)(2,1)S(1)}, bf16[2,64,1024]{2,1,0:T(8,128)(2,1)S(1)}, u32[]{:S(2)}, u32[]{:S(2)}) collective-permute-start(bf16[2,64,1024]{2,1,0:T(8,128)(2,1)S(1)} %get-tuple-element.117), channel_id=1, source_target_pairs={{0,1},{1,0},{2,3},{3,2},{4,5},{5,4},{6,7},{7,6},{8,9},{9,8},{10,11... | collective-permute-start | bytes 786440 | tf_op jit(solution)/shard_map/ppermute | solution.py:256
  100.2 15.9 %collective-permute-start.25 = (bf16[4,64,1024]{2,1,0:T(8,128)(2,1)S(1)}, bf16[4,64,1024]{2,1,0:T(8,128)(2,1)S(1)}, u32[]{:S(2)}, u32[]{:S(2)}) collective-permute-start(bf16[4,64,1024]{2,1,0:T(8,128)(2,1)S(1)} %pad_maximum_fusion.5), channel_id=1, source_target_pairs={{0,2},{1,3},{2,6},{3,7},{4,0},{5,1},{6,4},{7,5},{8,10},{9,11},{10,... | collective-permute-start | bytes 1572872 | tf_op jit(solution)/shard_map/ppermute | solution.py:265
  107.6 24.3 %copy-start.1 = (s32[128,8]{0,1:T(8,128)S(1)}, s32[128,8]{0,1:T(8,128)}, u32[]{:S(2)}) copy-start(s32[128,8]{0,1:T(8,128)} %param.11) | copy-start | bytes 12292
  107.6 8.5 %collective-permute-start.27 = (bf16[2,64,1024]{2,1,0:T(8,128)(2,1)S(1)}, bf16[2,64,1024]{2,1,0:T(8,128)(2,1)S(1)}, u32[]{:S(2)}, u32[]{:S(2)}) collective-permute-start(bf16[2,64,1024]{2,1,0:T(8,128)(2,1)S(1)} %get-tuple-element.128), channel_id=1, source_target_pairs={{0,1},{1,0},{2,3},{3,2},{4,5},{5,4},{6,7},{7,6},{8,9},{9,8},{10,11... | collective-permute-start | bytes 786440 | tf_op jit(solution)/shard_map/ppermute | solution.py:256
  108.2 7.9 %collective-permute-start.24 = (bf16[2,64,1024]{2,1,0:T(8,128)(2,1)S(1)}, bf16[2,64,1024]{2,1,0:T(8,128)(2,1)S(1)}, u32[]{:S(2)}, u32[]{:S(2)}) collective-permute-start(bf16[2,64,1024]{2,1,0:T(8,128)(2,1)S(1)} %get-tuple-element.126), channel_id=1, source_target_pairs={{0,8},{8,0},{1,9},{9,1},{2,10},{10,2},{3,11},{11,3},{4,12},{12,4},... | collective-permute-start | bytes 786440 | tf_op jit(solution)/shard_map/ppermute | solution.py:250
  109.7 6.4 %collective-permute-start.28 = (f32[4,2,2,128]{3,1,2,0:T(2,128)S(1)}, f32[4,2,2,128]{3,1,2,0:T(2,128)S(1)}, u32[]{:S(2)}, u32[]{:S(2)}) collective-permute-start(f32[4,2,2,128]{3,1,2,0:T(2,128)S(1)} %constant_dynamic-update-slice_fusion), channel_id=1, source_target_pairs={{0,8},{8,0},{1,9},{9,1},{2,10},{10,2},{3,11},{11,3},{4,12},{12,4},... | collective-permute-start | bytes 24584 | tf_op jit(solution)/shard_map/ppermute | solution.py:250
  116.3 7.5 %collective-permute-start.26 = (bf16[64,1024]{1,0:T(8,128)(2,1)S(1)}, bf16[64,1024]{1,0:T(8,128)(2,1)S(1)}, u32[]{:S(2)}, u32[]{:S(2)}) collective-permute-start(bf16[64,1024]{1,0:T(8,128)(2,1)S(1)} %get-tuple-element.144), channel_id=1, source_target_pairs={{0,1},{1,0},{2,3},{3,2},{4,5},{5,4},{6,7},{7,6},{8,9},{9,8},{10,11... | collective-permute-start | bytes 393224 | tf_op jit(solution)/shard_map/ppermute | solution.py:256
  117.8 5.9 %collective-permute-start.29 = (bf16[64,1024]{1,0:T(8,128)(2,1)S(1)}, bf16[64,1024]{1,0:T(8,128)(2,1)S(1)}, u32[]{:S(2)}, u32[]{:S(2)}) collective-permute-start(bf16[64,1024]{1,0:T(8,128)(2,1)S(1)} %get-tuple-element.145), channel_id=1, source_target_pairs={{0,8},{8,0},{1,9},{9,1},{2,10},{10,2},{3,11},{11,3},{4,12},{12,4},... | collective-permute-start | bytes 393224 | tf_op jit(solution)/shard_map/ppermute | solution.py:250
  119.3 7.4 %collective-permute-start.33 = (f32[2,2,128]{2,0,1:T(2,128)S(1)}, f32[2,2,128]{2,0,1:T(2,128)S(1)}, u32[]{:S(2)}, u32[]{:S(2)}) collective-permute-start(f32[2,2,128]{2,0,1:T(2,128)S(1)} %get-tuple-element.154), channel_id=1, source_target_pairs={{0,4},{1,5},{2,0},{3,1},{4,6},{5,7},{6,2},{7,3},{8,12},{9,13},{10,... | collective-permute-start | bytes 6152 | tf_op jit(solution)/shard_map/ppermute | solution.py:265
  120.2 7.6 %collective-permute-start.34 = (f32[2,2,128]{2,0,1:T(2,128)S(1)}, f32[2,2,128]{2,0,1:T(2,128)S(1)}, u32[]{:S(2)}, u32[]{:S(2)}) collective-permute-start(f32[2,2,128]{2,0,1:T(2,128)S(1)} %get-tuple-element.153), channel_id=1, source_target_pairs={{0,6},{1,7},{2,4},{3,5},{4,2},{5,3},{6,0},{7,1},{8,14},{9,15},{10,... | collective-permute-start | bytes 6152 | tf_op jit(solution)/shard_map/ppermute | solution.py:265
  123.8 4.5 %collective-permute-start.35 = (f32[2,2,128]{2,0,1:T(2,128)S(1)}, f32[2,2,128]{2,0,1:T(2,128)S(1)}, u32[]{:S(2)}, u32[]{:S(2)}) collective-permute-start(f32[2,2,128]{2,0,1:T(2,128)S(1)} %get-tuple-element.152), channel_id=1, source_target_pairs={{0,2},{1,3},{2,6},{3,7},{4,0},{5,1},{6,4},{7,5},{8,10},{9,11},{10,... | collective-permute-start | bytes 6152 | tf_op jit(solution)/shard_map/ppermute | solution.py:265
  124.0 9.1 %collective-permute-start.31 = (bf16[128,1024]{1,0:T(8,128)(2,1)S(1)}, bf16[128,1024]{1,0:T(8,128)(2,1)S(1)}, u32[]{:S(2)}, u32[]{:S(2)}) collective-permute-start(bf16[128,1024]{1,0:T(8,128)(2,1)S(1)} %pad_maximum_fusion.6), channel_id=1, source_target_pairs={{0,2},{1,3},{2,6},{3,7},{4,0},{5,1},{6,4},{7,5},{8,10},{9,11},{10,... | collective-permute-start | bytes 786440 | tf_op jit(solution)/shard_map/ppermute | solution.py:265
  125.5 7.6 %collective-permute-start.32 = (bf16[64,1024]{1,0:T(8,128)(2,1)S(1)}, bf16[64,1024]{1,0:T(8,128)(2,1)S(1)}, u32[]{:S(2)}, u32[]{:S(2)}) collective-permute-start(bf16[64,1024]{1,0:T(8,128)(2,1)S(1)} %fusion.7), channel_id=1, source_target_pairs={{0,8},{8,0},{1,9},{9,1},{2,10},{10,2},{3,11},{11,3},{4,12},{12,4},... | collective-permute-start | bytes 393224 | tf_op jit(solution)/shard_map/ppermute | solution.py:250
  126.8 6.3 %collective-permute-start.30 = (bf16[64,1024]{1,0:T(8,128)(2,1)S(1)}, bf16[64,1024]{1,0:T(8,128)(2,1)S(1)}, u32[]{:S(2)}, u32[]{:S(2)}) collective-permute-start(bf16[64,1024]{1,0:T(8,128)(2,1)S(1)} %fusion.6), channel_id=1, source_target_pairs={{0,1},{1,0},{2,3},{3,2},{4,5},{5,4},{6,7},{7,6},{8,9},{9,8},{10,11... | collective-permute-start | bytes 393224 | tf_op jit(solution)/shard_map/ppermute | solution.py:256
  128.3 3.7 %collective-permute-start.36 = (f32[4,2,128]{2,1,0:T(2,128)S(1)}, f32[4,2,128]{2,1,0:T(2,128)S(1)}, u32[]{:S(2)}, u32[]{:S(2)}) collective-permute-start(f32[4,2,128]{2,1,0:T(2,128)S(1)} %get-tuple-element.150), channel_id=1, source_target_pairs={{0,1},{1,0},{2,3},{3,2},{4,5},{5,4},{6,7},{7,6},{8,9},{9,8},{10,11... | collective-permute-start | bytes 12296 | tf_op jit(solution)/shard_map/ppermute | solution.py:256
